TPU v7x, 512 devices: a whole 4x4x16 slice. The times are simulated.
512 devices in a mesh: seq: 32 (over z_hi, x, core), dp: 16 (over y, z_lo).
Axes of the slice: x: 4, y: 4, z: 16 (z_hi: 4, z_lo: 4; z = z_hi * 4 + z_lo), core: 2. Of those that a mesh axis runs over, the one named last changes fastest.
Arguments:
- queries: bfloat16 [2048, 32, 1024], P('seq', 'dp'), may hold values from -12 to 12
- key_vectors: bfloat16 [2048, 32, 1024], P('seq', 'dp'), may hold values from -12 to 12
- value_vectors: bfloat16 [2048, 32, 1024], P('seq', 'dp'), may hold values from -6 to 6
- features: bfloat16 [2048, 32, 1024], P('seq', 'dp'), may hold values from -6 to 6
- cotangent: bfloat16 [2048, 32, 1024], P('seq', 'dp'), may hold values from -6 to 6
- frames: int32 [32], P('dp'), may hold values from 512 to 2048, as said below
- conv_kernel: float32 [31, 1024], replicated, may hold values from -1 to 1
- conv_bias: float32 [1024], replicated, may hold values from -3 to 3
Outputs:
- block_out: bfloat16 [2048, 32, 1024], P('seq', 'dp')
- grad_features: bfloat16 [2048, 32, 1024], P('seq', 'dp')
- grad_queries: bfloat16 [2048, 32, 1024], P('seq', 'dp')
- grad_keys: bfloat16 [2048, 32, 1024], P('seq', 'dp')
- grad_values: bfloat16 [2048, 32, 1024], P('seq', 'dp')
- grad_kernel: float32 [31, 1024], replicated
- grad_bias: float32 [1024], replicated
Inputs may be any that keep to these rules, and one draw needn't show every extreme that they name: Every utterance has at least 512 valid frames, and utterance 0 has all 2048.
All inputs are finite; a program needn't handle non-finite values.
Results may differ from a plain program's by a relative error of at most 0.0065.
Values may be sent and summed in bfloat16 or wider, within the bound.
No kernel may reach another device: no remote copies, remote signals or barrier semaphores. Data moves between devices by JAX's collectives and lax.ppermute only.
A program may use at most 64 MiB of HBM per device.

v0:
```python
import math

import jax
import jax.numpy as jnp
from jax import lax
from jax.sharding import PartitionSpec as P

HEADS = 16
TAPS = 31


def extended(block, sides, width):
    for axis, dim in sides:
        count = lax.axis_size(axis)
        forward = [(i, i + 1) for i in range(count - 1)]
        backward = [(target, source) for source, target in forward]
        low = lax.ppermute(
            lax.slice_in_dim(block, block.shape[dim] - width, None, axis=dim), axis, forward
        )
        high = lax.ppermute(lax.slice_in_dim(block, 0, width, axis=dim), axis, backward)
        block = jnp.concatenate([low, block, high], axis=dim)
    return block


def to_heads(stacked):
    return lax.all_to_all(stacked, "seq", split_axis=1, concat_axis=0, tiled=True)


def to_frames(stacked):
    return lax.all_to_all(stacked, "seq", split_axis=0, concat_axis=1, tiled=True)


def conv_rim(field):
    return extended(field, (("seq", 0),), TAPS // 2)


def block_probs(query_block, key_rows, key_count):
    score_scale = 1.0 / math.sqrt(key_rows.shape[1])
    scores = (
        jnp.einsum("qd,kd->qk", query_block, key_rows, preferred_element_type=jnp.float32)
        * score_scale
    )
    allowed = jnp.arange(key_rows.shape[0]) < key_count
    scores = jnp.where(allowed[None, :], scores, -jnp.inf)
    row_max = jnp.max(scores, axis=1, keepdims=True)
    exp_scores = jnp.exp(scores - row_max)
    return exp_scores / jnp.sum(exp_scores, axis=1, keepdims=True)


def attend_forward(query_rows, key_rows, value_rows, key_count):
    seq_len = query_rows.shape[0]
    block_rows = min(512, seq_len)

    def one_block(block_index):
        query_block = lax.dynamic_slice_in_dim(query_rows, block_index * block_rows, block_rows, 0)
        probs_bf = block_probs(query_block, key_rows, key_count).astype(jnp.bfloat16)
        return jnp.dot(probs_bf, value_rows, preferred_element_type=jnp.float32).astype(
            jnp.bfloat16
        )

    outputs = lax.map(one_block, jnp.arange(seq_len // block_rows))
    return outputs.reshape(seq_len, query_rows.shape[1])


def attend_backward(query_rows, key_rows, value_rows, grad_out, key_count):
    seq_len, head_dim = query_rows.shape
    block_rows = min(512, seq_len)
    score_scale = 1.0 / math.sqrt(head_dim)

    def one_block(totals, block_index):
        grad_key_acc, grad_val_acc = totals
        first_row = block_index * block_rows
        query_block = lax.dynamic_slice_in_dim(query_rows, first_row, block_rows, 0)
        grad_block = lax.dynamic_slice_in_dim(grad_out, first_row, block_rows, 0)
        probs = block_probs(query_block, key_rows, key_count)
        probs_bf = probs.astype(jnp.bfloat16)
        grad_probs = jnp.einsum(
            "qd,kd->qk", grad_block, value_rows, preferred_element_type=jnp.float32
        )
        grad_val_acc = grad_val_acc + jnp.einsum(
            "qk,qd->kd", probs_bf, grad_block, preferred_element_type=jnp.float32
        )
        row_delta = jnp.sum(probs * grad_probs, axis=1, keepdims=True)
        grad_scores = (probs * (grad_probs - row_delta) * score_scale).astype(jnp.bfloat16)
        grad_query = jnp.dot(grad_scores, key_rows, preferred_element_type=jnp.float32).astype(
            jnp.bfloat16
        )
        grad_key_acc = grad_key_acc + jnp.einsum(
            "qk,qd->kd", grad_scores, query_block, preferred_element_type=jnp.float32
        )
        return ((grad_key_acc, grad_val_acc), grad_query)

    zero_rows = jnp.zeros((seq_len, head_dim), jnp.float32)
    final, grad_queries = lax.scan(
        one_block, (zero_rows, zero_rows), jnp.arange(seq_len // block_rows)
    )
    return (
        grad_queries.reshape(seq_len, head_dim),
        final[0].astype(jnp.bfloat16),
        final[1].astype(jnp.bfloat16),
    )


def depthwise(padded, kernel, row_count, reverse_taps):
    result = None
    for tap_index in range(TAPS):
        offset = TAPS - 1 - tap_index if reverse_taps else tap_index
        tap_term = kernel[tap_index] * lax.slice_in_dim(
            padded, offset, offset + row_count, axis=0
        ).astype(jnp.float32)
        result = tap_term if tap_index == 0 else result + tap_term
    return result


def conv_module(hidden, valid_rows, kernel, bias, cotangent, pad_field):
    row_count = hidden.shape[0]
    lead_axes = tuple(range(hidden.ndim - 1))
    masked = jnp.where(valid_rows, hidden, 0.0).astype(jnp.bfloat16)
    padded = pad_field(masked)
    conv_out = bias + depthwise(padded, kernel, row_count, False)
    gate_value = jax.nn.sigmoid(conv_out)
    block_out = (hidden + conv_out * gate_value).astype(jnp.bfloat16)
    cot_rows = cotangent.astype(jnp.float32)
    grad_conv = cot_rows * gate_value * (1.0 + conv_out * (1.0 - gate_value))
    grad_padded = pad_field(grad_conv.astype(jnp.bfloat16))
    grad_masked = depthwise(grad_padded, kernel, row_count, True)
    grad_features = (cot_rows + jnp.where(valid_rows, grad_masked, 0.0)).astype(jnp.bfloat16)
    grad_kernel = jnp.stack(
        [
            jnp.sum(
                grad_conv
                * lax.slice_in_dim(padded, tap_index, tap_index + row_count, axis=0).astype(
                    jnp.float32
                ),
                axis=lead_axes,
            )
            for tap_index in range(TAPS)
        ]
    )
    grad_bias = jnp.sum(grad_conv, axis=lead_axes)
    return (block_out, grad_features, grad_kernel, grad_bias)


def on_device(
    queries, key_vectors, value_vectors, features, cotangent, frames, conv_kernel, conv_bias
):
    local_len, utt_local, model_width = queries.shape
    head_dim = model_width // HEADS
    item_total = utt_local * HEADS
    seq_devices = lax.axis_size("seq")
    item_count = item_total // seq_devices
    item_ids = lax.axis_index("seq") * item_count + jnp.arange(item_count)
    item_utt = item_ids // HEADS
    item_frames = jnp.sum(
        jnp.where(item_utt[:, None] == jnp.arange(utt_local)[None, :], frames[None, :], 0), axis=1
    )

    def by_items(field):
        return field.reshape(local_len, item_total, head_dim)

    def from_items(field):
        return field.reshape(local_len, utt_local, model_width)

    stacked = jnp.concatenate(
        (by_items(queries), by_items(key_vectors), by_items(value_vectors)), axis=2
    )
    arrived = to_heads(stacked)

    def forward_item(item_index):
        packed = lax.dynamic_index_in_dim(arrived, item_index, 1, keepdims=False)
        return attend_forward(
            packed[:, :head_dim],
            packed[:, head_dim : 2 * head_dim],
            packed[:, 2 * head_dim :],
            item_frames[item_index],
        )

    context = lax.map(forward_item, jnp.arange(item_count))
    context = from_items(to_frames(jnp.moveaxis(context, 0, 1)))
    hidden = features.astype(jnp.float32) + context.astype(jnp.float32)
    positions = lax.axis_index("seq") * local_len + jnp.arange(local_len)
    valid_rows = (positions[:, None] < frames[None, :])[:, :, None]
    block_out, grad_features, grad_kernel, grad_bias = conv_module(
        hidden, valid_rows, conv_kernel, conv_bias, cotangent, conv_rim
    )
    grad_arrived = to_heads(by_items(grad_features))

    def backward_item(item_index):
        packed = lax.dynamic_index_in_dim(arrived, item_index, 1, keepdims=False)
        grad_out = lax.dynamic_index_in_dim(grad_arrived, item_index, 1, keepdims=False)
        grad_triple = attend_backward(
            packed[:, :head_dim],
            packed[:, head_dim : 2 * head_dim],
            packed[:, 2 * head_dim :],
            grad_out,
            item_frames[item_index],
        )
        return jnp.concatenate(grad_triple, axis=1)

    grad_rows = lax.map(backward_item, jnp.arange(item_count))
    grad_rows = to_frames(jnp.moveaxis(grad_rows, 0, 1))
    grad_queries = from_items(grad_rows[:, :, :head_dim])
    grad_keys = from_items(grad_rows[:, :, head_dim : 2 * head_dim])
    grad_values = from_items(grad_rows[:, :, 2 * head_dim :])
    grad_kernel, grad_bias = lax.psum((grad_kernel, grad_bias), ("seq", "dp"))
    return (block_out, grad_features, grad_queries, grad_keys, grad_values, grad_kernel, grad_bias)


def solution(mesh):
    return jax.shard_map(
        on_device,
        mesh=mesh,
        in_specs=(
            P("seq", "dp", None),
            P("seq", "dp", None),
            P("seq", "dp", None),
            P("seq", "dp", None),
            P("seq", "dp", None),
            P("dp"),
            P(),
            P(),
        ),
        out_specs=(
            P("seq", "dp", None),
            P("seq", "dp", None),
            P("seq", "dp", None),
            P("seq", "dp", None),
            P("seq", "dp", None),
            P(),
            P(),
        ),
        check_vma=False,
    )
```

profile of v0, /device:TPU:1, one launch (start us, length us, event | category | flops | bytes accessed | tf_op | source)
XLA Modules:
  0.0 755.6 jit_solution(1275026097187744903)
XLA Ops:
  11.8 1.5 pad_maximum_fusion
  13.3 19.2 %all-to-all-start = ((bf16[64,32,192]{2,0,1:T(8,128)(2,1)}), bf16[64,32,192]{2,0,1:T(8,128)(2,1)S(1)}, u32[]{:S(2)}, u32[]{:S(2)}) async-start(bf16[64,32,192]{2,0,1:T(8,128)(2,1)} %pad_maximum_fusion), calls=%async_computation | async-start | bytes 2097152 | tf_op jit(solution)/shard_map/all_to_all | solution.py:26
  33.2 52.1 %all-to-all-done = bf16[64,32,192]{2,0,1:T(8,128)(2,1)S(1)} async-done(((bf16[64,32,192]{2,0,1:T(8,128)(2,1)}), bf16[64,32,192]{2,0,1:T(8,128)(2,1)S(1)}, u32[]{:S(2)}, u32[]{:S(2)}) %all-to-all-start) | async-done | bytes 786464 | tf_op jit(solution)/shard_map/all_to_all | solution.py:26
  85.7 19.7 %while.41 = (s32[]{:T(128)}, bf16[4,512,64]{1,2,0:T(8,128)(2,1)S(1)}, s32[]{:T(128)}, s32[4]{0:T(128)S(1)}, bf16[2048,64]{1,0:T(8,128)(2,1)S(1)}, /*index=5*/bf1...) while((s32[]{:T(128)}, ...), condition=%wide.region_4.5_spmd, body=%wide.region_1.4_spmd.sunk | while | flops 281052160 | bytes 13846715 | solution.py:61
  107.3 11.6 %reduce.2 = bf16[2048,64]{1,0:T(8,128)(2,1)S(1)} reduce(bf16[2048,1,64]{2,1,0:T(2,128)(2,1)S(1)} %reshape.153, bf16[]{:T(256)} %broadcast.102), dimensions={1}, to_apply=%reshape.153.reduce_sub_computation | reduce | bytes 524290 | tf_op jit(solution)/shard_map/transpose | solution.py:179
  120.0 8.1 %all-to-all-start.1 = ((bf16[32,2,2048]{2,1,0:T(2,128)(2,1)}), bf16[32,2,2048]{2,1,0:T(2,128)(2,1)S(1)}, u32[]{:S(2)}, u32[]{:S(2)}) async-start(bf16[32,2,2048]{2,1,0:T(2,128)(2,1)} %reshape.154), calls=%async_computation.1 | async-start | bytes 524288 | tf_op jit(solution)/shard_map/all_to_all | solution.py:30
  128.2 18.8 %all-to-all-done.1 = bf16[32,2,2048]{2,1,0:T(2,128)(2,1)S(1)} async-done(((bf16[32,2,2048]{2,1,0:T(2,128)(2,1)}), bf16[32,2,2048]{2,1,0:T(2,128)(2,1)S(1)}, u32[]{:S(2)}, u32[]{:S(2)}) %all-to-all-start.1) | async-done | bytes 262176 | tf_op jit(solution)/shard_map/all_to_all | solution.py:30
  148.7 2.0 copy.75
  150.7 1.7 reshape.151
  152.7 2.1 collective-permute-start
  154.8 2.2 collective-permute-start.1
  157.1 3.3 collective-permute-done.1
  160.4 5.0 fusion.89
  166.6 1.9 collective-permute-start.2
  168.5 3.6 collective-permute-start.3
  173.5 3.3 fusion.91
  181.2 29.3 %all-to-all-start.2 = ((bf16[32,2,2048]{2,1,0:T(2,128)(2,1)}), bf16[32,2,2048]{2,1,0:T(2,128)(2,1)}, u32[]{:S(2)}, u32[]{:S(2)}) async-start(bf16[32,2,2048]{2,1,0:T(2,128)(2,1)} %reshape.156), calls=%async_computation.2 | async-start | bytes 524288 | tf_op jit(solution)/shard_map/all_to_all | solution.py:26
  210.5 19.9 %all-to-all-done.2 = bf16[32,2,2048]{2,1,0:T(2,128)(2,1)} async-done(((bf16[32,2,2048]{2,1,0:T(2,128)(2,1)}), bf16[32,2,2048]{2,1,0:T(2,128)(2,1)}, u32[]{:S(2)}, u32[]{:S(2)}) %all-to-all-start.2) | async-done | bytes 262176 | tf_op jit(solution)/shard_map/all_to_all | solution.py:26
  230.5 2.1 reshape.157
  233.3 40.2 %while.42 = (s32[]{:T(128)}, f32[2048,64]{0,1:T(8,128)S(1)}, f32[2048,64]{0,1:T(8,128)}, bf16[4,512,64]{1,2,0:T(8,128)(2,1)}, s32[]{:T(128)}, /*index=5*/s32[4]{...) while((s32[]{:T(128)}, f32[2048,64]{0,1:T(8,128)S(1)}, ...), condition=%wide.region_9.10_spmd.clone, body=%wide.region_5.9_spmd.clone.sunk | while | flops 698909184 | bytes 45975896 | solution.py:94
  239.7 1.7 multiply_convert_fusion.2
  249.7 1.7 multiply_convert_fusion.2
  259.8 1.7 multiply_convert_fusion.2
  269.9 1.7 multiply_convert_fusion.2
  275.7 1.9 reduce.3
  279.2 2.1 reshape.158
  281.3 6.0 all-to-all-start.3
  290.0 2.7 stack.127
  292.7 107.3 %psum.15 = f32[1024]{0:T(1024)} all-reduce(f32[1024]{0:T(1024)S(1)} %copy-done.25), channel_id=1, replica_groups=mesh['seq'=32,'dp'=16] {'seq','dp'}, use_global_device_ids=true, to_apply=%region_43.44 | all-reduce | flops 1024 | bytes 8192 | tf_op jit(solution)/shard_map/psum | solution.py:205
  400.0 4.5 reshape.159
  409.1 338.1 %all-reduce.2.cloned.1.call-done = f32[31,1024]{1,0:T(8,128)} async-done(((f32[31,1024]{1,0:T(8,128)}), f32[31,1024]{1,0:T(8,128)}) %all-reduce.2.cloned.1.call-update) | async-done | bytes 126992 | tf_op jit(solution)/shard_map/psum | solution.py:205
  747.2 1.6 copy.125
  (188 shorter events, 76.6 us)
Async XLA Ops:
  8.7 23.8 %copy-start.27 = (s32[2]{0:T(128)S(1)}, s32[2]{0:T(128)}, u32[]{:S(2)}) copy-start(s32[2]{0:T(128)} %param.17) | copy-start | bytes 28
  13.3 72.0 %all-to-all-start = ((bf16[64,32,192]{2,0,1:T(8,128)(2,1)}), bf16[64,32,192]{2,0,1:T(8,128)(2,1)S(1)}, u32[]{:S(2)}, u32[]{:S(2)}) async-start(bf16[64,32,192]{2,0,1:T(8,128)(2,1)} %pad_maximum_fusion), calls=%async_computation | async-start | bytes 2097152 | tf_op jit(solution)/shard_map/all_to_all | solution.py:26
  106.2 22.0 %copy-start.9 = (f32[31,1024]{1,0:T(8,128)S(1)}, f32[31,1024]{1,0:T(8,128)}, u32[]{:S(2)}) copy-start(f32[31,1024]{1,0:T(8,128)} %param.18) | copy-start | bytes 380932
  120.0 32.5 %copy-start.2 = (bf16[64,2,1024]{2,1,0:T(2,128)(2,1)S(1)}, bf16[64,2,1024]{2,1,0:T(2,128)(2,1)}, u32[]{:S(2)}) copy-start(bf16[64,2,1024]{2,1,0:T(2,128)(2,1)} %param.15) | copy-start | bytes 786436
  120.0 27.1 %all-to-all-start.1 = ((bf16[32,2,2048]{2,1,0:T(2,128)(2,1)}), bf16[32,2,2048]{2,1,0:T(2,128)(2,1)S(1)}, u32[]{:S(2)}, u32[]{:S(2)}) async-start(bf16[32,2,2048]{2,1,0:T(2,128)(2,1)} %reshape.154), calls=%async_computation.1 | async-start | bytes 524288 | tf_op jit(solution)/shard_map/all_to_all | solution.py:30
  128.2 24.3 %copy-start.26 = (pred[64,2]{0,1:T(4,128)(4,1)}, pred[64,2]{0,1:T(4,128)(4,1)S(1)}, u32[]{:S(2)}) copy-start(pred[64,2]{0,1:T(4,128)(4,1)S(1)} %broadcast_compare_fusion) | copy-start | bytes 388
  147.7 12.7 %copy-start.1 = (bf16[64,2,1024]{2,1,0:T(2,128)(2,1)S(1)}, bf16[64,2,1024]{2,1,0:T(2,128)(2,1)}, u32[]{:S(2)}) copy-start(bf16[64,2,1024]{2,1,0:T(2,128)(2,1)} %param.16) | copy-start | bytes 786436
  152.7 4.4 collective-permute-start
  154.8 5.6 collective-permute-start.1
  166.6 5.6 collective-permute-start.2
  168.5 5.0 collective-permute-start.3
  181.2 49.3 %all-to-all-start.2 = ((bf16[32,2,2048]{2,1,0:T(2,128)(2,1)}), bf16[32,2,2048]{2,1,0:T(2,128)(2,1)}, u32[]{:S(2)}, u32[]{:S(2)}) async-start(bf16[32,2,2048]{2,1,0:T(2,128)(2,1)} %reshape.156), calls=%async_computation.2 | async-start | bytes 524288 | tf_op jit(solution)/shard_map/all_to_all | solution.py:26
  245.3 1.8 copy-start.4
  275.7 11.7 %copy-start.3 = (bf16[64,2,1024]{2,1,0:T(2,128)(2,1)S(1)}, bf16[64,2,1024]{2,1,0:T(2,128)(2,1)}, u32[]{:S(2)}) copy-start(bf16[64,2,1024]{2,1,0:T(2,128)(2,1)} %param.15) | copy-start | bytes 786436
  277.7 12.2 %copy-start.10 = (f32[1024]{0:T(1024)S(1)}, f32[1024]{0:T(1024)}, u32[]{:S(2)}) copy-start(f32[1024]{0:T(1024)} %get-tuple-element.177) | copy-start | bytes 12292
  277.7 12.2 %copy-start.11 = (f32[1024]{0:T(1024)S(1)}, f32[1024]{0:T(1024)}, u32[]{:S(2)}) copy-start(f32[1024]{0:T(1024)} %get-tuple-element.178) | copy-start | bytes 12292
  277.7 12.2 %copy-start.12 = (f32[1024]{0:T(1024)S(1)}, f32[1024]{0:T(1024)}, u32[]{:S(2)}) copy-start(f32[1024]{0:T(1024)} %get-tuple-element.179) | copy-start | bytes 12292
  277.7 12.2 %copy-start.13 = (f32[1024]{0:T(1024)S(1)}, f32[1024]{0:T(1024)}, u32[]{:S(2)}) copy-start(f32[1024]{0:T(1024)} %get-tuple-element.180) | copy-start | bytes 12292
  277.7 12.2 %copy-start.14 = (f32[1024]{0:T(1024)S(1)}, f32[1024]{0:T(1024)}, u32[]{:S(2)}) copy-start(f32[1024]{0:T(1024)} %get-tuple-element.181) | copy-start | bytes 12292
  277.7 12.2 %copy-start.15 = (f32[1024]{0:T(1024)S(1)}, f32[1024]{0:T(1024)}, u32[]{:S(2)}) copy-start(f32[1024]{0:T(1024)} %get-tuple-element.182) | copy-start | bytes 12292
  277.7 12.2 %copy-start.16 = (f32[1024]{0:T(1024)S(1)}, f32[1024]{0:T(1024)}, u32[]{:S(2)}) copy-start(f32[1024]{0:T(1024)} %get-tuple-element.183) | copy-start | bytes 12292
  277.7 12.2 %copy-start.17 = (f32[1024]{0:T(1024)S(1)}, f32[1024]{0:T(1024)}, u32[]{:S(2)}) copy-start(f32[1024]{0:T(1024)} %get-tuple-element.184) | copy-start | bytes 12292
  277.7 12.2 %copy-start.18 = (f32[1024]{0:T(1024)S(1)}, f32[1024]{0:T(1024)}, u32[]{:S(2)}) copy-start(f32[1024]{0:T(1024)} %get-tuple-element.185) | copy-start | bytes 12292
  277.7 12.2 %copy-start.19 = (f32[1024]{0:T(1024)S(1)}, f32[1024]{0:T(1024)}, u32[]{:S(2)}) copy-start(f32[1024]{0:T(1024)} %get-tuple-element.186) | copy-start | bytes 12292
  277.7 12.2 %copy-start.20 = (f32[1024]{0:T(1024)S(1)}, f32[1024]{0:T(1024)}, u32[]{:S(2)}) copy-start(f32[1024]{0:T(1024)} %get-tuple-element.187) | copy-start | bytes 12292
  277.7 12.2 %copy-start.21 = (f32[1024]{0:T(1024)S(1)}, f32[1024]{0:T(1024)}, u32[]{:S(2)}) copy-start(f32[1024]{0:T(1024)} %get-tuple-element.188) | copy-start | bytes 12292
  277.7 12.2 %copy-start.22 = (f32[1024]{0:T(1024)S(1)}, f32[1024]{0:T(1024)}, u32[]{:S(2)}) copy-start(f32[1024]{0:T(1024)} %get-tuple-element.189) | copy-start | bytes 12292
  277.8 12.2 %copy-start.23 = (f32[1024]{0:T(1024)S(1)}, f32[1024]{0:T(1024)}, u32[]{:S(2)}) copy-start(f32[1024]{0:T(1024)} %get-tuple-element.190) | copy-start | bytes 12292
  277.8 12.2 %copy-start.24 = (f32[1024]{0:T(1024)S(1)}, f32[1024]{0:T(1024)}, u32[]{:S(2)}) copy-start(f32[1024]{0:T(1024)} %get-tuple-element.206) | copy-start | bytes 12292
  279.2 13.5 %copy-start.25 = (f32[1024]{0:T(1024)S(1)}, f32[1024]{0:T(1024)}, u32[]{:S(2)}) copy-start(f32[1024]{0:T(1024)} %get-tuple-element.207) | copy-start | bytes 12292
  281.3 118.7 %all-to-all-start.3 = ((bf16[32,2,6144]{2,1,0:T(2,128)(2,1)}), bf16[32,2,6144]{2,1,0:T(2,128)(2,1)}, u32[]{:S(2)}, u32[]{:S(2)}) async-start(bf16[32,2,6144]{2,1,0:T(2,128)(2,1)} %reshape.158), calls=%async_computation.3 | async-start | bytes 1572864 | tf_op jit(solution)/shard_map/all_to_all | solution.py:30
  287.3 459.9 %all-reduce.2.cloned.1.call-start = ((), (), s32[]{:S(2)}) async-start(), calls=%async_computation.4 | async-start | bytes 262144 | tf_op jit(solution)/shard_map/psum | solution.py:205
  (17 other events, 24.6 us)
Sparse Core Ops, SparseCore 0:
  294.2 452.9 all-reduce.1
where the time goes:
time: 757 us; the launch traced here: 756 us
  waiting for transfers between devices  434 us (57%)
  blocking collectives  107 us (14%)
  starting transfers between devices  72.5 us (10%)
  other arithmetic  47.4 us (6%)
  local copies, waits for them, and re-layouts  44.5 us (6%)
  matrix products  29.9 us (4%)
  between operations  14.7 us (2%)
    psum x1, waiting for transfers between devices, on_device(): grad_kernel, grad_bias = lax.psum((grad_kernel, grad_bias), ('seq', 'dp'))  338 us
    psum x1, blocking collectives, on_device(): grad_kernel, grad_bias = lax.psum((grad_kernel, grad_bias), ('seq', 'dp'))  107 us
    all_to_all x2, waiting for transfers between devices, to_heads(): lax.all_to_all(stacked, 'seq', split_axis=1, concat_axis=0, tiled=True)  72.1 us
    all_to_all x2, starting transfers between devices, to_heads(): lax.all_to_all(stacked, 'seq', split_axis=1, concat_axis=0, tiled=True)  48.5 us
    all_to_all x2, waiting for transfers between devices, to_frames(): lax.all_to_all(stacked, 'seq', split_axis=0, concat_axis=1, tiled=True)  18.8 us
    unnamed x59, local copies, waits for them, and re-layouts  17.6 us
  transfers between devices with their start and end apart: 9, of which 6 were waited for; matrix products, arithmetic and copies ran while one was open for 2% of the time, Pallas kernels for 0%

commit v1 on v0

v1 whole, which is shorter than its diff:
```python
import math

import jax
import jax.numpy as jnp
from jax import lax
from jax.experimental import pallas as pl
from jax.experimental.pallas import tpu as pltpu
from jax.sharding import PartitionSpec as P

HEADS = 16
TAPS = 31
HD = 64
LANES = 128
PAD = 16
QB = 512
KC = 512
F32 = jnp.float32
BF16 = jnp.bfloat16
NEG = -1e30
LOG2E = math.log2(math.e)

VMEM = pl.BlockSpec(memory_space=pltpu.VMEM)
SMEM = pl.BlockSpec(memory_space=pltpu.SMEM)


def params(mib):
    return pltpu.CompilerParams(vmem_limit_bytes=mib * 1024 * 1024)


def lane_pair(low, high):
    return jnp.concatenate([low, high], axis=-1)


def swap_halves(x):
    return pltpu.roll(x, HD, x.ndim - 1)


def lane_ids(shape):
    return lax.broadcasted_iota(jnp.int32, shape, len(shape) - 1)


def pack_pair(a_ref, b_ref, out_ref, u):
    rows = a_ref.shape[0]
    a = a_ref[:, u, :]
    b = b_ref[:, u, :]
    for h in range(HEADS):
        part = slice(h * HD, (h + 1) * HD)
        out_ref[u * HEADS + h, 0:rows, :] = lane_pair(a[:, part], b[:, part])


def pack_qkv_kernel(q_ref, k_ref, v_ref, out_ref):
    rows, utts, _ = q_ref.shape
    for u in range(utts):
        pack_pair(q_ref, k_ref, out_ref, u)
        v = v_ref[:, u, :]
        for h in range(HEADS):
            part = slice(h * HD, (h + 1) * HD)
            out_ref[u * HEADS + h, rows:, :] = lane_pair(
                v[: rows // 2, part], v[rows // 2 :, part]
            )


def pack_fc_kernel(f_ref, c_ref, out_ref):
    for u in range(f_ref.shape[1]):
        pack_pair(f_ref, c_ref, out_ref, u)


def unpack_pair(in_ref, a_ref, b_ref):
    rows, utts, _ = a_ref.shape
    firsts, seconds = [], []
    for u in range(utts):
        blocks = [in_ref[u * HEADS + h, 0:rows, :] for h in range(HEADS)]
        firsts.append(jnp.concatenate([x[:, :HD] for x in blocks], axis=1))
        seconds.append(jnp.concatenate([x[:, HD:] for x in blocks], axis=1))
    a_ref[...] = jnp.stack(firsts, axis=1)
    b_ref[...] = jnp.stack(seconds, axis=1)


def unpack_pair_kernel(in_ref, a_ref, b_ref):
    unpack_pair(in_ref, a_ref, b_ref)


def unpack_qkv_kernel(in_ref, q_ref, k_ref, v_ref):
    unpack_pair(in_ref, q_ref, k_ref)
    rows, utts, _ = v_ref.shape
    values = []
    for u in range(utts):
        blocks = [in_ref[u * HEADS + h, rows:, :] for h in range(HEADS)]
        top = jnp.concatenate([x[:, :HD] for x in blocks], axis=1)
        bottom = jnp.concatenate([x[:, HD:] for x in blocks], axis=1)
        values.append(jnp.concatenate([top, bottom], axis=0))
    v_ref[...] = jnp.stack(values, axis=1)


def value_rows(qkv_ref, rows):
    half = qkv_ref[:, rows:, :]
    full = jnp.concatenate([half, half], axis=1)
    lane = lane_ids(full.shape)
    return full, lane


def spread_values(qkv_ref, rows):
    half = qkv_ref[:, rows:, :].astype(F32)
    sources = half.shape[0]
    swapped = pltpu.roll(half.reshape(-1, LANES), HD, 1).reshape(half.shape)
    return jnp.concatenate([half, swapped], axis=1).reshape(sources * rows, LANES)


def forward_kernel(frames_ref, qkv_ref, e_ref, ctx_ref, kaug, vt, scores):
    rows = qkv_ref.shape[1] * 2 // 3
    sources = qkv_ref.shape[0]
    length = sources * rows
    block = pl.program_id(0)
    per_block = QB // rows

    @pl.when(block == 0)
    def _():
        qk = qkv_ref[:, :rows, :].reshape(length, LANES).astype(F32)
        lane = lane_ids(qk.shape)
        position = lax.broadcasted_iota(jnp.int32, qk.shape, 0)
        bias = jnp.where(position < frames_ref[0], 0.0, NEG)
        tail = jnp.where(lane == HD, bias, 0.0)
        kaug[...] = jnp.where(lane < HD, swap_halves(qk), tail).astype(BF16)
        values = spread_values(qkv_ref, rows)
        values = jnp.where(lane < HD, values, jnp.where(lane == HD, 1.0, 0.0))
        vt[...] = values.T.astype(BF16)

    q = qkv_ref[pl.ds(block * per_block, per_block), :rows, :].reshape(QB, LANES).astype(F32)
    lane = lane_ids(q.shape)
    q = jnp.where(lane < HD, q * 0.125, jnp.where(lane == HD, 1.0, 0.0)).astype(BF16)
    top = None
    for c in range(length // KC):
        part = slice(c * KC, (c + 1) * KC)
        s = lax.dot_general(kaug[part, :], q, (((1,), (1,)), ((), ())), preferred_element_type=F32)
        scores[part, :] = s
        high = jnp.max(s, axis=0, keepdims=True)
        top = high if top is None else jnp.maximum(top, high)
    total = None
    for c in range(length // KC):
        part = slice(c * KC, (c + 1) * KC)
        e = jnp.exp2((scores[part, :] - top) * LOG2E).astype(BF16)
        e_ref[0, part, :] = e
        term = jnp.dot(vt[:, part], e, preferred_element_type=F32)
        total = term if total is None else total + term
    total = total.T
    divisor = total[:, HD : HD + 1]
    ctx_ref[...] = jnp.where(lane < HD, total / divisor, 1.0 / divisor)


def conv_kernel_body(
    frames_ref, fc_ref, ctx_ref, taps_ref, bogf_ref, sums_ref, gaug_ref, field, grad, hid, cot, bo
):
    sources, rows, _ = fc_ref.shape
    length = sources * rows
    half = length // 2
    mid = sources // 2
    step = 64
    steps = half // step
    lane = lane_ids((half, LANES))
    valid = frames_ref[0]
    fc_low = fc_ref[:mid].reshape(half, LANES).astype(F32)
    fc_high = fc_ref[mid:].reshape(half, LANES).astype(F32)
    features = jnp.where(lane < HD, fc_low, swap_halves(fc_high))
    cot[...] = jnp.where(lane < HD, swap_halves(fc_low), fc_high)
    ctx = jnp.where(lane < HD, ctx_ref[:half, :], swap_halves(ctx_ref[half:, :]))
    hidden = features + ctx.astype(BF16).astype(F32)
    hid[...] = hidden
    position = lax.broadcasted_iota(jnp.int32, (half, LANES), 0) + jnp.where(lane < HD, 0, half)
    masked = jnp.where(position < valid, hidden, 0.0).astype(BF16).astype(F32)
    small = lane_ids((PAD, LANES))
    field[PAD : PAD + half, :] = masked
    field[:PAD, :] = jnp.where(small < HD, 0.0, swap_halves(masked[half - PAD :, :]))
    field[PAD + half :, :] = jnp.where(small < HD, swap_halves(masked[:PAD, :]), 0.0)
    sums_ref[...] = jnp.zeros_like(sums_ref)
    bias = taps_ref[TAPS : TAPS + 1, :]

    def forward_step(i, carry):
        base = pl.multiple_of(i * step, step)
        out = jnp.broadcast_to(bias, (step, LANES))
        for k in range(TAPS):
            out = out + taps_ref[k : k + 1, :] * field[pl.ds(base + (k + 1), step), :]
        gate = 1.0 / (1.0 + jnp.exp(-out))
        bo[pl.ds(base, step), :] = hid[pl.ds(base, step), :] + out * gate
        g = cot[pl.ds(base, step), :] * gate * (1.0 + out * (1.0 - gate))
        grad[pl.ds(base + PAD, step), :] = g.astype(BF16).astype(F32)
        for k in range(TAPS):
            term = g * field[pl.ds(base + (k + 1), step), :]
            part = slice(8 * k, 8 * k + 8)
            sums_ref[part, :] += jnp.sum(term.reshape(step // 8, 8, LANES), axis=0)
        part = slice(8 * TAPS, 8 * TAPS + 8)
        sums_ref[part, :] += jnp.sum(g.reshape(step // 8, 8, LANES), axis=0)
        return carry

    lax.fori_loop(0, steps, forward_step, 0)
    grad[:PAD, :] = jnp.where(small < HD, 0.0, swap_halves(grad[half : half + PAD, :]))
    grad[PAD + half :, :] = jnp.where(small < HD, swap_halves(grad[PAD : 2 * PAD, :]), 0.0)
    lane_step = lane_ids((step, LANES))
    rows_step = lax.broadcasted_iota(jnp.int32, (step, LANES), 0)
    place = rows_step + jnp.where(lane_step < HD, 0, half)
    per_step = step // rows

    def augmented(gf, context):
        inverse = context[:, HD : HD + 1]
        gn = (gf * (inverse * 0.125)).astype(BF16).astype(F32)
        delta = jnp.sum(jnp.where(lane_step < HD, gn * context, 0.0), axis=1, keepdims=True)
        upper = delta.astype(BF16).astype(F32)
        tail = jnp.where(lane_step == HD, -upper, jnp.where(lane_step == HD + 1, upper - delta, 0.0))
        return jnp.where(lane_step < HD, gn, tail).astype(BF16)

    def backward_step(i, carry):
        base = pl.multiple_of(i * step, step)
        out = None
        for k in range(TAPS):
            term = taps_ref[k : k + 1, :] * grad[pl.ds(base + (TAPS - k), step), :]
            out = term if out is None else out + term
        out = jnp.where(place + base < valid, out, 0.0)
        gf = (cot[pl.ds(base, step), :] + out).astype(BF16).astype(F32)
        swapped = swap_halves(gf)
        block = bo[pl.ds(base, step), :]
        low = jnp.where(lane_step < HD, block, swapped).astype(BF16)
        high = jnp.where(lane_step < HD, swap_halves(block), gf).astype(BF16)
        at = i * per_step
        bogf_ref[pl.ds(at, per_step)] = low.reshape(per_step, rows, LANES)
        bogf_ref[pl.ds(mid + at, per_step)] = high.reshape(per_step, rows, LANES)
        gaug_ref[pl.ds(base, step), :] = augmented(gf, ctx_ref[pl.ds(base, step), :])
        other = pl.multiple_of(base + half, step)
        gaug_ref[pl.ds(other, step), :] = augmented(swapped, ctx_ref[pl.ds(other, step), :])
        return carry

    lax.fori_loop(0, steps, backward_step, 0)


def backward_kernel(qkv_ref, gaug_ref, e_ref, out_ref, vaug, kt, gq, acc_k, acc_v):
    rows = qkv_ref.shape[1] * 2 // 3
    sources = qkv_ref.shape[0]
    length = sources * rows
    block = pl.program_id(0)
    per_block = QB // rows

    @pl.when(block == 0)
    def _():
        qk = qkv_ref[:, :rows, :].reshape(length, LANES).astype(F32)
        lane = lane_ids(qk.shape)
        kt[...] = jnp.where(lane < HD, swap_halves(qk), 0.0).T.astype(BF16)
        values = spread_values(qkv_ref, rows)
        vaug[...] = jnp.where(lane < HD, values, jnp.where(lane < HD + 2, 1.0, 0.0)).astype(BF16)
        acc_k[...] = jnp.zeros_like(acc_k)
        acc_v[...] = jnp.zeros_like(acc_v)

    q = qkv_ref[pl.ds(block * per_block, per_block), :rows, :].reshape(QB, LANES)
    g = gaug_ref[...]
    total = None
    for c in range(length // KC):
        part = slice(c * KC, (c + 1) * KC)
        e = e_ref[0, part, :]
        dp = lax.dot_general(vaug[part, :], g, (((1,), (1,)), ((), ())), preferred_element_type=F32)
        ds = (e.astype(F32) * dp).astype(BF16)
        acc_v[part, :] += jnp.dot(e, g, preferred_element_type=F32)
        acc_k[part, :] += jnp.dot(ds, q, preferred_element_type=F32)
        term = jnp.dot(kt[:, part], ds, preferred_element_type=F32)
        total = term if total is None else total + term
    gq[pl.ds(pl.multiple_of(block * QB, QB), QB), :] = total.T

    @pl.when(block == length // QB - 1)
    def _():
        lane = lane_ids((length, LANES))
        qk = jnp.where(lane < HD, gq[...], swap_halves(acc_k[...]))
        out_ref[:, :rows, :] = qk.astype(BF16).reshape(sources, rows, LANES)
        gv = acc_v[...] * 8.0
        low = gv.reshape(sources, rows, LANES)[:, : rows // 2, :]
        high = swap_halves(gv).reshape(sources, rows, LANES)[:, rows // 2 :, :]
        pick = lane_ids(low.shape) < HD
        out_ref[:, rows:, :] = jnp.where(pick, low, high).astype(BF16)


def shape_of(*dims, dtype=BF16):
    return jax.ShapeDtypeStruct(dims, dtype)


def pack_qkv(q, k, v):
    rows = q.shape[0]
    items = q.shape[1] * HEADS
    return pl.pallas_call(
        pack_qkv_kernel,
        out_shape=shape_of(items, rows * 3 // 2, LANES),
        in_specs=[VMEM] * 3,
        out_specs=VMEM,
        compiler_params=params(24),
        name="pack_qkv",
    )(q, k, v)


def pack_fc(f, c):
    rows = f.shape[0]
    items = f.shape[1] * HEADS
    return pl.pallas_call(
        pack_fc_kernel,
        out_shape=shape_of(items, rows, LANES),
        in_specs=[VMEM] * 2,
        out_specs=VMEM,
        compiler_params=params(24),
        name="pack_fc",
    )(f, c)


def unpack(kernel, field, rows, utts, count):
    return pl.pallas_call(
        kernel,
        out_shape=[shape_of(rows, utts, HEADS * HD)] * count,
        in_specs=[VMEM],
        out_specs=[VMEM] * count,
        compiler_params=params(24),
        name="unpack%d" % count,
    )(field)


def forward(frames, qkv):
    sources, tall, _ = qkv.shape
    length = sources * (tall * 2 // 3)
    blocks = length // QB
    return pl.pallas_call(
        forward_kernel,
        grid=(blocks,),
        out_shape=[shape_of(blocks, length, QB), shape_of(length, LANES, dtype=F32)],
        in_specs=[SMEM, VMEM],
        out_specs=[
            pl.BlockSpec((1, length, QB), lambda i: (i, 0, 0)),
            pl.BlockSpec((QB, LANES), lambda i: (i, 0)),
        ],
        scratch_shapes=[
            pltpu.VMEM((length, LANES), BF16),
            pltpu.VMEM((LANES, length), BF16),
            pltpu.VMEM((length, QB), F32),
        ],
        compiler_params=params(32),
        cost_estimate=pl.CostEstimate(
            flops=40_000_000_000 // 4, bytes_accessed=10_000_000, transcendentals=length * length
        ),
        name="attention_forward",
    )(frames, qkv)


def conv(frames, fc, ctx, taps):
    sources, rows, _ = fc.shape
    length = sources * rows
    half = length // 2
    return pl.pallas_call(
        conv_kernel_body,
        out_shape=[
            shape_of(sources, rows, LANES),
            shape_of(8 * (TAPS + 1), LANES, dtype=F32),
            shape_of(length, LANES),
        ],
        in_specs=[SMEM, VMEM, VMEM, VMEM],
        out_specs=[VMEM] * 3,
        scratch_shapes=[
            pltpu.VMEM((half + 2 * PAD, LANES), F32),
            pltpu.VMEM((half + 2 * PAD, LANES), F32),
            pltpu.VMEM((half, LANES), F32),
            pltpu.VMEM((half, LANES), F32),
            pltpu.VMEM((half, LANES), F32),
        ],
        compiler_params=params(32),
        name="conv",
    )(frames, fc, ctx, taps)


def backward(qkv, gaug, e):
    sources, tall, _ = qkv.shape
    length = sources * (tall * 2 // 3)
    blocks = length // QB
    return pl.pallas_call(
        backward_kernel,
        grid=(blocks,),
        out_shape=shape_of(sources, tall, LANES),
        in_specs=[
            VMEM,
            pl.BlockSpec((QB, LANES), lambda i: (i, 0)),
            pl.BlockSpec((1, length, QB), lambda i: (i, 0, 0)),
        ],
        out_specs=VMEM,
        scratch_shapes=[
            pltpu.VMEM((length, LANES), BF16),
            pltpu.VMEM((LANES, length), BF16),
            pltpu.VMEM((length, LANES), F32),
            pltpu.VMEM((length, LANES), F32),
            pltpu.VMEM((length, LANES), F32),
        ],
        compiler_params=params(32),
        cost_estimate=pl.CostEstimate(
            flops=20_000_000_000, bytes_accessed=10_000_000, transcendentals=0
        ),
        name="attention_backward",
    )(qkv, gaug, e)


def exchange(field):
    return lax.all_to_all(field, "seq", split_axis=0, concat_axis=0, tiled=True)


def swap(field, axis, bit):
    count = lax.axis_size(axis)
    return lax.ppermute(field, axis, [(i, i ^ bit) for i in range(count)])


def joined(field, axis, bit):
    other = swap(field, axis, bit)
    upper = (lax.axis_index(axis) & bit) != 0
    first = jnp.where(upper, other, field)
    second = jnp.where(upper, field, other)
    return jnp.concatenate([first, second], axis=0)


def reduce_params(sums):
    part = jnp.sum(sums.reshape(TAPS + 1, 8, 2, HD), axis=(1, 2))
    for bit in (1, 2, 4, 8):
        part = part + swap(part, "dp", bit)
    part = part + swap(part, "seq", HEADS)
    part = part[None]
    for bit in (1, 2, 4, 8):
        part = joined(part, "seq", bit)
    whole = jnp.moveaxis(part, 0, 1).reshape(TAPS + 1, HEADS * HD)
    return whole[:TAPS], whole[TAPS]


def on_device(
    queries, key_vectors, value_vectors, features, cotangent, frames, conv_kernel, conv_bias
):
    rows, utts, _ = queries.shape
    item = lax.axis_index("seq")
    utt = item // HEADS
    head = item % HEADS
    valid = jnp.sum(jnp.where(jnp.arange(utts) == utt, frames, 0), keepdims=True)
    taps = jnp.concatenate([conv_kernel, conv_bias[None]], axis=0)
    taps = lax.dynamic_slice_in_dim(taps, head * HD, HD, axis=1)
    taps = jnp.concatenate([taps, taps], axis=1)

    qkv = exchange(pack_qkv(queries, key_vectors, value_vectors))
    fc = exchange(pack_fc(features, cotangent))
    e, ctx = forward(valid, qkv)
    bogf, sums, gaug = conv(valid, fc, ctx, taps)
    bogf = exchange(bogf)
    grads = exchange(backward(qkv, gaug, e))
    grad_kernel, grad_bias = reduce_params(sums)
    block_out, grad_features = unpack(unpack_pair_kernel, bogf, rows, utts, 2)
    grad_q, grad_k, grad_v = unpack(unpack_qkv_kernel, grads, rows, utts, 3)
    return block_out, grad_features, grad_q, grad_k, grad_v, grad_kernel, grad_bias


def solution(mesh):
    field = P("seq", "dp", None)
    return jax.shard_map(
        on_device,
        mesh=mesh,
        in_specs=(field,) * 5 + (P("dp"), P(), P()),
        out_specs=(field,) * 5 + (P(), P()),
        check_vma=False,
    )
```

time: 757 us -> 270 us (0.36)
  waiting for transfers between devices: 434 us -> 121 us
  blocking collectives: 107 us -> 0 us
  other arithmetic: 47.4 us -> 2.61 us
  Pallas kernels: 0 us -> 38.4 us
  local copies, waits for them, and re-layouts: 44.5 us -> 13 us
  matrix products: 29.9 us -> 0 us
  starting transfers between devices: 72.5 us -> 92.5 us
  between operations: 14.7 us -> 0.91 us
    psum x1 -> x0, waiting for transfers between devices: 338 us -> none  [on_device(): grad_kernel, grad_bias = lax.psum((grad_kernel, grad_bias), ('seq', 'dp'))]
    psum x1 -> x0, blocking collectives: 107 us -> none  [on_device(): grad_kernel, grad_bias = lax.psum((grad_kernel, grad_bias), ('seq', 'dp'))]
    ppermute x4 -> x9, waiting for transfers between devices: 4.58 us -> 55.1 us  [swap(): return lax.ppermute(field, axis, [(i, i ^ bit) for i in range(count)])]
    pallas_call x0 -> x7, Pallas kernels: none -> 38.4 us  [the longest x1 10.6 us: backward(): pl.pallas_call(backward_kernel, grid=(blocks,), out_shape=shape_of(source...]
    ppermute x4 -> x9, starting transfers between devices: 9.89 us -> 46.6 us  [swap(): return lax.ppermute(field, axis, [(i, i ^ bit) for i in range(count)])]
    dot_general x28 -> x0, matrix products: 29.9 us -> none  [the longest x8 6.37 us: block_probs(): jnp.einsum('qd,kd->qk', query_block, key_rows, preferred_element_type=jnp...]
    all_to_all x4, waiting for transfers between devices: 90.9 us -> 66.1 us  [exchange(): return lax.all_to_all(field, 'seq', split_axis=0, concat_axis=0, tiled=True)]
    all_to_all x4, starting transfers between devices: 62.6 us -> 45.9 us  [exchange(): return lax.all_to_all(field, 'seq', split_axis=0, concat_axis=0, tiled=True)]
  transfers between devices with their start and end apart: 9 -> 13, of which waited for: 6 -> 12; matrix products, arithmetic and copies ran while one was open for 2% -> 2% of each run, Pallas kernels for 0% -> 9%
where the time goes in v1:
time: 270 us; the launch traced here: 269 us
  waiting for transfers between devices  121 us (45%)
  starting transfers between devices  92.5 us (34%)
  Pallas kernels  38.4 us (14%)
  local copies, waits for them, and re-layouts  13 us (5%)
    all_to_all x4, waiting for transfers between devices, exchange(): return lax.all_to_all(field, 'seq', split_axis=0, concat_axis=0, tiled=True)  66.1 us
    ppermute x9, waiting for transfers between devices, swap(): return lax.ppermute(field, axis, [(i, i ^ bit) for i in range(count)])  55.1 us
    ppermute x9, starting transfers between devices, swap(): return lax.ppermute(field, axis, [(i, i ^ bit) for i in range(count)])  46.6 us
    all_to_all x4, starting transfers between devices, exchange(): return lax.all_to_all(field, 'seq', split_axis=0, concat_axis=0, tiled=True)  45.9 us
    unnamed x14, local copies, waits for them, and re-layouts  11.4 us
    pallas_call x1, Pallas kernels, backward(): pl.pallas_call(backward_kernel, grid=(blocks,), out_shape=shape_of(source...  10.6 us
    pallas_call x1, Pallas kernels, forward(): pl.pallas_call(forward_kernel, grid=(blocks,), out_shape=[shape_of(blocks...  9.26 us
    pallas_call x1, Pallas kernels, conv(): pl.pallas_call(conv_kernel_body, out_shape=[shape_of(sources, rows, LANES...  8.7 us
  transfers between devices with their start and end apart: 13, of which 12 were waited for; matrix products, arithmetic and copies ran while one was open for 2% of the time, Pallas kernels for 9%

profile of v1, /device:TPU:1, one launch (start us, length us, event | category | flops | bytes accessed | tf_op | source)
XLA Modules:
  0.0 268.7 jit_solution(3173975830336617358)
XLA Ops:
  3.5 3.4 %pack_qkv.1 = bf16[32,96,128]{2,1,0:T(8,128)(2,1)} custom-call(bf16[64,2,1024]{2,1,0:T(2,128)(2,1)S(1)} %copy-done, bf16[64,2,1024]{2,1,0:T(2,128)(2,1)S(1)} %copy-done.1, bf16[64,2,1024]{2,1,0:T(2,128)(2,1)S(1)} %copy-done.2), custom_call_target="tpu_custom_call" | custom-call | tf_op jit(solution)/shard_map/pack_qkv/pallas_call | solution.py:283
  6.9 19.2 %all-to-all-start.1 = ((bf16[32,96,128]{2,1,0:T(8,128)(2,1)}), bf16[32,96,128]{2,1,0:T(8,128)(2,1)S(1)}, u32[]{:S(2)}, u32[]{:S(2)}) async-start(bf16[32,96,128]{2,1,0:T(8,128)(2,1)} %pack_qkv.1), calls=%async_computation.1 | async-start | bytes 1572864 | tf_op jit(solution)/shard_map/all_to_all | solution.py:398
  28.0 2.5 pack_fc.1
  30.5 36.3 %all-to-all-done.1.qkv_ref = bf16[32,96,128]{2,1,0:T(8,128)(2,1)S(1)} async-done(((bf16[32,96,128]{2,1,0:T(8,128)(2,1)}), bf16[32,96,128]{2,1,0:T(8,128)(2,1)S(1)}, u32[]{:S(2)}, u32[]{:S(2)}) %all-to-all-start.1) | async-done | bytes 786464 | tf_op jit(solution)/shard_map/all_to_all | solution.py:398
  66.8 8.8 %all-to-all-start = ((bf16[32,64,128]{2,1,0:T(8,128)(2,1)}), bf16[32,64,128]{2,1,0:T(8,128)(2,1)S(1)}, u32[]{:S(2)}, u32[]{:S(2)}) async-start(bf16[32,64,128]{2,1,0:T(8,128)(2,1)} %pack_fc.1), calls=%async_computation | async-start | bytes 1048576 | tf_op jit(solution)/shard_map/all_to_all | solution.py:398
  75.6 1.3 fusion.1
  77.7 9.3 %attention_forward.1 = (bf16[4,2048,512]{2,1,0:T(8,128)(2,1)S(1)}, f32[2048,128]{1,0:T(8,128)S(1)}) custom-call(s32[1]{0:T(128)} %bitcast.frames_ref, bf16[32,96,128]{2,1,0:T(8,128)(2,1)S(1)} %all-to-all-done.1.qkv_ref), custom_call_target="tpu_custom_call" | custom-call | flops 10000000000 | bytes 10000000 | tf_op jit(solution)/shard_map/attention_forward/pallas_call | solution.py:321
  87.0 3.3 %copy-done.5 = bf16[4,2048,512]{2,1,0:T(8,128)(2,1)} copy-done((bf16[4,2048,512]{2,1,0:T(8,128)(2,1)}, bf16[4,2048,512]{2,1,0:T(8,128)(2,1)S(1)}, u32[]{:S(2)}) %copy-start.5) | copy-done | bytes 8388632
  90.3 14.0 %all-to-all-done.fc_ref = bf16[32,64,128]{2,1,0:T(8,128)(2,1)S(1)} async-done(((bf16[32,64,128]{2,1,0:T(8,128)(2,1)}), bf16[32,64,128]{2,1,0:T(8,128)(2,1)S(1)}, u32[]{:S(2)}, u32[]{:S(2)}) %all-to-all-start) | async-done | bytes 524320 | tf_op jit(solution)/shard_map/all_to_all | solution.py:398
  104.3 8.7 %conv.1 = (bf16[32,64,128]{2,1,0:T(8,128)(2,1)}, f32[256,128]{1,0:T(8,128)S(1)}, bf16[2048,128]{1,0:T(8,128)(2,1)S(1)}) custom-call(s32[1]{0:T(128)} %bitcast.frames_ref, bf16[32,64,128]{2,1,0:T(8,128)(2,1)S(1)} %all-to-all-done.fc_ref, f32[2048,128]{1,0:T(8,128)S(1)} %get-tuple-element.17.ctx_ref, f32[32,128]{1,0:T(8,128)S(1)} %pad_maximum_fusion.3.taps_ref), custom_call_target="tpu_custom_call" | custom-call | tf_op jit(solution)/shard_map/conv/pallas_call | solution.py:347
  113.0 9.5 %all-to-all-start.2 = ((bf16[32,64,128]{2,1,0:T(8,128)(2,1)}), bf16[32,64,128]{2,1,0:T(8,128)(2,1)S(1)}, u32[]{:S(2)}, u32[]{:S(2)}) async-start(bf16[32,64,128]{2,1,0:T(8,128)(2,1)} %get-tuple-element.18), calls=%async_computation.2 | async-start | bytes 1048576 | tf_op jit(solution)/shard_map/all_to_all | solution.py:398
  122.5 3.4 %copy-done.6 = bf16[4,2048,512]{2,1,0:T(8,128)(2,1)S(1)} copy-done((bf16[4,2048,512]{2,1,0:T(8,128)(2,1)S(1)}, bf16[4,2048,512]{2,1,0:T(8,128)(2,1)}, u32[]{:S(2)}) %copy-start.6) | copy-done | bytes 8388632
  125.9 10.6 %attention_backward.1 = bf16[32,96,128]{2,1,0:T(8,128)(2,1)} custom-call(bf16[32,96,128]{2,1,0:T(8,128)(2,1)S(1)} %all-to-all-done.1.qkv_ref, bf16[2048,128]{1,0:T(8,128)(2,1)S(1)} %get-tuple-element.21.gaug_ref, bf16[4,2048,512]{2,1,0:T(8,128)(2,1)S(1)} %copy-done.6), custom_call_target="tpu_custom_call" | custom-call | flops 20000000000 | bytes 10000000 | tf_op jit(solution)/shard_map/attention_backward/pallas_call | solution.py:372
  136.5 15.8 %all-to-all-done.2.in_ref = bf16[32,64,128]{2,1,0:T(8,128)(2,1)S(1)} async-done(((bf16[32,64,128]{2,1,0:T(8,128)(2,1)}), bf16[32,64,128]{2,1,0:T(8,128)(2,1)S(1)}, u32[]{:S(2)}, u32[]{:S(2)}) %all-to-all-start.2) | async-done | bytes 524320 | tf_op jit(solution)/shard_map/all_to_all | solution.py:398
  152.3 8.4 %all-to-all-start.3 = ((bf16[32,96,128]{2,1,0:T(8,128)(2,1)}), bf16[32,96,128]{2,1,0:T(8,128)(2,1)S(1)}, u32[]{:S(2)}, u32[]{:S(2)}) async-start(bf16[32,96,128]{2,1,0:T(8,128)(2,1)} %attention_backward.1), calls=%async_computation.3 | async-start | bytes 1572864 | tf_op jit(solution)/shard_map/all_to_all | solution.py:398
  161.1 2.9 %collective-permute-start = (f32[32,64]{1,0:T(8,128)S(1)}, f32[32,64]{1,0:T(8,128)S(1)}, u32[]{:S(2)}, u32[]{:S(2)}) collective-permute-start(f32[32,64]{1,0:T(8,128)S(1)} %reduce_sum.19), channel_id=1, source_target_pairs={{0,1},{1,0},{2,3},{3,2},{4,5},{5,4},{6,7},{7,6},{8,9},{9,8},{10,11... | collective-permute-start | bytes 24584 | tf_op jit(solution)/shard_map/ppermute | solution.py:403
  164.0 31.1 %collective-permute-done = f32[32,64]{1,0:T(8,128)S(1)} collective-permute-done((f32[32,64]{1,0:T(8,128)S(1)}, f32[32,64]{1,0:T(8,128)S(1)}, u32[]{:S(2)}, u32[]{:S(2)}) %collective-permute-start) | collective-permute-done | bytes 8224 | tf_op jit(solution)/shard_map/ppermute | solution.py:403
  195.1 1.9 collective-permute-start.1
  197.0 3.9 %collective-permute-done.1 = f32[32,64]{1,0:T(8,128)S(1)} collective-permute-done((f32[32,64]{1,0:T(8,128)S(1)}, f32[32,64]{1,0:T(8,128)S(1)}, u32[]{:S(2)}, u32[]{:S(2)}) %collective-permute-start.1) | collective-permute-done | bytes 8224 | tf_op jit(solution)/shard_map/ppermute | solution.py:403
  200.9 3.2 %collective-permute-start.2 = (f32[32,64]{1,0:T(8,128)S(1)}, f32[32,64]{1,0:T(8,128)S(1)}, u32[]{:S(2)}, u32[]{:S(2)}) collective-permute-start(f32[32,64]{1,0:T(8,128)S(1)} %add.26), channel_id=1, source_target_pairs={{0,4},{1,5},{2,6},{3,7},{4,0},{5,1},{6,2},{7,3},{8,12},{9,13},{10,... | collective-permute-start | bytes 24584 | tf_op jit(solution)/shard_map/ppermute | solution.py:403
  204.1 1.3 collective-permute-done.2
  205.4 4.8 %collective-permute-start.3 = (f32[32,64]{1,0:T(8,128)S(1)}, f32[32,64]{1,0:T(8,128)S(1)}, u32[]{:S(2)}, u32[]{:S(2)}) collective-permute-start(f32[32,64]{1,0:T(8,128)S(1)} %add.27), channel_id=1, source_target_pairs={{0,8},{1,9},{2,10},{3,11},{4,12},{5,13},{6,14},{7,15},{8,0},{9,1},... | collective-permute-start | bytes 24584 | tf_op jit(solution)/shard_map/ppermute | solution.py:403
  211.4 12.9 %collective-permute-start.4 = (f32[32,64]{1,0:T(8,128)S(1)}, f32[32,64]{1,0:T(8,128)S(1)}, u32[]{:S(2)}, u32[]{:S(2)}) collective-permute-start(f32[32,64]{1,0:T(8,128)S(1)} %add.28), channel_id=1, source_target_pairs={{0,256},{16,272},{32,288},{48,304},{64,320},{80,336},{96,352},{112... | collective-permute-start | bytes 24584 | tf_op jit(solution)/shard_map/ppermute | solution.py:403
  225.4 6.7 %collective-permute-start.5 = (f32[1,32,64]{2,0,1:T(1,128)S(1)}, f32[1,32,64]{2,0,1:T(1,128)S(1)}, u32[]{:S(2)}, u32[]{:S(2)}) collective-permute-start(f32[1,32,64]{2,0,1:T(1,128)S(1)} %bitcast.13), channel_id=1, source_target_pairs={{0,16},{16,0},{32,48},{48,32},{64,80},{80,64},{96,112},{112,96},{1... | collective-permute-start | bytes 24584 | tf_op jit(solution)/shard_map/ppermute | solution.py:403
  232.9 3.4 %collective-permute-start.6 = (f32[2,32,64]{2,0,1:T(2,128)S(1)}, f32[2,32,64]{2,0,1:T(2,128)S(1)}, u32[]{:S(2)}, u32[]{:S(2)}) collective-permute-start(f32[2,32,64]{2,0,1:T(2,128)S(1)} %pad_maximum_fusion.2), channel_id=1, source_target_pairs={{0,32},{16,48},{32,0},{48,16},{64,96},{80,112},{96,64},{112,80},{1... | collective-permute-start | bytes 49160 | tf_op jit(solution)/shard_map/ppermute | solution.py:403
  236.4 1.3 collective-permute-done.6
  237.8 4.6 %collective-permute-start.7 = (f32[4,32,64]{2,0,1:T(4,128)S(1)}, f32[4,32,64]{2,0,1:T(4,128)S(1)}, u32[]{:S(2)}, u32[]{:S(2)}) collective-permute-start(f32[4,32,64]{2,0,1:T(4,128)S(1)} %pad_maximum_fusion.1), channel_id=1, source_target_pairs={{0,64},{16,80},{32,96},{48,112},{64,0},{80,16},{96,32},{112,48},{1... | collective-permute-start | bytes 98312 | tf_op jit(solution)/shard_map/ppermute | solution.py:403
  242.4 1.9 collective-permute-done.7
  244.4 6.2 %collective-permute-start.8 = (f32[8,32,64]{2,0,1:T(8,128)S(1)}, f32[8,32,64]{2,0,1:T(8,128)S(1)}, u32[]{:S(2)}, u32[]{:S(2)}) collective-permute-start(f32[8,32,64]{2,0,1:T(8,128)S(1)} %pad_maximum_fusion), channel_id=1, source_target_pairs={{0,128},{16,144},{32,160},{48,176},{64,192},{80,208},{96,224},{112... | collective-permute-start | bytes 196616 | tf_op jit(solution)/shard_map/ppermute | solution.py:403
  250.6 12.5 %collective-permute-done.8 = f32[8,32,64]{2,0,1:T(8,128)S(1)} collective-permute-done((f32[8,32,64]{2,0,1:T(8,128)S(1)}, f32[8,32,64]{2,0,1:T(8,128)S(1)}, u32[]{:S(2)}, u32[]{:S(2)}) %collective-permute-start.8) | collective-permute-done | bytes 65568 | tf_op jit(solution)/shard_map/ppermute | solution.py:403
  264.7 1.7 unpack2.1
  266.5 2.2 unpack3.1
  (37 shorter events, 10.8 us)
Async XLA Ops:
  0.6 1.0 copy-start
  1.6 0.9 copy-start.1
  2.5 0.9 copy-start.2
  6.9 59.9 %all-to-all-start.1 = ((bf16[32,96,128]{2,1,0:T(8,128)(2,1)}), bf16[32,96,128]{2,1,0:T(8,128)(2,1)S(1)}, u32[]{:S(2)}, u32[]{:S(2)}) async-start(bf16[32,96,128]{2,1,0:T(8,128)(2,1)} %pack_qkv.1), calls=%async_computation.1 | async-start | bytes 1572864 | tf_op jit(solution)/shard_map/all_to_all | solution.py:398
  26.1 1.0 copy-start.3
  27.0 0.9 copy-start.4
  66.8 37.5 %all-to-all-start = ((bf16[32,64,128]{2,1,0:T(8,128)(2,1)}), bf16[32,64,128]{2,1,0:T(8,128)(2,1)S(1)}, u32[]{:S(2)}, u32[]{:S(2)}) async-start(bf16[32,64,128]{2,1,0:T(8,128)(2,1)} %pack_fc.1), calls=%async_computation | async-start | bytes 1048576 | tf_op jit(solution)/shard_map/all_to_all | solution.py:398
  87.0 3.3 %copy-start.5 = (bf16[4,2048,512]{2,1,0:T(8,128)(2,1)}, bf16[4,2048,512]{2,1,0:T(8,128)(2,1)S(1)}, u32[]{:S(2)}) copy-start(bf16[4,2048,512]{2,1,0:T(8,128)(2,1)S(1)} %get-tuple-element.22.e_ref) | copy-start | bytes 25165828
  113.0 39.3 %all-to-all-start.2 = ((bf16[32,64,128]{2,1,0:T(8,128)(2,1)}), bf16[32,64,128]{2,1,0:T(8,128)(2,1)S(1)}, u32[]{:S(2)}, u32[]{:S(2)}) async-start(bf16[32,64,128]{2,1,0:T(8,128)(2,1)} %get-tuple-element.18), calls=%async_computation.2 | async-start | bytes 1048576 | tf_op jit(solution)/shard_map/all_to_all | solution.py:398
  122.5 3.4 %copy-start.6 = (bf16[4,2048,512]{2,1,0:T(8,128)(2,1)S(1)}, bf16[4,2048,512]{2,1,0:T(8,128)(2,1)}, u32[]{:S(2)}) copy-start(bf16[4,2048,512]{2,1,0:T(8,128)(2,1)} %copy-done.5) | copy-start | bytes 25165828
  152.3 114.1 %all-to-all-start.3 = ((bf16[32,96,128]{2,1,0:T(8,128)(2,1)}), bf16[32,96,128]{2,1,0:T(8,128)(2,1)S(1)}, u32[]{:S(2)}, u32[]{:S(2)}) async-start(bf16[32,96,128]{2,1,0:T(8,128)(2,1)} %attention_backward.1), calls=%async_computation.3 | async-start | bytes 1572864 | tf_op jit(solution)/shard_map/all_to_all | solution.py:398
  161.1 34.0 %collective-permute-start = (f32[32,64]{1,0:T(8,128)S(1)}, f32[32,64]{1,0:T(8,128)S(1)}, u32[]{:S(2)}, u32[]{:S(2)}) collective-permute-start(f32[32,64]{1,0:T(8,128)S(1)} %reduce_sum.19), channel_id=1, source_target_pairs={{0,1},{1,0},{2,3},{3,2},{4,5},{5,4},{6,7},{7,6},{8,9},{9,8},{10,11... | collective-permute-start | bytes 24584 | tf_op jit(solution)/shard_map/ppermute | solution.py:403
  195.1 5.8 %collective-permute-start.1 = (f32[32,64]{1,0:T(8,128)S(1)}, f32[32,64]{1,0:T(8,128)S(1)}, u32[]{:S(2)}, u32[]{:S(2)}) collective-permute-start(f32[32,64]{1,0:T(8,128)S(1)} %add.25), channel_id=1, source_target_pairs={{0,2},{1,3},{2,0},{3,1},{4,6},{5,7},{6,4},{7,5},{8,10},{9,11},{10,... | collective-permute-start | bytes 24584 | tf_op jit(solution)/shard_map/ppermute | solution.py:403
  200.9 4.5 %collective-permute-start.2 = (f32[32,64]{1,0:T(8,128)S(1)}, f32[32,64]{1,0:T(8,128)S(1)}, u32[]{:S(2)}, u32[]{:S(2)}) collective-permute-start(f32[32,64]{1,0:T(8,128)S(1)} %add.26), channel_id=1, source_target_pairs={{0,4},{1,5},{2,6},{3,7},{4,0},{5,1},{6,2},{7,3},{8,12},{9,13},{10,... | collective-permute-start | bytes 24584 | tf_op jit(solution)/shard_map/ppermute | solution.py:403
  205.4 6.0 %collective-permute-start.3 = (f32[32,64]{1,0:T(8,128)S(1)}, f32[32,64]{1,0:T(8,128)S(1)}, u32[]{:S(2)}, u32[]{:S(2)}) collective-permute-start(f32[32,64]{1,0:T(8,128)S(1)} %add.27), channel_id=1, source_target_pairs={{0,8},{1,9},{2,10},{3,11},{4,12},{5,13},{6,14},{7,15},{8,0},{9,1},... | collective-permute-start | bytes 24584 | tf_op jit(solution)/shard_map/ppermute | solution.py:403
  211.4 14.0 %collective-permute-start.4 = (f32[32,64]{1,0:T(8,128)S(1)}, f32[32,64]{1,0:T(8,128)S(1)}, u32[]{:S(2)}, u32[]{:S(2)}) collective-permute-start(f32[32,64]{1,0:T(8,128)S(1)} %add.28), channel_id=1, source_target_pairs={{0,256},{16,272},{32,288},{48,304},{64,320},{80,336},{96,352},{112... | collective-permute-start | bytes 24584 | tf_op jit(solution)/shard_map/ppermute | solution.py:403
  225.4 7.5 %collective-permute-start.5 = (f32[1,32,64]{2,0,1:T(1,128)S(1)}, f32[1,32,64]{2,0,1:T(1,128)S(1)}, u32[]{:S(2)}, u32[]{:S(2)}) collective-permute-start(f32[1,32,64]{2,0,1:T(1,128)S(1)} %bitcast.13), channel_id=1, source_target_pairs={{0,16},{16,0},{32,48},{48,32},{64,80},{80,64},{96,112},{112,96},{1... | collective-permute-start | bytes 24584 | tf_op jit(solution)/shard_map/ppermute | solution.py:403
  232.9 4.7 %collective-permute-start.6 = (f32[2,32,64]{2,0,1:T(2,128)S(1)}, f32[2,32,64]{2,0,1:T(2,128)S(1)}, u32[]{:S(2)}, u32[]{:S(2)}) collective-permute-start(f32[2,32,64]{2,0,1:T(2,128)S(1)} %pad_maximum_fusion.2), channel_id=1, source_target_pairs={{0,32},{16,48},{32,0},{48,16},{64,96},{80,112},{96,64},{112,80},{1... | collective-permute-start | bytes 49160 | tf_op jit(solution)/shard_map/ppermute | solution.py:403
  237.8 6.5 %collective-permute-start.7 = (f32[4,32,64]{2,0,1:T(4,128)S(1)}, f32[4,32,64]{2,0,1:T(4,128)S(1)}, u32[]{:S(2)}, u32[]{:S(2)}) collective-permute-start(f32[4,32,64]{2,0,1:T(4,128)S(1)} %pad_maximum_fusion.1), channel_id=1, source_target_pairs={{0,64},{16,80},{32,96},{48,112},{64,0},{80,16},{96,32},{112,48},{1... | collective-permute-start | bytes 98312 | tf_op jit(solution)/shard_map/ppermute | solution.py:403
  244.4 18.8 %collective-permute-start.8 = (f32[8,32,64]{2,0,1:T(8,128)S(1)}, f32[8,32,64]{2,0,1:T(8,128)S(1)}, u32[]{:S(2)}, u32[]{:S(2)}) collective-permute-start(f32[8,32,64]{2,0,1:T(8,128)S(1)} %pad_maximum_fusion), channel_id=1, source_target_pairs={{0,128},{16,144},{32,160},{48,176},{64,192},{80,208},{96,224},{112... | collective-permute-start | bytes 196616 | tf_op jit(solution)/shard_map/ppermute | solution.py:403

commit v2 on v1

v2 whole, which is shorter than its diff:
```python
import math

import jax
import jax.numpy as jnp
from jax import lax
from jax.experimental import pallas as pl
from jax.experimental.pallas import tpu as pltpu
from jax.sharding import PartitionSpec as P

HEADS = 16
TAPS = 31
HD = 64
LANES = 128
PAD = 16
QB = 1024
KC = 256
F32 = jnp.float32
BF16 = jnp.bfloat16
NEG = -1e30
LOG2E = math.log2(math.e)

VMEM = pl.BlockSpec(memory_space=pltpu.VMEM)
SMEM = pl.BlockSpec(memory_space=pltpu.SMEM)


def params(mib):
    return pltpu.CompilerParams(vmem_limit_bytes=mib * 1024 * 1024)


def lane_pair(low, high):
    return jnp.concatenate([low, high], axis=-1)


def swap_halves(x):
    return pltpu.roll(x, HD, x.ndim - 1)


def lane_ids(shape):
    return lax.broadcasted_iota(jnp.int32, shape, len(shape) - 1)


def pack_kernel(q_hbm, k_hbm, v_hbm, f_hbm, c_hbm, out_ref, q_ref, k_ref, v_ref, f_ref, c_ref, sems):
    pairs = ((q_hbm, q_ref), (k_hbm, k_ref), (v_hbm, v_ref), (f_hbm, f_ref), (c_hbm, c_ref))
    copies = [pltpu.make_async_copy(a, b, sems.at[n]) for n, (a, b) in enumerate(pairs)]
    for copy in copies:
        copy.start()
    rows, utts, _ = q_ref.shape

    def pair(a_ref, b_ref, first):
        for u in range(utts):
            a = a_ref[:, u, :]
            b = b_ref[:, u, :]
            for h in range(HEADS):
                part = slice(h * HD, (h + 1) * HD)
                out_ref[u * HEADS + h, first : first + rows, :] = lane_pair(a[:, part], b[:, part])

    copies[0].wait()
    copies[1].wait()
    pair(q_ref, k_ref, 0)
    copies[2].wait()
    for u in range(utts):
        v = v_ref[:, u, :]
        for h in range(HEADS):
            part = slice(h * HD, (h + 1) * HD)
            out_ref[u * HEADS + h, rows : rows * 3 // 2, :] = lane_pair(
                v[: rows // 2, part], v[rows // 2 :, part]
            )
    copies[3].wait()
    copies[4].wait()
    pair(f_ref, c_ref, rows * 3 // 2)


def unpack_kernel(in_ref, q_ref, k_ref, v_ref, f_ref, c_ref):
    rows, utts, _ = q_ref.shape

    def pair(a_ref, b_ref, first):
        firsts, seconds = [], []
        for u in range(utts):
            blocks = [in_ref[u * HEADS + h, first : first + rows, :] for h in range(HEADS)]
            firsts.append(jnp.concatenate([x[:, :HD] for x in blocks], axis=1))
            seconds.append(jnp.concatenate([x[:, HD:] for x in blocks], axis=1))
        a_ref[...] = jnp.stack(firsts, axis=1)
        b_ref[...] = jnp.stack(seconds, axis=1)

    pair(f_ref, c_ref, rows * 3 // 2)
    pair(q_ref, k_ref, 0)
    values = []
    for u in range(utts):
        blocks = [in_ref[u * HEADS + h, rows : rows * 3 // 2, :] for h in range(HEADS)]
        top = jnp.concatenate([x[:, :HD] for x in blocks], axis=1)
        bottom = jnp.concatenate([x[:, HD:] for x in blocks], axis=1)
        values.append(jnp.concatenate([top, bottom], axis=0))
    v_ref[...] = jnp.stack(values, axis=1)


def attend_forward(valid, in_ref, e_ref, ctx_ref, kaug, vaug, vt, kt, scores):
    sources = in_ref.shape[0]
    rows = in_ref.shape[1] * 2 // 5
    length = sources * rows
    per_block = QB // rows
    blocks = length // QB

    qk = in_ref[:, :rows, :].reshape(length, LANES).astype(F32)
    lane = lane_ids(qk.shape)
    position = lax.broadcasted_iota(jnp.int32, qk.shape, 0)
    bias = jnp.where(position < valid, 0.0, NEG)
    keys = jnp.where(lane < HD, swap_halves(qk), jnp.where(lane == HD, bias, 0.0))
    kaug[...] = keys.astype(BF16)
    half = in_ref[:, rows : rows * 3 // 2, :].astype(F32)
    swapped = swap_halves(half.reshape(length // 2, LANES)).reshape(half.shape)
    values = jnp.concatenate([half, swapped], axis=1).reshape(length, LANES)
    values = jnp.where(lane < HD, values, jnp.where(lane < HD + 2, 1.0, 0.0))
    vaug[...] = values.astype(BF16)
    vt[...] = values.T.astype(BF16)
    kt[...] = jnp.where(lane < HD, keys, 0.0).T.astype(BF16)

    def query_block(block):
        q = in_ref[pl.ds(block * per_block, per_block), :rows, :].reshape(QB, LANES).astype(F32)
        lane = lane_ids(q.shape)
        return jnp.where(lane < HD, q * 0.125, jnp.where(lane == HD, 1.0, 0.0)).astype(BF16)

    def score(slot, q, c):
        part = slice(c * KC, (c + 1) * KC)
        s = lax.dot_general(kaug[part, :], q, (((1,), (1,)), ((), ())), preferred_element_type=F32)
        scores[slot, part, :] = s
        return jnp.max(s, axis=0, keepdims=True)

    def weigh(block, slot, top, c):
        part = slice(c * KC, (c + 1) * KC)
        e = jnp.exp2((scores[slot, part, :] - top) * LOG2E).astype(BF16)
        e_ref[block, part, :] = e
        return jnp.dot(vt[:, part], e, preferred_element_type=F32)

    def finish(block, total):
        inverse = 1.0 / total[HD : HD + 1, :]
        row = lax.broadcasted_iota(jnp.int32, total.shape, 0)
        total = jnp.where(row < HD, total, 1.0) * inverse
        ctx_ref[pl.ds(pl.multiple_of(block * QB, QB), QB), :] = total.T

    chunks = range(length // KC)
    q = query_block(0)
    top = None
    for c in chunks:
        high = score(0, q, c)
        top = high if top is None else jnp.maximum(top, high)

    def step(block, top):
        slot = block % 2
        q = query_block(block + 1)
        total, later = None, None
        for c in chunks:
            high = score(1 - slot, q, c)
            term = weigh(block, slot, top, c)
            total = term if total is None else total + term
            later = high if later is None else jnp.maximum(later, high)
        finish(block, total)
        return later

    top = lax.fori_loop(0, blocks - 1, step, top)
    total = None
    for c in chunks:
        term = weigh(blocks - 1, (blocks - 1) % 2, top, c)
        total = term if total is None else total + term
    finish(blocks - 1, total)


def convolve(valid, in_ref, ctx_ref, taps_ref, out_ref, sums_ref, gaug_ref, field, grad, hid, cot, bo):
    sources = in_ref.shape[0]
    rows = in_ref.shape[1] * 2 // 5
    first = rows * 3 // 2
    length = sources * rows
    half = length // 2
    mid = sources // 2
    step = 64
    steps = half // step
    lane = lane_ids((half, LANES))
    fc_low = in_ref[:mid, first:, :].reshape(half, LANES).astype(F32)
    fc_high = in_ref[mid:, first:, :].reshape(half, LANES).astype(F32)
    features = jnp.where(lane < HD, fc_low, swap_halves(fc_high))
    cot[...] = jnp.where(lane < HD, swap_halves(fc_low), fc_high)
    ctx = jnp.where(lane < HD, ctx_ref[:half, :], swap_halves(ctx_ref[half:, :]))
    hidden = features + ctx.astype(BF16).astype(F32)
    hid[...] = hidden
    position = lax.broadcasted_iota(jnp.int32, (half, LANES), 0) + jnp.where(lane < HD, 0, half)
    masked = jnp.where(position < valid, hidden, 0.0).astype(BF16).astype(F32)
    small = lane_ids((PAD, LANES))
    field[PAD : PAD + half, :] = masked
    field[:PAD, :] = jnp.where(small < HD, 0.0, swap_halves(masked[half - PAD :, :]))
    field[PAD + half :, :] = jnp.where(small < HD, swap_halves(masked[:PAD, :]), 0.0)
    sums_ref[...] = jnp.zeros_like(sums_ref)
    bias = taps_ref[TAPS : TAPS + 1, :]

    def forward_step(i, carry):
        base = pl.multiple_of(i * step, step)
        out = jnp.broadcast_to(bias, (step, LANES))
        for k in range(TAPS):
            out = out + taps_ref[k : k + 1, :] * field[pl.ds(base + (k + 1), step), :]
        gate = 1.0 / (1.0 + jnp.exp(-out))
        bo[pl.ds(base, step), :] = hid[pl.ds(base, step), :] + out * gate
        g = cot[pl.ds(base, step), :] * gate * (1.0 + out * (1.0 - gate))
        grad[pl.ds(base + PAD, step), :] = g.astype(BF16).astype(F32)
        for k in range(TAPS):
            term = g * field[pl.ds(base + (k + 1), step), :]
            part = slice(8 * k, 8 * k + 8)
            sums_ref[part, :] += jnp.sum(term.reshape(step // 8, 8, LANES), axis=0)
        part = slice(8 * TAPS, 8 * TAPS + 8)
        sums_ref[part, :] += jnp.sum(g.reshape(step // 8, 8, LANES), axis=0)
        return carry

    lax.fori_loop(0, steps, forward_step, 0)
    grad[:PAD, :] = jnp.where(small < HD, 0.0, swap_halves(grad[half : half + PAD, :]))
    grad[PAD + half :, :] = jnp.where(small < HD, swap_halves(grad[PAD : 2 * PAD, :]), 0.0)
    lane_step = lane_ids((step, LANES))
    rows_step = lax.broadcasted_iota(jnp.int32, (step, LANES), 0)
    place = rows_step + jnp.where(lane_step < HD, 0, half)
    per_step = step // rows

    def augmented(gf, context):
        inverse = context[:, HD : HD + 1]
        gn = (gf * (inverse * 0.125)).astype(BF16).astype(F32)
        delta = jnp.sum(jnp.where(lane_step < HD, gn * context, 0.0), axis=1, keepdims=True)
        upper = delta.astype(BF16).astype(F32)
        tail = jnp.where(lane_step == HD, -upper, jnp.where(lane_step == HD + 1, upper - delta, 0.0))
        return jnp.where(lane_step < HD, gn, tail).astype(BF16)

    def backward_step(i, carry):
        base = pl.multiple_of(i * step, step)
        out = None
        for k in range(TAPS):
            term = taps_ref[k : k + 1, :] * grad[pl.ds(base + (TAPS - k), step), :]
            out = term if out is None else out + term
        out = jnp.where(place + base < valid, out, 0.0)
        gf = (cot[pl.ds(base, step), :] + out).astype(BF16).astype(F32)
        swapped = swap_halves(gf)
        block = bo[pl.ds(base, step), :]
        low = jnp.where(lane_step < HD, block, swapped).astype(BF16)
        high = jnp.where(lane_step < HD, swap_halves(block), gf).astype(BF16)
        at = i * per_step
        out_ref[pl.ds(at, per_step), first:, :] = low.reshape(per_step, rows, LANES)
        out_ref[pl.ds(mid + at, per_step), first:, :] = high.reshape(per_step, rows, LANES)
        gaug_ref[pl.ds(base, step), :] = augmented(gf, ctx_ref[pl.ds(base, step), :])
        other = pl.multiple_of(base + half, step)
        gaug_ref[pl.ds(other, step), :] = augmented(swapped, ctx_ref[pl.ds(other, step), :])
        return carry

    lax.fori_loop(0, steps, backward_step, 0)


def attend_backward(in_ref, e_ref, gaug_ref, out_ref, vaug, kt, acc):
    sources = in_ref.shape[0]
    rows = in_ref.shape[1] * 2 // 5
    length = sources * rows
    per_block = QB // rows
    chunks = length // KC
    acc[...] = jnp.zeros_like(acc)

    def step(block, carry):
        q = in_ref[pl.ds(block * per_block, per_block), :rows, :].reshape(QB, LANES).astype(F32)
        g = gaug_ref[pl.ds(pl.multiple_of(block * QB, QB), QB), :]
        lane = lane_ids(q.shape)
        right = jnp.where(lane < HD, 0.0, swap_halves(q)).astype(BF16)
        left = jnp.where(lane < HD, g.astype(F32), 0.0).astype(BF16)

        def spread(c):
            return lax.dot_general(
                vaug[c * KC : (c + 1) * KC, :],
                g,
                (((1,), (1,)), ((), ())),
                preferred_element_type=F32,
            )

        total = None
        dp = spread(0)
        for c in range(chunks):
            part = slice(c * KC, (c + 1) * KC)
            e = e_ref[block, part, :]
            ds = (e.astype(F32) * dp).astype(BF16)
            if c + 1 < chunks:
                dp = spread(c + 1)
            acc[part, :] += jnp.dot(e, left, preferred_element_type=F32) + jnp.dot(
                ds, right, preferred_element_type=F32
            )
            term = jnp.dot(kt[:, part], ds, preferred_element_type=F32)
            total = term if total is None else total + term
        at = pl.ds(block * per_block, per_block)
        out_ref[at, :rows, :] = total.T.astype(BF16).reshape(per_block, rows, LANES)
        return carry

    lax.fori_loop(0, length // QB, step, 0)
    both = acc[...].reshape(sources, rows, LANES)
    lane = lane_ids(both.shape)
    gq = out_ref[:, :rows, :].astype(F32)
    out_ref[:, :rows, :] = jnp.where(lane < HD, gq, both).astype(BF16)
    half = rows // 2
    upper = swap_halves(both[:, half:, :].reshape(length // 2, LANES)).reshape(sources, half, LANES)
    gv = jnp.where(lane_ids(upper.shape) < HD, both[:, :half, :], upper) * 8.0
    out_ref[:, rows : rows * 3 // 2, :] = gv.astype(BF16)


def item_kernel(
    frames_ref,
    in_ref,
    taps_ref,
    out_ref,
    sums_ref,
    e_ref,
    scores,
    ctx_ref,
    acc,
    kaug,
    vaug,
    vt,
    kt,
    gaug_ref,
    field,
    grad,
    hid,
    cot,
    bo,
):
    valid = frames_ref[0]
    attend_forward(valid, in_ref, e_ref, ctx_ref, kaug, vaug, vt, kt, scores)
    convolve(valid, in_ref, ctx_ref, taps_ref, out_ref, sums_ref, gaug_ref, field, grad, hid, cot, bo)
    attend_backward(in_ref, e_ref, gaug_ref, out_ref, vaug, kt, acc)


def shape_of(*dims, dtype=BF16):
    return jax.ShapeDtypeStruct(dims, dtype)


def pack(*fields):
    rows, utts, width = fields[0].shape
    return pl.pallas_call(
        pack_kernel,
        out_shape=shape_of(utts * HEADS, rows * 5 // 2, LANES),
        in_specs=[pl.BlockSpec(memory_space=pltpu.HBM)] * 5,
        out_specs=VMEM,
        scratch_shapes=[pltpu.VMEM((rows, utts, width), BF16)] * 5 + [pltpu.SemaphoreType.DMA((5,))],
        compiler_params=params(60),
        name="pack",
    )(*fields)


def unpack(field, rows, utts):
    return pl.pallas_call(
        unpack_kernel,
        out_shape=[shape_of(rows, utts, HEADS * HD)] * 5,
        in_specs=[VMEM],
        out_specs=[VMEM] * 5,
        compiler_params=params(24),
        name="unpack",
    )(field)


def item_step(frames, field, taps):
    sources, tall, _ = field.shape
    length = sources * (tall * 2 // 5)
    half = length // 2
    wide = (length, LANES)
    return pl.pallas_call(
        item_kernel,
        out_shape=[
            shape_of(sources, tall, LANES),
            shape_of(8 * (TAPS + 1), LANES, dtype=F32),
        ],
        in_specs=[SMEM, VMEM, VMEM],
        out_specs=[VMEM] * 2,
        scratch_shapes=[
            pltpu.VMEM((length // QB, length, QB), BF16),
            pltpu.VMEM((2, length, QB), F32),
            pltpu.VMEM(wide, F32),
            pltpu.VMEM(wide, F32),
            pltpu.VMEM(wide, BF16),
            pltpu.VMEM(wide, BF16),
            pltpu.VMEM((LANES, length), BF16),
            pltpu.VMEM((LANES, length), BF16),
            pltpu.VMEM(wide, BF16),
            pltpu.VMEM((half + 2 * PAD, LANES), F32),
            pltpu.VMEM((half + 2 * PAD, LANES), F32),
            pltpu.VMEM((half, LANES), F32),
            pltpu.VMEM((half, LANES), F32),
            pltpu.VMEM((half, LANES), F32),
        ],
        compiler_params=params(48),
        name="item_step",
    )(frames, field, taps)


def exchange(field):
    return lax.all_to_all(field, "seq", split_axis=0, concat_axis=0, tiled=True)


def swap(field, axis, bit):
    count = lax.axis_size(axis)
    return lax.ppermute(field, axis, [(i, i ^ bit) for i in range(count)])


def joined(field, axis, bit):
    other = swap(field, axis, bit)
    upper = (lax.axis_index(axis) & bit) != 0
    first = jnp.where(upper, other, field)
    second = jnp.where(upper, field, other)
    return jnp.concatenate([first, second], axis=0)


def reduce_params(sums):
    part = jnp.sum(sums.reshape(TAPS + 1, 8, 2, HD), axis=(1, 2))
    for bit in (4, 8):
        part = part + swap(part, "dp", bit)
    part = part + swap(part, "dp", 1) + swap(part, "dp", 2) + swap(part, "dp", 3)
    other = swap(part, "seq", 8) + swap(part, "seq", 24)
    part = part + swap(part, "seq", 16)
    upper = (lax.axis_index("seq") & 8) != 0
    part = jnp.stack([jnp.where(upper, other, part), jnp.where(upper, part, other)])[None]
    for bit in (1, 2, 4):
        part = joined(part, "seq", bit)
    whole = part.transpose(2, 1, 0, 3).reshape(TAPS + 1, HEADS * HD)
    return whole[:TAPS], whole[TAPS]


def on_device(
    queries, key_vectors, value_vectors, features, cotangent, frames, conv_kernel, conv_bias
):
    rows, utts, _ = queries.shape
    item = lax.axis_index("seq")
    utt = item // HEADS
    head = item % HEADS
    valid = jnp.sum(jnp.where(jnp.arange(utts) == utt, frames, 0), keepdims=True)
    taps = jnp.concatenate([conv_kernel, conv_bias[None]], axis=0)
    taps = lax.dynamic_slice_in_dim(taps, head * HD, HD, axis=1)
    taps = jnp.concatenate([taps, taps], axis=1)

    field = exchange(pack(queries, key_vectors, value_vectors, features, cotangent))
    field, sums = item_step(valid, field, taps)
    field = exchange(field)
    grad_kernel, grad_bias = reduce_params(sums)
    grad_q, grad_k, grad_v, block_out, grad_features = unpack(field, rows, utts)
    return block_out, grad_features, grad_q, grad_k, grad_v, grad_kernel, grad_bias


def solution(mesh):
    field = P("seq", "dp", None)
    return jax.shard_map(
        on_device,
        mesh=mesh,
        in_specs=(field,) * 5 + (P("dp"), P(), P()),
        out_specs=(field,) * 5 + (P(), P()),
        check_vma=False,
    )
```

time: 270 us -> 234 us (0.87)
  starting transfers between devices: 92.5 us -> 78.6 us
  local copies, waits for them, and re-layouts: 13 us -> 1.67 us
  waiting for transfers between devices: 121 us -> 116 us
  Pallas kernels: 38.4 us -> 34.2 us
    all_to_all x4 -> x2, starting transfers between devices: 45.9 us -> 27.6 us  [exchange(): return lax.all_to_all(field, 'seq', split_axis=0, concat_axis=0, tiled=True)]
    unnamed x14 -> x6, local copies, waits for them, and re-layouts: 11.4 us -> 0.02 us
    ppermute x9 -> x11, starting transfers between devices: 46.6 us -> 50.9 us  [swap(): return lax.ppermute(field, axis, [(i, i ^ bit) for i in range(count)])]
    pallas_call x7 -> x3, Pallas kernels: 38.4 us -> 34.2 us  [the longest x1 24.6 us: item_step(): pl.pallas_call(item_kernel, out_shape=[shape_of(sources, tall, LANES), sh...]
    ppermute x9 -> x11, waiting for transfers between devices: 55.1 us -> 52.2 us  [swap(): return lax.ppermute(field, axis, [(i, i ^ bit) for i in range(count)])]
    all_to_all x4 -> x2, waiting for transfers between devices: 66.1 us -> 63.4 us  [exchange(): return lax.all_to_all(field, 'seq', split_axis=0, concat_axis=0, tiled=True)]
  transfers between devices with their start and end apart: 13 -> 13, of which waited for: 12 -> 8; matrix products, arithmetic and copies ran while one was open for 2% -> 1% of each run, Pallas kernels for 9% -> 0%
where the time goes in v2:
time: 234 us; the launch traced here: 232 us
  waiting for transfers between devices  116 us (50%)
  starting transfers between devices  78.6 us (34%)
  Pallas kernels  34.2 us (15%)
    all_to_all x2, waiting for transfers between devices, exchange(): return lax.all_to_all(field, 'seq', split_axis=0, concat_axis=0, tiled=True)  63.4 us
    ppermute x11, waiting for transfers between devices, swap(): return lax.ppermute(field, axis, [(i, i ^ bit) for i in range(count)])  52.2 us
    ppermute x11, starting transfers between devices, swap(): return lax.ppermute(field, axis, [(i, i ^ bit) for i in range(count)])  50.9 us
    all_to_all x2, starting transfers between devices, exchange(): return lax.all_to_all(field, 'seq', split_axis=0, concat_axis=0, tiled=True)  27.6 us
    pallas_call x1, Pallas kernels, item_step(): pl.pallas_call(item_kernel, out_shape=[shape_of(sources, tall, LANES), sh...  24.6 us
    pallas_call x1, Pallas kernels, pack(): pl.pallas_call(pack_kernel, out_shape=shape_of(utts * HEADS, rows * 5 //...  6.34 us
  transfers between devices with their start and end apart: 13, of which 8 were waited for; matrix products, arithmetic and copies ran while one was open for 1% of the time, Pallas kernels for 0%

profile of v2, /device:TPU:1, one launch (start us, length us, event | category | flops | bytes accessed | tf_op | source)
XLA Modules:
  0.0 232.4 jit_solution(7145824068573151825)
XLA Ops:
  0.6 6.3 %pack.1 = bf16[32,160,128]{2,1,0:T(8,128)(2,1)} custom-call(bf16[64,2,1024]{2,1,0:T(2,128)(2,1)} %q_hbm.1, bf16[64,2,1024]{2,1,0:T(2,128)(2,1)} %k_hbm.1, bf16[64,2,1024]{2,1,0:T(2,128)(2,1)} %v_hbm.1, bf16[64,2,1024]{2,1,0:T(2,128)(2,1)} %f_hbm.1, bf16[64,2,1024]{2,1,0:T(2,128)(2,1)} %c_hbm.1), custom_call_target="tpu_custom_call" | custom-call | tf_op jit(solution)/shard_map/pack/pallas_call | solution.py:333
  7.0 19.4 %all-to-all-start = ((bf16[32,160,128]{2,1,0:T(8,128)(2,1)}), bf16[32,160,128]{2,1,0:T(8,128)(2,1)S(1)}, u32[]{:S(2)}, u32[]{:S(2)}) async-start(bf16[32,160,128]{2,1,0:T(8,128)(2,1)} %pack.1), calls=%async_computation | async-start | bytes 2621440 | tf_op jit(solution)/shard_map/all_to_all | solution.py:390
  26.4 0.6 fusion.1
  27.1 0.1 pad_maximum_fusion.3.taps_ref
  27.2 63.4 %all-to-all-done.in_ref = bf16[32,160,128]{2,1,0:T(8,128)(2,1)S(1)} async-done(((bf16[32,160,128]{2,1,0:T(8,128)(2,1)}), bf16[32,160,128]{2,1,0:T(8,128)(2,1)S(1)}, u32[]{:S(2)}, u32[]{:S(2)}) %all-to-all-start) | async-done | bytes 1310752 | tf_op jit(solution)/shard_map/all_to_all | solution.py:390
  90.6 24.6 %item_step.1 = (bf16[32,160,128]{2,1,0:T(8,128)(2,1)}, f32[256,128]{1,0:T(8,128)S(1)}) custom-call(s32[1]{0:T(128)} %bitcast.frames_ref, bf16[32,160,128]{2,1,0:T(8,128)(2,1)S(1)} %all-to-all-done.in_ref, f32[32,128]{1,0:T(8,128)S(1)} %pad_maximum_fusion.3.taps_ref), custom_call_target="tpu_custom_call" | custom-call | tf_op jit(solution)/shard_map/item_step/pallas_call | solution.py:360
  115.2 8.3 %all-to-all-start.1 = ((bf16[32,160,128]{2,1,0:T(8,128)(2,1)}), bf16[32,160,128]{2,1,0:T(8,128)(2,1)S(1)}, u32[]{:S(2)}, u32[]{:S(2)}) async-start(bf16[32,160,128]{2,1,0:T(8,128)(2,1)} %get-tuple-element.14), calls=%async_computation.1 | async-start | bytes 2621440 | tf_op jit(solution)/shard_map/all_to_all | solution.py:390
  123.5 0.2 reshape.21
  123.7 0.1 reduce_sum.19
  123.8 3.2 %collective-permute-start = (f32[32,64]{1,0:T(8,128)S(1)}, f32[32,64]{1,0:T(8,128)S(1)}, u32[]{:S(2)}, u32[]{:S(2)}) collective-permute-start(f32[32,64]{1,0:T(8,128)S(1)} %reduce_sum.19), channel_id=1, source_target_pairs={{0,4},{1,5},{2,6},{3,7},{4,0},{5,1},{6,2},{7,3},{8,12},{9,13},{10,... | collective-permute-start | bytes 24584 | tf_op jit(solution)/shard_map/ppermute | solution.py:395
  127.1 1.6 collective-permute-done
  128.6 4.8 %collective-permute-start.1 = (f32[32,64]{1,0:T(8,128)S(1)}, f32[32,64]{1,0:T(8,128)S(1)}, u32[]{:S(2)}, u32[]{:S(2)}) collective-permute-start(f32[32,64]{1,0:T(8,128)S(1)} %add.31), channel_id=1, source_target_pairs={{0,8},{1,9},{2,10},{3,11},{4,12},{5,13},{6,14},{7,15},{8,0},{9,1},... | collective-permute-start | bytes 24584 | tf_op jit(solution)/shard_map/ppermute | solution.py:395
  133.4 1.4 collective-permute-done.1
  134.9 2.2 collective-permute-start.2
  137.1 2.6 %collective-permute-start.3 = (f32[32,64]{1,0:T(8,128)S(1)}, f32[32,64]{1,0:T(8,128)S(1)}, u32[]{:S(2)}, u32[]{:S(2)}) collective-permute-start(f32[32,64]{1,0:T(8,128)S(1)} %add.32), channel_id=1, source_target_pairs={{0,2},{1,3},{2,0},{3,1},{4,6},{5,7},{6,4},{7,5},{8,10},{9,11},{10,... | collective-permute-start | bytes 24584 | tf_op jit(solution)/shard_map/ppermute | solution.py:395
  139.7 4.4 %collective-permute-start.4 = (f32[32,64]{1,0:T(8,128)S(1)}, f32[32,64]{1,0:T(8,128)S(1)}, u32[]{:S(2)}, u32[]{:S(2)}) collective-permute-start(f32[32,64]{1,0:T(8,128)S(1)} %add.32), channel_id=1, source_target_pairs={{0,3},{1,2},{2,1},{3,0},{4,7},{5,6},{6,5},{7,4},{8,11},{9,10},{10,... | collective-permute-start | bytes 24584 | tf_op jit(solution)/shard_map/ppermute | solution.py:395
  144.2 32.4 %collective-permute-done.2 = f32[32,64]{1,0:T(8,128)S(1)} collective-permute-done((f32[32,64]{1,0:T(8,128)S(1)}, f32[32,64]{1,0:T(8,128)S(1)}, u32[]{:S(2)}, u32[]{:S(2)}) %collective-permute-start.2) | collective-permute-done | bytes 8224 | tf_op jit(solution)/shard_map/ppermute | solution.py:395
  176.6 7.7 %collective-permute-start.5 = (f32[32,64]{1,0:T(8,128)S(1)}, f32[32,64]{1,0:T(8,128)S(1)}, u32[]{:S(2)}, u32[]{:S(2)}) collective-permute-start(f32[32,64]{1,0:T(8,128)S(1)} %add_add_fusion), channel_id=1, source_target_pairs={{0,128},{16,144},{32,160},{48,176},{64,192},{80,208},{96,224},{112... | collective-permute-start | bytes 24584 | tf_op jit(solution)/shard_map/ppermute | solution.py:395
  184.3 12.1 %collective-permute-start.6 = (f32[32,64]{1,0:T(8,128)S(1)}, f32[32,64]{1,0:T(8,128)S(1)}, u32[]{:S(2)}, u32[]{:S(2)}) collective-permute-start(f32[32,64]{1,0:T(8,128)S(1)} %add_add_fusion), channel_id=1, source_target_pairs={{0,384},{16,400},{32,416},{48,432},{64,448},{80,464},{96,480},{112... | collective-permute-start | bytes 24584 | tf_op jit(solution)/shard_map/ppermute | solution.py:395
  196.5 1.9 collective-permute-start.7
  198.4 11.3 %collective-permute-done.7 = f32[32,64]{1,0:T(8,128)S(1)} collective-permute-done((f32[32,64]{1,0:T(8,128)S(1)}, f32[32,64]{1,0:T(8,128)S(1)}, u32[]{:S(2)}, u32[]{:S(2)}) %collective-permute-start.7) | collective-permute-done | bytes 8224 | tf_op jit(solution)/shard_map/ppermute | solution.py:395
  209.8 4.3 %collective-permute-start.8 = (f32[1,2,32,64]{3,0,1,2:T(1,128)S(1)}, f32[1,2,32,64]{3,0,1,2:T(1,128)S(1)}, u32[]{:S(2)}, u32[]{:S(2)}) collective-permute-start(f32[1,2,32,64]{3,0,1,2:T(1,128)S(1)} %bitcast.13), channel_id=1, source_target_pairs={{0,16},{16,0},{32,48},{48,32},{64,80},{80,64},{96,112},{112,96},{1... | collective-permute-start | bytes 49160 | tf_op jit(solution)/shard_map/ppermute | solution.py:395
  214.1 0.8 collective-permute-done.8
  215.1 3.0 %collective-permute-start.9 = (f32[2,2,32,64]{3,0,1,2:T(2,128)S(1)}, f32[2,2,32,64]{3,0,1,2:T(2,128)S(1)}, u32[]{:S(2)}, u32[]{:S(2)}) collective-permute-start(f32[2,2,32,64]{3,0,1,2:T(2,128)S(1)} %pad_maximum_fusion.1), channel_id=1, source_target_pairs={{0,32},{16,48},{32,0},{48,16},{64,96},{80,112},{96,64},{112,80},{1... | collective-permute-start | bytes 98312 | tf_op jit(solution)/shard_map/ppermute | solution.py:395
  218.1 2.0 collective-permute-done.9
  220.1 0.1 broadcast_select_fusion.3
  220.3 4.6 %collective-permute-start.10 = (f32[4,2,32,64]{3,0,1,2:T(4,128)S(1)}, f32[4,2,32,64]{3,0,1,2:T(4,128)S(1)}, u32[]{:S(2)}, u32[]{:S(2)}) collective-permute-start(f32[4,2,32,64]{3,0,1,2:T(4,128)S(1)} %pad_maximum_fusion), channel_id=1, source_target_pairs={{0,64},{16,80},{32,96},{48,112},{64,0},{80,16},{96,32},{112,48},{1... | collective-permute-start | bytes 196616 | tf_op jit(solution)/shard_map/ppermute | solution.py:395
  224.9 2.7 %collective-permute-done.10 = f32[4,2,32,64]{3,0,1,2:T(4,128)S(1)} collective-permute-done((f32[4,2,32,64]{3,0,1,2:T(4,128)S(1)}, f32[4,2,32,64]{3,0,1,2:T(4,128)S(1)}, u32[]{:S(2)}, u32[]{:S(2)}) %collective-permute-start.10) | collective-permute-done | bytes 65568 | tf_op jit(solution)/shard_map/ppermute | solution.py:395
  227.5 0.1 broadcast_select_fusion.5
  227.7 0.8 slice.11
  228.5 0.7 squeeze.3
  229.2 3.2 %unpack.1 = (bf16[64,2,1024]{2,1,0:T(2,128)(2,1)}, bf16[64,2,1024]{2,1,0:T(2,128)(2,1)}, bf16[64,2,1024]{2,1,0:T(2,128)(2,1)}, bf16[64,2,1024]{2,1,0:T(2,128)(2,1)}, bf16[64,2,1024]{2,1,0:T(2,128)(2,1)}) custom-call(bf16[32,160,128]{2,1,0:T(8,128)(2,1)S(1)} %all-to-all-done.1.in_ref), custom_call_target="tpu_custom_call" | custom-call | tf_op jit(solution)/shard_map/unpack/pallas_call | solution.py:345
  (23 shorter events, 0.5 us)
Async XLA Ops:
  7.0 19.4 %copy-start.2 = (s32[2]{0:T(128)S(1)}, s32[2]{0:T(128)}, u32[]{:S(2)}) copy-start(s32[2]{0:T(128)} %param.13) | copy-start | bytes 28
  7.0 20.1 %copy-start = (f32[31,1024]{1,0:T(8,128)S(1)}, f32[31,1024]{1,0:T(8,128)}, u32[]{:S(2)}) copy-start(f32[31,1024]{1,0:T(8,128)} %param.14) | copy-start | bytes 380932
  7.0 20.1 %copy-start.1 = (f32[1024]{0:T(1024)S(1)}, f32[1024]{0:T(1024)}, u32[]{:S(2)}) copy-start(f32[1024]{0:T(1024)} %param.15) | copy-start | bytes 12292
  7.0 83.6 %all-to-all-start = ((bf16[32,160,128]{2,1,0:T(8,128)(2,1)}), bf16[32,160,128]{2,1,0:T(8,128)(2,1)S(1)}, u32[]{:S(2)}, u32[]{:S(2)}) async-start(bf16[32,160,128]{2,1,0:T(8,128)(2,1)} %pack.1), calls=%async_computation | async-start | bytes 2621440 | tf_op jit(solution)/shard_map/all_to_all | solution.py:390
  115.2 114.0 %all-to-all-start.1 = ((bf16[32,160,128]{2,1,0:T(8,128)(2,1)}), bf16[32,160,128]{2,1,0:T(8,128)(2,1)S(1)}, u32[]{:S(2)}, u32[]{:S(2)}) async-start(bf16[32,160,128]{2,1,0:T(8,128)(2,1)} %get-tuple-element.14), calls=%async_computation.1 | async-start | bytes 2621440 | tf_op jit(solution)/shard_map/all_to_all | solution.py:390
  123.8 4.8 %collective-permute-start = (f32[32,64]{1,0:T(8,128)S(1)}, f32[32,64]{1,0:T(8,128)S(1)}, u32[]{:S(2)}, u32[]{:S(2)}) collective-permute-start(f32[32,64]{1,0:T(8,128)S(1)} %reduce_sum.19), channel_id=1, source_target_pairs={{0,4},{1,5},{2,6},{3,7},{4,0},{5,1},{6,2},{7,3},{8,12},{9,13},{10,... | collective-permute-start | bytes 24584 | tf_op jit(solution)/shard_map/ppermute | solution.py:395
  128.6 6.3 %collective-permute-start.1 = (f32[32,64]{1,0:T(8,128)S(1)}, f32[32,64]{1,0:T(8,128)S(1)}, u32[]{:S(2)}, u32[]{:S(2)}) collective-permute-start(f32[32,64]{1,0:T(8,128)S(1)} %add.31), channel_id=1, source_target_pairs={{0,8},{1,9},{2,10},{3,11},{4,12},{5,13},{6,14},{7,15},{8,0},{9,1},... | collective-permute-start | bytes 24584 | tf_op jit(solution)/shard_map/ppermute | solution.py:395
  134.9 41.7 %collective-permute-start.2 = (f32[32,64]{1,0:T(8,128)S(1)}, f32[32,64]{1,0:T(8,128)S(1)}, u32[]{:S(2)}, u32[]{:S(2)}) collective-permute-start(f32[32,64]{1,0:T(8,128)S(1)} %add.32), channel_id=1, source_target_pairs={{0,1},{1,0},{2,3},{3,2},{4,5},{5,4},{6,7},{7,6},{8,9},{9,8},{10,11... | collective-permute-start | bytes 24584 | tf_op jit(solution)/shard_map/ppermute | solution.py:395
  137.1 39.5 %collective-permute-start.3 = (f32[32,64]{1,0:T(8,128)S(1)}, f32[32,64]{1,0:T(8,128)S(1)}, u32[]{:S(2)}, u32[]{:S(2)}) collective-permute-start(f32[32,64]{1,0:T(8,128)S(1)} %add.32), channel_id=1, source_target_pairs={{0,2},{1,3},{2,0},{3,1},{4,6},{5,7},{6,4},{7,5},{8,10},{9,11},{10,... | collective-permute-start | bytes 24584 | tf_op jit(solution)/shard_map/ppermute | solution.py:395
  139.7 36.9 %collective-permute-start.4 = (f32[32,64]{1,0:T(8,128)S(1)}, f32[32,64]{1,0:T(8,128)S(1)}, u32[]{:S(2)}, u32[]{:S(2)}) collective-permute-start(f32[32,64]{1,0:T(8,128)S(1)} %add.32), channel_id=1, source_target_pairs={{0,3},{1,2},{2,1},{3,0},{4,7},{5,6},{6,5},{7,4},{8,11},{9,10},{10,... | collective-permute-start | bytes 24584 | tf_op jit(solution)/shard_map/ppermute | solution.py:395
  176.6 21.8 %collective-permute-start.5 = (f32[32,64]{1,0:T(8,128)S(1)}, f32[32,64]{1,0:T(8,128)S(1)}, u32[]{:S(2)}, u32[]{:S(2)}) collective-permute-start(f32[32,64]{1,0:T(8,128)S(1)} %add_add_fusion), channel_id=1, source_target_pairs={{0,128},{16,144},{32,160},{48,176},{64,192},{80,208},{96,224},{112... | collective-permute-start | bytes 24584 | tf_op jit(solution)/shard_map/ppermute | solution.py:395
  184.3 14.1 %collective-permute-start.6 = (f32[32,64]{1,0:T(8,128)S(1)}, f32[32,64]{1,0:T(8,128)S(1)}, u32[]{:S(2)}, u32[]{:S(2)}) collective-permute-start(f32[32,64]{1,0:T(8,128)S(1)} %add_add_fusion), channel_id=1, source_target_pairs={{0,384},{16,400},{32,416},{48,432},{64,448},{80,464},{96,480},{112... | collective-permute-start | bytes 24584 | tf_op jit(solution)/shard_map/ppermute | solution.py:395
  196.5 13.3 %collective-permute-start.7 = (f32[32,64]{1,0:T(8,128)S(1)}, f32[32,64]{1,0:T(8,128)S(1)}, u32[]{:S(2)}, u32[]{:S(2)}) collective-permute-start(f32[32,64]{1,0:T(8,128)S(1)} %add_add_fusion), channel_id=1, source_target_pairs={{0,256},{16,272},{32,288},{48,304},{64,320},{80,336},{96,352},{112... | collective-permute-start | bytes 24584 | tf_op jit(solution)/shard_map/ppermute | solution.py:395
  209.8 5.2 %collective-permute-start.8 = (f32[1,2,32,64]{3,0,1,2:T(1,128)S(1)}, f32[1,2,32,64]{3,0,1,2:T(1,128)S(1)}, u32[]{:S(2)}, u32[]{:S(2)}) collective-permute-start(f32[1,2,32,64]{3,0,1,2:T(1,128)S(1)} %bitcast.13), channel_id=1, source_target_pairs={{0,16},{16,0},{32,48},{48,32},{64,80},{80,64},{96,112},{112,96},{1... | collective-permute-start | bytes 49160 | tf_op jit(solution)/shard_map/ppermute | solution.py:395
  215.1 5.0 %collective-permute-start.9 = (f32[2,2,32,64]{3,0,1,2:T(2,128)S(1)}, f32[2,2,32,64]{3,0,1,2:T(2,128)S(1)}, u32[]{:S(2)}, u32[]{:S(2)}) collective-permute-start(f32[2,2,32,64]{3,0,1,2:T(2,128)S(1)} %pad_maximum_fusion.1), channel_id=1, source_target_pairs={{0,32},{16,48},{32,0},{48,16},{64,96},{80,112},{96,64},{112,80},{1... | collective-permute-start | bytes 98312 | tf_op jit(solution)/shard_map/ppermute | solution.py:395
  220.3 7.2 %collective-permute-start.10 = (f32[4,2,32,64]{3,0,1,2:T(4,128)S(1)}, f32[4,2,32,64]{3,0,1,2:T(4,128)S(1)}, u32[]{:S(2)}, u32[]{:S(2)}) collective-permute-start(f32[4,2,32,64]{3,0,1,2:T(4,128)S(1)} %pad_maximum_fusion), channel_id=1, source_target_pairs={{0,64},{16,80},{32,96},{48,112},{64,0},{80,16},{96,32},{112,48},{1... | collective-permute-start | bytes 196616 | tf_op jit(solution)/shard_map/ppermute | solution.py:395

commit v3 on v2

--- a/solution.py
+++ b/solution.py
@@ -164,7 +164,9 @@
     finish(blocks - 1, total)
 
 
-def convolve(valid, in_ref, ctx_ref, taps_ref, out_ref, sums_ref, gaug_ref, field, grad, hid, cot, bo):
+def convolve(
+    valid, in_ref, ctx_ref, taps_ref, out_ref, part_ref, gaug_ref, field, grad, hid, cot, bo, sums_ref
+):
     sources = in_ref.shape[0]
     rows = in_ref.shape[1] * 2 // 5
     first = rows * 3 // 2
@@ -208,6 +210,11 @@
         return carry
 
     lax.fori_loop(0, steps, forward_step, 0)
+    folded = jnp.sum(sums_ref[...].reshape(TAPS + 1, 8, LANES), axis=1)
+    folded = folded + swap_halves(folded)
+    taps_half = (TAPS + 1) // 2
+    part_lane = lane_ids((taps_half, LANES))
+    part_ref[...] = jnp.where(part_lane < HD, folded[:taps_half], folded[taps_half:])
     grad[:PAD, :] = jnp.where(small < HD, 0.0, swap_halves(grad[half : half + PAD, :]))
     grad[PAD + half :, :] = jnp.where(small < HD, swap_halves(grad[PAD : 2 * PAD, :]), 0.0)
     lane_step = lane_ids((step, LANES))
@@ -236,8 +243,8 @@
         low = jnp.where(lane_step < HD, block, swapped).astype(BF16)
         high = jnp.where(lane_step < HD, swap_halves(block), gf).astype(BF16)
         at = i * per_step
-        out_ref[pl.ds(at, per_step), first:, :] = low.reshape(per_step, rows, LANES)
-        out_ref[pl.ds(mid + at, per_step), first:, :] = high.reshape(per_step, rows, LANES)
+        out_ref[pl.ds(at, per_step), :, :] = low.reshape(per_step, rows, LANES)
+        out_ref[pl.ds(mid + at, per_step), :, :] = high.reshape(per_step, rows, LANES)
         gaug_ref[pl.ds(base, step), :] = augmented(gf, ctx_ref[pl.ds(base, step), :])
         other = pl.multiple_of(base + half, step)
         gaug_ref[pl.ds(other, step), :] = augmented(swapped, ctx_ref[pl.ds(other, step), :])
@@ -246,13 +253,14 @@
     lax.fori_loop(0, steps, backward_step, 0)
 
 
-def attend_backward(in_ref, e_ref, gaug_ref, out_ref, vaug, kt, acc):
+def backward_kernel(in_ref, e_ref, gaug_ref, vaug, kt, bogf_ref, out_ref, acc):
     sources = in_ref.shape[0]
     rows = in_ref.shape[1] * 2 // 5
     length = sources * rows
     per_block = QB // rows
     chunks = length // KC
     acc[...] = jnp.zeros_like(acc)
+    out_ref[:, rows * 3 // 2 :, :] = bogf_ref[...]
 
     def step(block, carry):
         q = in_ref[pl.ds(block * per_block, per_block), :rows, :].reshape(QB, LANES).astype(F32)
@@ -297,31 +305,45 @@
     out_ref[:, rows : rows * 3 // 2, :] = gv.astype(BF16)
 
 
-def item_kernel(
+def forward_kernel(
     frames_ref,
     in_ref,
     taps_ref,
-    out_ref,
-    sums_ref,
     e_ref,
+    gaug_ref,
+    vaug,
+    kt,
+    bogf_ref,
+    part_ref,
     scores,
     ctx_ref,
-    acc,
     kaug,
-    vaug,
     vt,
-    kt,
-    gaug_ref,
     field,
     grad,
     hid,
     cot,
     bo,
+    sums_ref,
 ):
     valid = frames_ref[0]
     attend_forward(valid, in_ref, e_ref, ctx_ref, kaug, vaug, vt, kt, scores)
-    convolve(valid, in_ref, ctx_ref, taps_ref, out_ref, sums_ref, gaug_ref, field, grad, hid, cot, bo)
-    attend_backward(in_ref, e_ref, gaug_ref, out_ref, vaug, kt, acc)
+    convolve(
+        valid, in_ref, ctx_ref, taps_ref, bogf_ref, part_ref, gaug_ref, field, grad, hid, cot, bo, sums_ref
+    )
+
+
+def params_kernel(in_ref, taps_ref, bias_ref):
+    half = in_ref.shape[1]
+    for h in range(0, HEADS, 2):
+        part = slice(h * HD, (h + 2) * HD)
+        a = in_ref[h]
+        b = in_ref[h + 1]
+        low = lane_pair(a[:, :HD], b[:, :HD])
+        high = lane_pair(a[:, HD:], b[:, HD:])
+        taps_ref[:half, part] = low
+        taps_ref[half:, part] = high[: TAPS - half]
+        bias_ref[:, part] = high[TAPS - half :]
 
 
 def shape_of(*dims, dtype=BF16):
@@ -352,38 +374,71 @@
     )(field)
 
 
-def item_step(frames, field, taps):
+def forward(frames, field, taps):
     sources, tall, _ = field.shape
-    length = sources * (tall * 2 // 5)
+    rows = tall * 2 // 5
+    length = sources * rows
     half = length // 2
     wide = (length, LANES)
     return pl.pallas_call(
-        item_kernel,
+        forward_kernel,
         out_shape=[
-            shape_of(sources, tall, LANES),
-            shape_of(8 * (TAPS + 1), LANES, dtype=F32),
+            shape_of(length // QB, length, QB),
+            shape_of(*wide),
+            shape_of(*wide),
+            shape_of(LANES, length),
+            shape_of(sources, rows, LANES),
+            shape_of((TAPS + 1) // 2, LANES, dtype=F32),
         ],
         in_specs=[SMEM, VMEM, VMEM],
-        out_specs=[VMEM] * 2,
+        out_specs=[VMEM] * 6,
         scratch_shapes=[
-            pltpu.VMEM((length // QB, length, QB), BF16),
             pltpu.VMEM((2, length, QB), F32),
             pltpu.VMEM(wide, F32),
-            pltpu.VMEM(wide, F32),
-            pltpu.VMEM(wide, BF16),
             pltpu.VMEM(wide, BF16),
             pltpu.VMEM((LANES, length), BF16),
-            pltpu.VMEM((LANES, length), BF16),
-            pltpu.VMEM(wide, BF16),
             pltpu.VMEM((half + 2 * PAD, LANES), F32),
             pltpu.VMEM((half + 2 * PAD, LANES), F32),
             pltpu.VMEM((half, LANES), F32),
             pltpu.VMEM((half, LANES), F32),
             pltpu.VMEM((half, LANES), F32),
+            pltpu.VMEM((8 * (TAPS + 1), LANES), F32),
         ],
-        compiler_params=params(48),
-        name="item_step",
+        compiler_params=params(36),
+        cost_estimate=pl.CostEstimate(
+            flops=8_000_000_000, bytes_accessed=20_000_000, transcendentals=4_000_000
+        ),
+        name="forward",
     )(frames, field, taps)
+
+
+def backward(field, e, gaug, vaug, kt, bogf):
+    length = e.shape[1]
+    return pl.pallas_call(
+        backward_kernel,
+        out_shape=shape_of(*field.shape),
+        in_specs=[VMEM] * 6,
+        out_specs=VMEM,
+        scratch_shapes=[pltpu.VMEM((length, LANES), F32)],
+        compiler_params=params(36),
+        cost_estimate=pl.CostEstimate(
+            flops=9_000_000_000, bytes_accessed=20_000_000, transcendentals=0
+        ),
+        name="backward",
+    )(field, e, gaug, vaug, kt, bogf)
+
+
+def unpack_params(parts):
+    width = HEADS * HD
+    taps, bias = pl.pallas_call(
+        params_kernel,
+        out_shape=[shape_of(TAPS, width, dtype=F32), shape_of(1, width, dtype=F32)],
+        in_specs=[VMEM],
+        out_specs=[VMEM] * 2,
+        compiler_params=params(8),
+        name="unpack_params",
+    )(parts)
+    return taps, bias.reshape(width)
 
 
 def exchange(field):
@@ -403,19 +458,22 @@
     return jnp.concatenate([first, second], axis=0)
 
 
-def reduce_params(sums):
-    part = jnp.sum(sums.reshape(TAPS + 1, 8, 2, HD), axis=(1, 2))
+def over_utterances(part):
+    other = swap(part, "seq", 8) + swap(part, "seq", 24)
+    part = part + swap(part, "seq", 16)
+    upper = (lax.axis_index("seq") & 8) != 0
+    return jnp.concatenate([jnp.where(upper, other, part), jnp.where(upper, part, other)], axis=0)
+
+
+def over_devices(part):
     for bit in (4, 8):
         part = part + swap(part, "dp", bit)
     part = part + swap(part, "dp", 1) + swap(part, "dp", 2) + swap(part, "dp", 3)
-    other = swap(part, "seq", 8) + swap(part, "seq", 24)
-    part = part + swap(part, "seq", 16)
-    upper = (lax.axis_index("seq") & 8) != 0
-    part = jnp.stack([jnp.where(upper, other, part), jnp.where(upper, part, other)])[None]
     for bit in (1, 2, 4):
         part = joined(part, "seq", bit)
-    whole = part.transpose(2, 1, 0, 3).reshape(TAPS + 1, HEADS * HD)
-    return whole[:TAPS], whole[TAPS]
+    half = (TAPS + 1) // 2
+    part = part.reshape(HEADS // 2, 2, half, LANES).swapaxes(0, 1)
+    return unpack_params(part.reshape(HEADS, half, LANES))
 
 
 def on_device(
@@ -431,9 +489,12 @@
     taps = jnp.concatenate([taps, taps], axis=1)
 
     field = exchange(pack(queries, key_vectors, value_vectors, features, cotangent))
-    field, sums = item_step(valid, field, taps)
+    *state, bogf, part = forward(valid, field, taps)
+    part = over_utterances(part)
+    field = backward(field, *state, bogf)
+    field, part = lax.optimization_barrier((field, part))
     field = exchange(field)
-    grad_kernel, grad_bias = reduce_params(sums)
+    grad_kernel, grad_bias = over_devices(part)
     grad_q, grad_k, grad_v, block_out, grad_features = unpack(field, rows, utts)
     return block_out, grad_features, grad_q, grad_k, grad_v, grad_kernel, grad_bias
 

time: 234 us -> 217 us (0.927)
  waiting for transfers between devices: 116 us -> 104 us
  starting transfers between devices: 78.6 us -> 73.8 us
    ppermute x11, waiting for transfers between devices: 52.2 us -> 40.2 us  [swap(): return lax.ppermute(field, axis, [(i, i ^ bit) for i in range(count)])]
    ppermute x11, starting transfers between devices: 50.9 us -> 45.3 us  [swap(): return lax.ppermute(field, axis, [(i, i ^ bit) for i in range(count)])]
    pallas_call x1 -> x3, Pallas kernels: 24.6 us -> 25.7 us  [the longest x1 15.2 us: forward(): pl.pallas_call(forward_kernel, out_shape=[shape_of(length // QB, length,...]
  transfers between devices with their start and end apart: 13 -> 13, of which waited for: 8 -> 9; matrix products, arithmetic and copies ran while one was open for 1% -> 0% of each run, Pallas kernels for 0% -> 5%
where the time goes in v3:
time: 217 us; the launch traced here: 214 us
  waiting for transfers between devices  104 us (48%)
  starting transfers between devices  73.8 us (34%)
  Pallas kernels  35.2 us (16%)
    all_to_all x2, waiting for transfers between devices, exchange(): return lax.all_to_all(field, 'seq', split_axis=0, concat_axis=0, tiled=True)  63.4 us
    ppermute x11, starting transfers between devices, swap(): return lax.ppermute(field, axis, [(i, i ^ bit) for i in range(count)])  45.3 us
    ppermute x11, waiting for transfers between devices, swap(): return lax.ppermute(field, axis, [(i, i ^ bit) for i in range(count)])  40.2 us
    all_to_all x2, starting transfers between devices, exchange(): return lax.all_to_all(field, 'seq', split_axis=0, concat_axis=0, tiled=True)  28.5 us
    pallas_call x1, Pallas kernels, forward(): pl.pallas_call(forward_kernel, out_shape=[shape_of(length // QB, length,...  15.2 us
    pallas_call x1, Pallas kernels, backward(): pl.pallas_call(backward_kernel, out_shape=shape_of(*field.shape), in_spec...  9.75 us
    pallas_call x1, Pallas kernels, pack(): pl.pallas_call(pack_kernel, out_shape=shape_of(utts * HEADS, rows * 5 //...  6.32 us
  transfers between devices with their start and end apart: 13, of which 9 were waited for; matrix products, arithmetic and copies ran while one was open for 0% of the time, Pallas kernels for 5%

profile of v3, /device:TPU:1, one launch (start us, length us, event | category | flops | bytes accessed | tf_op | source)
XLA Modules:
  0.0 214.4 jit_solution(14088236889770770109)
XLA Ops:
  0.6 6.3 %pack.1 = bf16[32,160,128]{2,1,0:T(8,128)(2,1)} custom-call(bf16[64,2,1024]{2,1,0:T(2,128)(2,1)} %q_hbm.1, bf16[64,2,1024]{2,1,0:T(2,128)(2,1)} %k_hbm.1, bf16[64,2,1024]{2,1,0:T(2,128)(2,1)} %v_hbm.1, bf16[64,2,1024]{2,1,0:T(2,128)(2,1)} %f_hbm.1, bf16[64,2,1024]{2,1,0:T(2,128)(2,1)} %c_hbm.1), custom_call_target="tpu_custom_call" | custom-call | tf_op jit(solution)/shard_map/pack/pallas_call | solution.py:355
  7.0 0.0 copy-start.2
  7.0 0.0 copy-start.1
  7.0 19.4 %all-to-all-start = ((bf16[32,160,128]{2,1,0:T(8,128)(2,1)}), bf16[32,160,128]{2,1,0:T(8,128)(2,1)S(1)}, u32[]{:S(2)}, u32[]{:S(2)}) async-start(bf16[32,160,128]{2,1,0:T(8,128)(2,1)} %pack.1), calls=%async_computation | async-start | bytes 2621440 | tf_op jit(solution)/shard_map/all_to_all | solution.py:445
  26.4 0.6 fusion.1
  27.0 0.1 fusion
  27.1 0.1 pad_maximum_fusion.3.taps_ref
  27.2 63.4 %all-to-all-done.in_ref = bf16[32,160,128]{2,1,0:T(8,128)(2,1)S(1)} async-done(((bf16[32,160,128]{2,1,0:T(8,128)(2,1)}), bf16[32,160,128]{2,1,0:T(8,128)(2,1)S(1)}, u32[]{:S(2)}, u32[]{:S(2)}) %all-to-all-start) | async-done | bytes 1310752 | tf_op jit(solution)/shard_map/all_to_all | solution.py:445
  90.6 15.2 %forward.1 = (bf16[2,2048,1024]{2,1,0:T(8,128)(2,1)S(1)}, bf16[2048,128]{1,0:T(8,128)(2,1)S(1)}, bf16[2048,128]{1,0:T(8,128)(2,1)S(1)}, bf16[128,2048]{1,0:T(8,1...) custom-call(s32[1]{0:T(128)} %bitcast.frames_ref, bf16[32,160,128]{2,1,0:T(8,128)(2,1)S(1)} %all-to-all-done.in_ref, ...), custom_call_target="tpu_custom_call" | custom-call | flops 8000000000 | bytes 20000000 | tf_op jit(solution)/shard_map/forward/pallas_call | solution.py:383
  105.8 7.1 %collective-permute-start.2 = (f32[16,128]{1,0:T(8,128)S(1)}, f32[16,128]{1,0:T(8,128)S(1)}, u32[]{:S(2)}, u32[]{:S(2)}) collective-permute-start(f32[16,128]{1,0:T(8,128)S(1)} %get-tuple-element.27), channel_id=1, source_target_pairs={{0,256},{16,272},{32,288},{48,304},{64,320},{80,336},{96,352},{112... | collective-permute-start | bytes 24584 | tf_op jit(solution)/shard_map/ppermute | solution.py:450
  112.9 2.1 collective-permute-start
  115.0 7.2 %collective-permute-start.1 = (f32[16,128]{1,0:T(8,128)S(1)}, f32[16,128]{1,0:T(8,128)S(1)}, u32[]{:S(2)}, u32[]{:S(2)}) collective-permute-start(f32[16,128]{1,0:T(8,128)S(1)} %get-tuple-element.27), channel_id=1, source_target_pairs={{0,384},{16,400},{32,416},{48,432},{64,448},{80,464},{96,480},{112... | collective-permute-start | bytes 24584 | tf_op jit(solution)/shard_map/ppermute | solution.py:450
  122.2 9.8 %backward.1 = bf16[32,160,128]{2,1,0:T(8,128)(2,1)} custom-call(bf16[32,160,128]{2,1,0:T(8,128)(2,1)S(1)} %all-to-all-done.in_ref, bf16[2,2048,1024]{2,1,0:T(8,128)(2,1)S(1)} %get-tuple-element.22.e_ref, bf16[2048,128]{1,0:T(8,128)(2,1)S(1)} %get-tuple-element.23.gaug_ref, bf16[2048,128]{1,0:T(8,128)(2,1)S(1)} %get-tuple-element.24.vaug, ...), custom_call_target="tpu_custom_call" | custom-call | flops 8999999488 | bytes 20000000 | tf_op jit(solution)/shard_map/backward/pallas_call | solution.py:417
  132.0 9.1 %all-to-all-start.1 = ((bf16[32,160,128]{2,1,0:T(8,128)(2,1)}), bf16[32,160,128]{2,1,0:T(8,128)(2,1)S(1)}, u32[]{:S(2)}, u32[]{:S(2)}) async-start(bf16[32,160,128]{2,1,0:T(8,128)(2,1)} %backward.1), calls=%async_computation.1 | async-start | bytes 2621440 | tf_op jit(solution)/shard_map/all_to_all | solution.py:445
  141.1 3.2 %collective-permute-start.3 = (f32[32,128]{1,0:T(8,128)S(1)}, f32[32,128]{1,0:T(8,128)S(1)}, u32[]{:S(2)}, u32[]{:S(2)}) collective-permute-start(f32[32,128]{1,0:T(8,128)S(1)} %pad_maximum_fusion.4), channel_id=1, source_target_pairs={{0,4},{1,5},{2,6},{3,7},{4,0},{5,1},{6,2},{7,3},{8,12},{9,13},{10,... | collective-permute-start | bytes 49160 | tf_op jit(solution)/shard_map/ppermute | solution.py:450
  144.4 1.6 collective-permute-done.3
  145.9 4.8 %collective-permute-start.4 = (f32[32,128]{1,0:T(8,128)S(1)}, f32[32,128]{1,0:T(8,128)S(1)}, u32[]{:S(2)}, u32[]{:S(2)}) collective-permute-start(f32[32,128]{1,0:T(8,128)S(1)} %add.33), channel_id=1, source_target_pairs={{0,8},{1,9},{2,10},{3,11},{4,12},{5,13},{6,14},{7,15},{8,0},{9,1},... | collective-permute-start | bytes 49160 | tf_op jit(solution)/shard_map/ppermute | solution.py:450
  150.7 1.4 collective-permute-done.4
  152.2 2.6 %collective-permute-start.7 = (f32[32,128]{1,0:T(8,128)S(1)}, f32[32,128]{1,0:T(8,128)S(1)}, u32[]{:S(2)}, u32[]{:S(2)}) collective-permute-start(f32[32,128]{1,0:T(8,128)S(1)} %add.34), channel_id=1, source_target_pairs={{0,3},{1,2},{2,1},{3,0},{4,7},{5,6},{6,5},{7,4},{8,11},{9,10},{10,... | collective-permute-start | bytes 49160 | tf_op jit(solution)/shard_map/ppermute | solution.py:450
  154.8 2.6 %collective-permute-start.6 = (f32[32,128]{1,0:T(8,128)S(1)}, f32[32,128]{1,0:T(8,128)S(1)}, u32[]{:S(2)}, u32[]{:S(2)}) collective-permute-start(f32[32,128]{1,0:T(8,128)S(1)} %add.34), channel_id=1, source_target_pairs={{0,2},{1,3},{2,0},{3,1},{4,6},{5,7},{6,4},{7,5},{8,10},{9,11},{10,... | collective-permute-start | bytes 49160 | tf_op jit(solution)/shard_map/ppermute | solution.py:450
  157.5 4.0 %collective-permute-start.5 = (f32[32,128]{1,0:T(8,128)S(1)}, f32[32,128]{1,0:T(8,128)S(1)}, u32[]{:S(2)}, u32[]{:S(2)}) collective-permute-start(f32[32,128]{1,0:T(8,128)S(1)} %add.34), channel_id=1, source_target_pairs={{0,1},{1,0},{2,3},{3,2},{4,5},{5,4},{6,7},{7,6},{8,9},{9,8},{10,11... | collective-permute-start | bytes 49160 | tf_op jit(solution)/shard_map/ppermute | solution.py:450
  161.5 17.3 %collective-permute-done.7 = f32[32,128]{1,0:T(8,128)S(1)} collective-permute-done((f32[32,128]{1,0:T(8,128)S(1)}, f32[32,128]{1,0:T(8,128)S(1)}, u32[]{:S(2)}, u32[]{:S(2)}) %collective-permute-start.7) | collective-permute-done | bytes 16416 | tf_op jit(solution)/shard_map/ppermute | solution.py:450
  178.8 0.4 collective-permute-done.6
  179.1 15.7 %collective-permute-done.5 = f32[32,128]{1,0:T(8,128)S(1)} collective-permute-done((f32[32,128]{1,0:T(8,128)S(1)}, f32[32,128]{1,0:T(8,128)S(1)}, u32[]{:S(2)}, u32[]{:S(2)}) %collective-permute-start.5) | collective-permute-done | bytes 16416 | tf_op jit(solution)/shard_map/ppermute | solution.py:450
  194.8 2.9 %collective-permute-start.8 = (f32[32,128]{1,0:T(8,128)S(1)}, f32[32,128]{1,0:T(8,128)S(1)}, u32[]{:S(2)}, u32[]{:S(2)}) collective-permute-start(f32[32,128]{1,0:T(8,128)S(1)} %add_add_fusion), channel_id=1, source_target_pairs={{0,16},{16,0},{32,48},{48,32},{64,80},{80,64},{96,112},{112,96},{1... | collective-permute-start | bytes 49160 | tf_op jit(solution)/shard_map/ppermute | solution.py:450
  197.7 0.8 collective-permute-done.8
  198.5 3.7 %collective-permute-start.9 = (f32[64,128]{1,0:T(8,128)S(1)}, f32[64,128]{1,0:T(8,128)S(1)}, u32[]{:S(2)}, u32[]{:S(2)}) collective-permute-start(f32[64,128]{1,0:T(8,128)S(1)} %pad_maximum_fusion.2), channel_id=1, source_target_pairs={{0,32},{16,48},{32,0},{48,16},{64,96},{80,112},{96,64},{112,80},{1... | collective-permute-start | bytes 98312 | tf_op jit(solution)/shard_map/ppermute | solution.py:450
  202.3 1.4 collective-permute-done.9
  203.7 5.0 %collective-permute-start.10 = (f32[128,128]{1,0:T(8,128)S(1)}, f32[128,128]{1,0:T(8,128)S(1)}, u32[]{:S(2)}, u32[]{:S(2)}) collective-permute-start(f32[128,128]{1,0:T(8,128)S(1)} %pad_maximum_fusion.1), channel_id=1, source_target_pairs={{0,64},{16,80},{32,96},{48,112},{64,0},{80,16},{96,32},{112,48},{1... | collective-permute-start | bytes 196616 | tf_op jit(solution)/shard_map/ppermute | solution.py:450
  208.7 1.6 collective-permute-done.10
  210.4 0.8 unpack_params.1
  211.2 3.2 %unpack.1 = (bf16[64,2,1024]{2,1,0:T(2,128)(2,1)}, bf16[64,2,1024]{2,1,0:T(2,128)(2,1)}, bf16[64,2,1024]{2,1,0:T(2,128)(2,1)}, bf16[64,2,1024]{2,1,0:T(2,128)(2,1)}, bf16[64,2,1024]{2,1,0:T(2,128)(2,1)}) custom-call(bf16[32,160,128]{2,1,0:T(8,128)(2,1)S(1)} %all-to-all-done.1.in_ref), custom_call_target="tpu_custom_call" | custom-call | tf_op jit(solution)/shard_map/unpack/pallas_call | solution.py:367
  (20 shorter events, 0.1 us)
Async XLA Ops:
  7.0 19.4 %copy-start.2 = (s32[2]{0:T(128)S(1)}, s32[2]{0:T(128)}, u32[]{:S(2)}) copy-start(s32[2]{0:T(128)} %param.13) | copy-start | bytes 28
  7.0 20.1 %copy-start = (f32[31,1024]{1,0:T(8,128)S(1)}, f32[31,1024]{1,0:T(8,128)}, u32[]{:S(2)}) copy-start(f32[31,1024]{1,0:T(8,128)} %param.14) | copy-start | bytes 380932
  7.0 20.1 %copy-start.1 = (f32[1024]{0:T(1024)S(1)}, f32[1024]{0:T(1024)}, u32[]{:S(2)}) copy-start(f32[1024]{0:T(1024)} %param.15) | copy-start | bytes 12292
  7.0 83.6 %all-to-all-start = ((bf16[32,160,128]{2,1,0:T(8,128)(2,1)}), bf16[32,160,128]{2,1,0:T(8,128)(2,1)S(1)}, u32[]{:S(2)}, u32[]{:S(2)}) async-start(bf16[32,160,128]{2,1,0:T(8,128)(2,1)} %pack.1), calls=%async_computation | async-start | bytes 2621440 | tf_op jit(solution)/shard_map/all_to_all | solution.py:445
  105.8 26.2 %collective-permute-start.2 = (f32[16,128]{1,0:T(8,128)S(1)}, f32[16,128]{1,0:T(8,128)S(1)}, u32[]{:S(2)}, u32[]{:S(2)}) collective-permute-start(f32[16,128]{1,0:T(8,128)S(1)} %get-tuple-element.27), channel_id=1, source_target_pairs={{0,256},{16,272},{32,288},{48,304},{64,320},{80,336},{96,352},{112... | collective-permute-start | bytes 24584 | tf_op jit(solution)/shard_map/ppermute | solution.py:450
  112.9 19.0 %collective-permute-start = (f32[16,128]{1,0:T(8,128)S(1)}, f32[16,128]{1,0:T(8,128)S(1)}, u32[]{:S(2)}, u32[]{:S(2)}) collective-permute-start(f32[16,128]{1,0:T(8,128)S(1)} %get-tuple-element.27), channel_id=1, source_target_pairs={{0,128},{16,144},{32,160},{48,176},{64,192},{80,208},{96,224},{112... | collective-permute-start | bytes 24584 | tf_op jit(solution)/shard_map/ppermute | solution.py:450
  115.0 16.9 %collective-permute-start.1 = (f32[16,128]{1,0:T(8,128)S(1)}, f32[16,128]{1,0:T(8,128)S(1)}, u32[]{:S(2)}, u32[]{:S(2)}) collective-permute-start(f32[16,128]{1,0:T(8,128)S(1)} %get-tuple-element.27), channel_id=1, source_target_pairs={{0,384},{16,400},{32,416},{48,432},{64,448},{80,464},{96,480},{112... | collective-permute-start | bytes 24584 | tf_op jit(solution)/shard_map/ppermute | solution.py:450
  132.0 79.2 %all-to-all-start.1 = ((bf16[32,160,128]{2,1,0:T(8,128)(2,1)}), bf16[32,160,128]{2,1,0:T(8,128)(2,1)S(1)}, u32[]{:S(2)}, u32[]{:S(2)}) async-start(bf16[32,160,128]{2,1,0:T(8,128)(2,1)} %backward.1), calls=%async_computation.1 | async-start | bytes 2621440 | tf_op jit(solution)/shard_map/all_to_all | solution.py:445
  141.1 4.8 %collective-permute-start.3 = (f32[32,128]{1,0:T(8,128)S(1)}, f32[32,128]{1,0:T(8,128)S(1)}, u32[]{:S(2)}, u32[]{:S(2)}) collective-permute-start(f32[32,128]{1,0:T(8,128)S(1)} %pad_maximum_fusion.4), channel_id=1, source_target_pairs={{0,4},{1,5},{2,6},{3,7},{4,0},{5,1},{6,2},{7,3},{8,12},{9,13},{10,... | collective-permute-start | bytes 49160 | tf_op jit(solution)/shard_map/ppermute | solution.py:450
  145.9 6.3 %collective-permute-start.4 = (f32[32,128]{1,0:T(8,128)S(1)}, f32[32,128]{1,0:T(8,128)S(1)}, u32[]{:S(2)}, u32[]{:S(2)}) collective-permute-start(f32[32,128]{1,0:T(8,128)S(1)} %add.33), channel_id=1, source_target_pairs={{0,8},{1,9},{2,10},{3,11},{4,12},{5,13},{6,14},{7,15},{8,0},{9,1},... | collective-permute-start | bytes 49160 | tf_op jit(solution)/shard_map/ppermute | solution.py:450
  152.2 26.6 %collective-permute-start.7 = (f32[32,128]{1,0:T(8,128)S(1)}, f32[32,128]{1,0:T(8,128)S(1)}, u32[]{:S(2)}, u32[]{:S(2)}) collective-permute-start(f32[32,128]{1,0:T(8,128)S(1)} %add.34), channel_id=1, source_target_pairs={{0,3},{1,2},{2,1},{3,0},{4,7},{5,6},{6,5},{7,4},{8,11},{9,10},{10,... | collective-permute-start | bytes 49160 | tf_op jit(solution)/shard_map/ppermute | solution.py:450
  154.8 24.3 %collective-permute-start.6 = (f32[32,128]{1,0:T(8,128)S(1)}, f32[32,128]{1,0:T(8,128)S(1)}, u32[]{:S(2)}, u32[]{:S(2)}) collective-permute-start(f32[32,128]{1,0:T(8,128)S(1)} %add.34), channel_id=1, source_target_pairs={{0,2},{1,3},{2,0},{3,1},{4,6},{5,7},{6,4},{7,5},{8,10},{9,11},{10,... | collective-permute-start | bytes 49160 | tf_op jit(solution)/shard_map/ppermute | solution.py:450
  157.5 37.3 %collective-permute-start.5 = (f32[32,128]{1,0:T(8,128)S(1)}, f32[32,128]{1,0:T(8,128)S(1)}, u32[]{:S(2)}, u32[]{:S(2)}) collective-permute-start(f32[32,128]{1,0:T(8,128)S(1)} %add.34), channel_id=1, source_target_pairs={{0,1},{1,0},{2,3},{3,2},{4,5},{5,4},{6,7},{7,6},{8,9},{9,8},{10,11... | collective-permute-start | bytes 49160 | tf_op jit(solution)/shard_map/ppermute | solution.py:450
  194.8 3.7 %collective-permute-start.8 = (f32[32,128]{1,0:T(8,128)S(1)}, f32[32,128]{1,0:T(8,128)S(1)}, u32[]{:S(2)}, u32[]{:S(2)}) collective-permute-start(f32[32,128]{1,0:T(8,128)S(1)} %add_add_fusion), channel_id=1, source_target_pairs={{0,16},{16,0},{32,48},{48,32},{64,80},{80,64},{96,112},{112,96},{1... | collective-permute-start | bytes 49160 | tf_op jit(solution)/shard_map/ppermute | solution.py:450
  198.5 5.1 %collective-permute-start.9 = (f32[64,128]{1,0:T(8,128)S(1)}, f32[64,128]{1,0:T(8,128)S(1)}, u32[]{:S(2)}, u32[]{:S(2)}) collective-permute-start(f32[64,128]{1,0:T(8,128)S(1)} %pad_maximum_fusion.2), channel_id=1, source_target_pairs={{0,32},{16,48},{32,0},{48,16},{64,96},{80,112},{96,64},{112,80},{1... | collective-permute-start | bytes 98312 | tf_op jit(solution)/shard_map/ppermute | solution.py:450
  203.7 6.6 %collective-permute-start.10 = (f32[128,128]{1,0:T(8,128)S(1)}, f32[128,128]{1,0:T(8,128)S(1)}, u32[]{:S(2)}, u32[]{:S(2)}) collective-permute-start(f32[128,128]{1,0:T(8,128)S(1)} %pad_maximum_fusion.1), channel_id=1, source_target_pairs={{0,64},{16,80},{32,96},{48,112},{64,0},{80,16},{96,32},{112,48},{1... | collective-permute-start | bytes 196616 | tf_op jit(solution)/shard_map/ppermute | solution.py:450

commit v4 on v3

--- a/solution.py
+++ b/solution.py
@@ -70,23 +70,23 @@
     pair(f_ref, c_ref, rows * 3 // 2)
 
 
-def unpack_kernel(in_ref, q_ref, k_ref, v_ref, f_ref, c_ref):
-    rows, utts, _ = q_ref.shape
-
-    def pair(a_ref, b_ref, first):
-        firsts, seconds = [], []
-        for u in range(utts):
-            blocks = [in_ref[u * HEADS + h, first : first + rows, :] for h in range(HEADS)]
-            firsts.append(jnp.concatenate([x[:, :HD] for x in blocks], axis=1))
-            seconds.append(jnp.concatenate([x[:, HD:] for x in blocks], axis=1))
-        a_ref[...] = jnp.stack(firsts, axis=1)
-        b_ref[...] = jnp.stack(seconds, axis=1)
-
-    pair(f_ref, c_ref, rows * 3 // 2)
-    pair(q_ref, k_ref, 0)
+def unpack_pair(in_ref, a_ref, b_ref):
+    rows, utts, _ = a_ref.shape
+    firsts, seconds = [], []
+    for u in range(utts):
+        blocks = [in_ref[u * HEADS + h, :rows, :] for h in range(HEADS)]
+        firsts.append(jnp.concatenate([x[:, :HD] for x in blocks], axis=1))
+        seconds.append(jnp.concatenate([x[:, HD:] for x in blocks], axis=1))
+    a_ref[...] = jnp.stack(firsts, axis=1)
+    b_ref[...] = jnp.stack(seconds, axis=1)
+
+
+def unpack_qkv_kernel(in_ref, q_ref, k_ref, v_ref):
+    unpack_pair(in_ref, q_ref, k_ref)
+    rows, utts, _ = v_ref.shape
     values = []
     for u in range(utts):
-        blocks = [in_ref[u * HEADS + h, rows : rows * 3 // 2, :] for h in range(HEADS)]
+        blocks = [in_ref[u * HEADS + h, rows:, :] for h in range(HEADS)]
         top = jnp.concatenate([x[:, :HD] for x in blocks], axis=1)
         bottom = jnp.concatenate([x[:, HD:] for x in blocks], axis=1)
         values.append(jnp.concatenate([top, bottom], axis=0))
@@ -253,14 +253,13 @@
     lax.fori_loop(0, steps, backward_step, 0)
 
 
-def backward_kernel(in_ref, e_ref, gaug_ref, vaug, kt, bogf_ref, out_ref, acc):
+def backward_kernel(in_ref, e_ref, gaug_ref, vaug, kt, out_ref, acc):
     sources = in_ref.shape[0]
     rows = in_ref.shape[1] * 2 // 5
     length = sources * rows
     per_block = QB // rows
     chunks = length // KC
     acc[...] = jnp.zeros_like(acc)
-    out_ref[:, rows * 3 // 2 :, :] = bogf_ref[...]
 
     def step(block, carry):
         q = in_ref[pl.ds(block * per_block, per_block), :rows, :].reshape(QB, LANES).astype(F32)
@@ -302,7 +301,7 @@
     half = rows // 2
     upper = swap_halves(both[:, half:, :].reshape(length // 2, LANES)).reshape(sources, half, LANES)
     gv = jnp.where(lane_ids(upper.shape) < HD, both[:, :half, :], upper) * 8.0
-    out_ref[:, rows : rows * 3 // 2, :] = gv.astype(BF16)
+    out_ref[:, rows:, :] = gv.astype(BF16)
 
 
 def forward_kernel(
@@ -363,14 +362,14 @@
     )(*fields)
 
 
-def unpack(field, rows, utts):
+def unpack(kernel, field, rows, utts, count):
     return pl.pallas_call(
-        unpack_kernel,
-        out_shape=[shape_of(rows, utts, HEADS * HD)] * 5,
+        kernel,
+        out_shape=[shape_of(rows, utts, HEADS * HD)] * count,
         in_specs=[VMEM],
-        out_specs=[VMEM] * 5,
+        out_specs=[VMEM] * count,
         compiler_params=params(24),
-        name="unpack",
+        name="unpack%d" % count,
     )(field)
 
 
@@ -412,12 +411,13 @@
     )(frames, field, taps)
 
 
-def backward(field, e, gaug, vaug, kt, bogf):
+def backward(field, e, gaug, vaug, kt):
+    sources, tall, _ = field.shape
     length = e.shape[1]
     return pl.pallas_call(
         backward_kernel,
-        out_shape=shape_of(*field.shape),
-        in_specs=[VMEM] * 6,
+        out_shape=shape_of(sources, tall * 3 // 5, LANES),
+        in_specs=[VMEM] * 5,
         out_specs=VMEM,
         scratch_shapes=[pltpu.VMEM((length, LANES), F32)],
         compiler_params=params(36),
@@ -425,7 +425,7 @@
             flops=9_000_000_000, bytes_accessed=20_000_000, transcendentals=0
         ),
         name="backward",
-    )(field, e, gaug, vaug, kt, bogf)
+    )(field, e, gaug, vaug, kt)
 
 
 def unpack_params(parts):
@@ -458,17 +458,21 @@
     return jnp.concatenate([first, second], axis=0)
 
 
-def over_utterances(part):
+def over_y(part):
+    for bit in (4, 8):
+        part = part + swap(part, "dp", bit)
+    return part
+
+
+def over_z_low(part):
+    return part + swap(part, "dp", 1) + swap(part, "dp", 2) + swap(part, "dp", 3)
+
+
+def over_seq(part):
     other = swap(part, "seq", 8) + swap(part, "seq", 24)
     part = part + swap(part, "seq", 16)
     upper = (lax.axis_index("seq") & 8) != 0
-    return jnp.concatenate([jnp.where(upper, other, part), jnp.where(upper, part, other)], axis=0)
-
-
-def over_devices(part):
-    for bit in (4, 8):
-        part = part + swap(part, "dp", bit)
-    part = part + swap(part, "dp", 1) + swap(part, "dp", 2) + swap(part, "dp", 3)
+    part = jnp.concatenate([jnp.where(upper, other, part), jnp.where(upper, part, other)], axis=0)
     for bit in (1, 2, 4):
         part = joined(part, "seq", bit)
     half = (TAPS + 1) // 2
@@ -490,12 +494,15 @@
 
     field = exchange(pack(queries, key_vectors, value_vectors, features, cotangent))
     *state, bogf, part = forward(valid, field, taps)
-    part = over_utterances(part)
-    field = backward(field, *state, bogf)
-    field, part = lax.optimization_barrier((field, part))
-    field = exchange(field)
-    grad_kernel, grad_bias = over_devices(part)
-    grad_q, grad_k, grad_v, block_out, grad_features = unpack(field, rows, utts)
+    bogf = exchange(bogf)
+    part = over_y(part)
+    part = over_z_low(part)
+    grads = backward(field, *state)
+    grads, part = lax.optimization_barrier((grads, part))
+    grads = exchange(grads)
+    block_out, grad_features = unpack(unpack_pair, bogf, rows, utts, 2)
+    grad_kernel, grad_bias = over_seq(part)
+    grad_q, grad_k, grad_v = unpack(unpack_qkv_kernel, grads, rows, utts, 3)
     return block_out, grad_features, grad_q, grad_k, grad_v, grad_kernel, grad_bias
 
 

time: 217 us -> 236 us (1.088)
  starting transfers between devices: 73.8 us -> 92.2 us
  waiting for transfers between devices: 104 us -> 94.6 us
  local copies, waits for them, and re-layouts: 0.03 us -> 8.51 us
    all_to_all x2 -> x3, starting transfers between devices: 28.5 us -> 44.8 us  [exchange(): return lax.all_to_all(field, 'seq', split_axis=0, concat_axis=0, tiled=True)]
    ppermute x11, waiting for transfers between devices: 40.2 us -> 31.2 us  [swap(): return lax.ppermute(field, axis, [(i, i ^ bit) for i in range(count)])]
    unnamed x6 -> x14, local copies, waits for them, and re-layouts: 0.02 us -> 8.5 us
    pallas_call x2 -> x3, Pallas kernels: 13 us -> 13.3 us  [the longest x1 9.34 us: backward(): pl.pallas_call(backward_kernel, out_shape=shape_of(sources, tall * 3 // 5...]
    all_to_all x2 -> x3, waiting for transfers between devices: 63.4 us -> 63.4 us  [exchange(): return lax.all_to_all(field, 'seq', split_axis=0, concat_axis=0, tiled=True)]
  transfers between devices with their start and end apart: 13 -> 14, of which waited for: 9 -> 7; matrix products, arithmetic and copies ran while one was open for 0% -> 0% of each run, Pallas kernels for 5% -> 5%
where the time goes in v4:
time: 236 us; the launch traced here: 233 us
  waiting for transfers between devices  94.6 us (40%)
  starting transfers between devices  92.2 us (39%)
  Pallas kernels  36.4 us (15%)
  local copies, waits for them, and re-layouts  8.51 us (4%)
    all_to_all x3, waiting for transfers between devices, exchange(): return lax.all_to_all(field, 'seq', split_axis=0, concat_axis=0, tiled=True)  63.4 us
    ppermute x11, starting transfers between devices, swap(): return lax.ppermute(field, axis, [(i, i ^ bit) for i in range(count)])  47.4 us
    all_to_all x3, starting transfers between devices, exchange(): return lax.all_to_all(field, 'seq', split_axis=0, concat_axis=0, tiled=True)  44.8 us
    ppermute x11, waiting for transfers between devices, swap(): return lax.ppermute(field, axis, [(i, i ^ bit) for i in range(count)])  31.2 us
    pallas_call x1, Pallas kernels, forward(): pl.pallas_call(forward_kernel, out_shape=[shape_of(length // QB, length,...  16 us
    pallas_call x1, Pallas kernels, backward(): pl.pallas_call(backward_kernel, out_shape=shape_of(sources, tall * 3 // 5...  9.34 us
    unnamed x14, local copies, waits for them, and re-layouts  8.5 us
    pallas_call x1, Pallas kernels, pack(): pl.pallas_call(pack_kernel, out_shape=shape_of(utts * HEADS, rows * 5 //...  6.32 us
  transfers between devices with their start and end apart: 14, of which 7 were waited for; matrix products, arithmetic and copies ran while one was open for 0% of the time, Pallas kernels for 5%

profile of v4, /device:TPU:1, one launch (start us, length us, event | category | flops | bytes accessed | tf_op | source)
XLA Modules:
  0.0 233.5 jit_solution(8939298012281618908)
XLA Ops:
  0.6 6.3 %pack.1 = bf16[32,160,128]{2,1,0:T(8,128)(2,1)} custom-call(bf16[64,2,1024]{2,1,0:T(2,128)(2,1)} %q_hbm.1, bf16[64,2,1024]{2,1,0:T(2,128)(2,1)} %k_hbm.1, bf16[64,2,1024]{2,1,0:T(2,128)(2,1)} %v_hbm.1, bf16[64,2,1024]{2,1,0:T(2,128)(2,1)} %f_hbm.1, bf16[64,2,1024]{2,1,0:T(2,128)(2,1)} %c_hbm.1), custom_call_target="tpu_custom_call" | custom-call | tf_op jit(solution)/shard_map/pack/pallas_call | solution.py:354
  7.0 19.4 %all-to-all-start = ((bf16[32,160,128]{2,1,0:T(8,128)(2,1)}), bf16[32,160,128]{2,1,0:T(8,128)(2,1)S(1)}, u32[]{:S(2)}, u32[]{:S(2)}) async-start(bf16[32,160,128]{2,1,0:T(8,128)(2,1)} %pack.1), calls=%async_computation | async-start | bytes 2621440 | tf_op jit(solution)/shard_map/all_to_all | solution.py:445
  26.4 0.6 fusion.1
  27.2 63.4 %all-to-all-done.in_ref = bf16[32,160,128]{2,1,0:T(8,128)(2,1)S(1)} async-done(((bf16[32,160,128]{2,1,0:T(8,128)(2,1)}), bf16[32,160,128]{2,1,0:T(8,128)(2,1)S(1)}, u32[]{:S(2)}, u32[]{:S(2)}) %all-to-all-start) | async-done | bytes 1310752 | tf_op jit(solution)/shard_map/all_to_all | solution.py:445
  90.6 16.0 %forward.1 = (bf16[2,2048,1024]{2,1,0:T(8,128)(2,1)S(1)}, bf16[2048,128]{1,0:T(8,128)(2,1)S(1)}, bf16[2048,128]{1,0:T(8,128)(2,1)S(1)}, bf16[128,2048]{1,0:T(8,1...) custom-call(s32[1]{0:T(128)} %bitcast.frames_ref, bf16[32,160,128]{2,1,0:T(8,128)(2,1)S(1)} %all-to-all-done.in_ref, ...), custom_call_target="tpu_custom_call" | custom-call | flops 8000000000 | bytes 20000000 | tf_op jit(solution)/shard_map/forward/pallas_call | solution.py:382
  106.6 3.3 %copy-done = bf16[2,2048,1024]{2,1,0:T(8,128)(2,1)} copy-done((bf16[2,2048,1024]{2,1,0:T(8,128)(2,1)}, bf16[2,2048,1024]{2,1,0:T(8,128)(2,1)S(1)}, u32[]{:S(2)}) %copy-start) | copy-done | bytes 8388632
  109.9 0.8 copy-done.2
  110.7 8.3 %all-to-all-start.1 = ((bf16[32,64,128]{2,1,0:T(8,128)(2,1)}), bf16[32,64,128]{2,1,0:T(8,128)(2,1)S(1)}, u32[]{:S(2)}, u32[]{:S(2)}) async-start(bf16[32,64,128]{2,1,0:T(8,128)(2,1)} %get-tuple-element.22), calls=%async_computation.1 | async-start | bytes 1048576 | tf_op jit(solution)/shard_map/all_to_all | solution.py:445
  119.0 3.2 %collective-permute-start = (f32[16,128]{1,0:T(8,128)S(1)}, f32[16,128]{1,0:T(8,128)S(1)}, u32[]{:S(2)}, u32[]{:S(2)}) collective-permute-start(f32[16,128]{1,0:T(8,128)S(1)} %get-tuple-element.29), channel_id=1, source_target_pairs={{0,4},{1,5},{2,6},{3,7},{4,0},{5,1},{6,2},{7,3},{8,12},{9,13},{10,... | collective-permute-start | bytes 24584 | tf_op jit(solution)/shard_map/ppermute | solution.py:450
  122.2 1.5 collective-permute-done
  123.7 4.8 %collective-permute-start.1 = (f32[16,128]{1,0:T(8,128)S(1)}, f32[16,128]{1,0:T(8,128)S(1)}, u32[]{:S(2)}, u32[]{:S(2)}) collective-permute-start(f32[16,128]{1,0:T(8,128)S(1)} %add.31), channel_id=1, source_target_pairs={{0,8},{1,9},{2,10},{3,11},{4,12},{5,13},{6,14},{7,15},{8,0},{9,1},... | collective-permute-start | bytes 24584 | tf_op jit(solution)/shard_map/ppermute | solution.py:450
  128.5 1.4 collective-permute-done.1
  129.8 2.2 collective-permute-start.2
  132.0 2.6 %collective-permute-start.3 = (f32[16,128]{1,0:T(8,128)S(1)}, f32[16,128]{1,0:T(8,128)S(1)}, u32[]{:S(2)}, u32[]{:S(2)}) collective-permute-start(f32[16,128]{1,0:T(8,128)S(1)} %add.32), channel_id=1, source_target_pairs={{0,2},{1,3},{2,0},{3,1},{4,6},{5,7},{6,4},{7,5},{8,10},{9,11},{10,... | collective-permute-start | bytes 24584 | tf_op jit(solution)/shard_map/ppermute | solution.py:450
  134.7 4.6 %collective-permute-start.4 = (f32[16,128]{1,0:T(8,128)S(1)}, f32[16,128]{1,0:T(8,128)S(1)}, u32[]{:S(2)}, u32[]{:S(2)}) collective-permute-start(f32[16,128]{1,0:T(8,128)S(1)} %add.32), channel_id=1, source_target_pairs={{0,3},{1,2},{2,1},{3,0},{4,7},{5,6},{6,5},{7,4},{8,11},{9,10},{10,... | collective-permute-start | bytes 24584 | tf_op jit(solution)/shard_map/ppermute | solution.py:450
  139.4 3.4 %copy-done.1 = bf16[2,2048,1024]{2,1,0:T(8,128)(2,1)S(1)} copy-done((bf16[2,2048,1024]{2,1,0:T(8,128)(2,1)S(1)}, bf16[2,2048,1024]{2,1,0:T(8,128)(2,1)}, u32[]{:S(2)}) %copy-start.1) | copy-done | bytes 8388632
  142.7 1.0 copy-done.3
  143.8 9.3 %backward.1 = bf16[32,96,128]{2,1,0:T(8,128)(2,1)} custom-call(bf16[32,160,128]{2,1,0:T(8,128)(2,1)S(1)} %all-to-all-done.in_ref, bf16[2,2048,1024]{2,1,0:T(8,128)(2,1)S(1)} %copy-done.1, bf16[2048,128]{1,0:T(8,128)(2,1)S(1)} %get-tuple-element.26.gaug_ref, bf16[2048,128]{1,0:T(8,128)(2,1)S(1)} %get-tuple-element.27.vaug, bf16[128,2048]{1,0:T(8,128)(2,1)S(1)} %copy-done.3), custom_call_target="tpu_custom_call" | custom-call | flops 8999999488 | bytes 20000000 | tf_op jit(solution)/shard_map/backward/pallas_call | solution.py:417
  153.2 17.2 %all-to-all-start.2 = ((bf16[32,96,128]{2,1,0:T(8,128)(2,1)}), bf16[32,96,128]{2,1,0:T(8,128)(2,1)S(1)}, u32[]{:S(2)}, u32[]{:S(2)}) async-start(bf16[32,96,128]{2,1,0:T(8,128)(2,1)} %backward.1), calls=%async_computation.2 | async-start | bytes 1572864 | tf_op jit(solution)/shard_map/all_to_all | solution.py:445
  170.3 7.2 %collective-permute-start.5 = (f32[16,128]{1,0:T(8,128)S(1)}, f32[16,128]{1,0:T(8,128)S(1)}, u32[]{:S(2)}, u32[]{:S(2)}) collective-permute-start(f32[16,128]{1,0:T(8,128)S(1)} %add_add_fusion), channel_id=1, source_target_pairs={{0,128},{16,144},{32,160},{48,176},{64,192},{80,208},{96,224},{112... | collective-permute-start | bytes 24584 | tf_op jit(solution)/shard_map/ppermute | solution.py:450
  177.5 7.0 %collective-permute-start.6 = (f32[16,128]{1,0:T(8,128)S(1)}, f32[16,128]{1,0:T(8,128)S(1)}, u32[]{:S(2)}, u32[]{:S(2)}) collective-permute-start(f32[16,128]{1,0:T(8,128)S(1)} %add_add_fusion), channel_id=1, source_target_pairs={{0,384},{16,400},{32,416},{48,432},{64,448},{80,464},{96,480},{112... | collective-permute-start | bytes 24584 | tf_op jit(solution)/shard_map/ppermute | solution.py:450
  184.5 2.0 collective-permute-start.7
  186.5 24.1 %collective-permute-done.5 = f32[16,128]{1,0:T(8,128)S(1)} collective-permute-done((f32[16,128]{1,0:T(8,128)S(1)}, f32[16,128]{1,0:T(8,128)S(1)}, u32[]{:S(2)}, u32[]{:S(2)}) %collective-permute-start.5) | collective-permute-done | bytes 8224 | tf_op jit(solution)/shard_map/ppermute | solution.py:450
  210.7 2.4 %collective-permute-start.8 = (f32[32,128]{1,0:T(8,128)S(1)}, f32[32,128]{1,0:T(8,128)S(1)}, u32[]{:S(2)}, u32[]{:S(2)}) collective-permute-start(f32[32,128]{1,0:T(8,128)S(1)} %pad_maximum_fusion.4), channel_id=1, source_target_pairs={{0,16},{16,0},{32,48},{48,32},{64,80},{80,64},{96,112},{112,96},{1... | collective-permute-start | bytes 49160 | tf_op jit(solution)/shard_map/ppermute | solution.py:450
  213.1 0.8 collective-permute-done.8
  213.9 7.0 %collective-permute-start.9 = (f32[64,128]{1,0:T(8,128)S(1)}, f32[64,128]{1,0:T(8,128)S(1)}, u32[]{:S(2)}, u32[]{:S(2)}) collective-permute-start(f32[64,128]{1,0:T(8,128)S(1)} %pad_maximum_fusion.2), channel_id=1, source_target_pairs={{0,32},{16,48},{32,0},{48,16},{64,96},{80,112},{96,64},{112,80},{1... | collective-permute-start | bytes 98312 | tf_op jit(solution)/shard_map/ppermute | solution.py:450
  220.9 1.3 collective-permute-done.9
  222.2 4.3 %collective-permute-start.10 = (f32[128,128]{1,0:T(8,128)S(1)}, f32[128,128]{1,0:T(8,128)S(1)}, u32[]{:S(2)}, u32[]{:S(2)}) collective-permute-start(f32[128,128]{1,0:T(8,128)S(1)} %pad_maximum_fusion.1), channel_id=1, source_target_pairs={{0,64},{16,80},{32,96},{48,112},{64,0},{80,16},{96,32},{112,48},{1... | collective-permute-start | bytes 196616 | tf_op jit(solution)/shard_map/ppermute | solution.py:450
  226.5 2.2 collective-permute-done.10
  228.7 0.8 unpack_params.1
  229.5 1.7 unpack2.1
  231.3 2.2 unpack3.1
  (31 shorter events, 0.3 us)
Async XLA Ops:
  7.0 19.4 %copy-start.6 = (s32[2]{0:T(128)S(1)}, s32[2]{0:T(128)}, u32[]{:S(2)}) copy-start(s32[2]{0:T(128)} %param.13) | copy-start | bytes 28
  7.0 20.1 %copy-start.4 = (f32[31,1024]{1,0:T(8,128)S(1)}, f32[31,1024]{1,0:T(8,128)}, u32[]{:S(2)}) copy-start(f32[31,1024]{1,0:T(8,128)} %param.14) | copy-start | bytes 380932
  7.0 20.1 %copy-start.5 = (f32[1024]{0:T(1024)S(1)}, f32[1024]{0:T(1024)}, u32[]{:S(2)}) copy-start(f32[1024]{0:T(1024)} %param.15) | copy-start | bytes 12292
  7.0 83.6 %all-to-all-start = ((bf16[32,160,128]{2,1,0:T(8,128)(2,1)}), bf16[32,160,128]{2,1,0:T(8,128)(2,1)S(1)}, u32[]{:S(2)}, u32[]{:S(2)}) async-start(bf16[32,160,128]{2,1,0:T(8,128)(2,1)} %pack.1), calls=%async_computation | async-start | bytes 2621440 | tf_op jit(solution)/shard_map/all_to_all | solution.py:445
  106.6 3.3 %copy-start = (bf16[2,2048,1024]{2,1,0:T(8,128)(2,1)}, bf16[2,2048,1024]{2,1,0:T(8,128)(2,1)S(1)}, u32[]{:S(2)}) copy-start(bf16[2,2048,1024]{2,1,0:T(8,128)(2,1)S(1)} %get-tuple-element.25.e_ref) | copy-start | bytes 25165828
  109.9 0.8 copy-start.2
  110.7 42.5 %all-to-all-start.1 = ((bf16[32,64,128]{2,1,0:T(8,128)(2,1)}), bf16[32,64,128]{2,1,0:T(8,128)(2,1)S(1)}, u32[]{:S(2)}, u32[]{:S(2)}) async-start(bf16[32,64,128]{2,1,0:T(8,128)(2,1)} %get-tuple-element.22), calls=%async_computation.1 | async-start | bytes 1048576 | tf_op jit(solution)/shard_map/all_to_all | solution.py:445
  119.0 4.7 %collective-permute-start = (f32[16,128]{1,0:T(8,128)S(1)}, f32[16,128]{1,0:T(8,128)S(1)}, u32[]{:S(2)}, u32[]{:S(2)}) collective-permute-start(f32[16,128]{1,0:T(8,128)S(1)} %get-tuple-element.29), channel_id=1, source_target_pairs={{0,4},{1,5},{2,6},{3,7},{4,0},{5,1},{6,2},{7,3},{8,12},{9,13},{10,... | collective-permute-start | bytes 24584 | tf_op jit(solution)/shard_map/ppermute | solution.py:450
  123.7 6.2 %collective-permute-start.1 = (f32[16,128]{1,0:T(8,128)S(1)}, f32[16,128]{1,0:T(8,128)S(1)}, u32[]{:S(2)}, u32[]{:S(2)}) collective-permute-start(f32[16,128]{1,0:T(8,128)S(1)} %add.31), channel_id=1, source_target_pairs={{0,8},{1,9},{2,10},{3,11},{4,12},{5,13},{6,14},{7,15},{8,0},{9,1},... | collective-permute-start | bytes 24584 | tf_op jit(solution)/shard_map/ppermute | solution.py:450
  129.8 23.3 %collective-permute-start.2 = (f32[16,128]{1,0:T(8,128)S(1)}, f32[16,128]{1,0:T(8,128)S(1)}, u32[]{:S(2)}, u32[]{:S(2)}) collective-permute-start(f32[16,128]{1,0:T(8,128)S(1)} %add.32), channel_id=1, source_target_pairs={{0,1},{1,0},{2,3},{3,2},{4,5},{5,4},{6,7},{7,6},{8,9},{9,8},{10,11... | collective-permute-start | bytes 24584 | tf_op jit(solution)/shard_map/ppermute | solution.py:450
  132.0 21.1 %collective-permute-start.3 = (f32[16,128]{1,0:T(8,128)S(1)}, f32[16,128]{1,0:T(8,128)S(1)}, u32[]{:S(2)}, u32[]{:S(2)}) collective-permute-start(f32[16,128]{1,0:T(8,128)S(1)} %add.32), channel_id=1, source_target_pairs={{0,2},{1,3},{2,0},{3,1},{4,6},{5,7},{6,4},{7,5},{8,10},{9,11},{10,... | collective-permute-start | bytes 24584 | tf_op jit(solution)/shard_map/ppermute | solution.py:450
  134.7 18.4 %collective-permute-start.4 = (f32[16,128]{1,0:T(8,128)S(1)}, f32[16,128]{1,0:T(8,128)S(1)}, u32[]{:S(2)}, u32[]{:S(2)}) collective-permute-start(f32[16,128]{1,0:T(8,128)S(1)} %add.32), channel_id=1, source_target_pairs={{0,3},{1,2},{2,1},{3,0},{4,7},{5,6},{6,5},{7,4},{8,11},{9,10},{10,... | collective-permute-start | bytes 24584 | tf_op jit(solution)/shard_map/ppermute | solution.py:450
  139.4 3.4 %copy-start.1 = (bf16[2,2048,1024]{2,1,0:T(8,128)(2,1)S(1)}, bf16[2,2048,1024]{2,1,0:T(8,128)(2,1)}, u32[]{:S(2)}) copy-start(bf16[2,2048,1024]{2,1,0:T(8,128)(2,1)} %copy-done) | copy-start | bytes 25165828
  142.7 1.0 copy-start.3
  153.2 78.1 %all-to-all-start.2 = ((bf16[32,96,128]{2,1,0:T(8,128)(2,1)}), bf16[32,96,128]{2,1,0:T(8,128)(2,1)S(1)}, u32[]{:S(2)}, u32[]{:S(2)}) async-start(bf16[32,96,128]{2,1,0:T(8,128)(2,1)} %backward.1), calls=%async_computation.2 | async-start | bytes 1572864 | tf_op jit(solution)/shard_map/all_to_all | solution.py:445
  170.3 40.3 %collective-permute-start.5 = (f32[16,128]{1,0:T(8,128)S(1)}, f32[16,128]{1,0:T(8,128)S(1)}, u32[]{:S(2)}, u32[]{:S(2)}) collective-permute-start(f32[16,128]{1,0:T(8,128)S(1)} %add_add_fusion), channel_id=1, source_target_pairs={{0,128},{16,144},{32,160},{48,176},{64,192},{80,208},{96,224},{112... | collective-permute-start | bytes 24584 | tf_op jit(solution)/shard_map/ppermute | solution.py:450
  177.5 33.1 %collective-permute-start.6 = (f32[16,128]{1,0:T(8,128)S(1)}, f32[16,128]{1,0:T(8,128)S(1)}, u32[]{:S(2)}, u32[]{:S(2)}) collective-permute-start(f32[16,128]{1,0:T(8,128)S(1)} %add_add_fusion), channel_id=1, source_target_pairs={{0,384},{16,400},{32,416},{48,432},{64,448},{80,464},{96,480},{112... | collective-permute-start | bytes 24584 | tf_op jit(solution)/shard_map/ppermute | solution.py:450
  184.5 26.1 %collective-permute-start.7 = (f32[16,128]{1,0:T(8,128)S(1)}, f32[16,128]{1,0:T(8,128)S(1)}, u32[]{:S(2)}, u32[]{:S(2)}) collective-permute-start(f32[16,128]{1,0:T(8,128)S(1)} %add_add_fusion), channel_id=1, source_target_pairs={{0,256},{16,272},{32,288},{48,304},{64,320},{80,336},{96,352},{112... | collective-permute-start | bytes 24584 | tf_op jit(solution)/shard_map/ppermute | solution.py:450
  210.7 3.2 %collective-permute-start.8 = (f32[32,128]{1,0:T(8,128)S(1)}, f32[32,128]{1,0:T(8,128)S(1)}, u32[]{:S(2)}, u32[]{:S(2)}) collective-permute-start(f32[32,128]{1,0:T(8,128)S(1)} %pad_maximum_fusion.4), channel_id=1, source_target_pairs={{0,16},{16,0},{32,48},{48,32},{64,80},{80,64},{96,112},{112,96},{1... | collective-permute-start | bytes 49160 | tf_op jit(solution)/shard_map/ppermute | solution.py:450
  213.9 8.3 %collective-permute-start.9 = (f32[64,128]{1,0:T(8,128)S(1)}, f32[64,128]{1,0:T(8,128)S(1)}, u32[]{:S(2)}, u32[]{:S(2)}) collective-permute-start(f32[64,128]{1,0:T(8,128)S(1)} %pad_maximum_fusion.2), channel_id=1, source_target_pairs={{0,32},{16,48},{32,0},{48,16},{64,96},{80,112},{96,64},{112,80},{1... | collective-permute-start | bytes 98312 | tf_op jit(solution)/shard_map/ppermute | solution.py:450
  222.2 6.5 %collective-permute-start.10 = (f32[128,128]{1,0:T(8,128)S(1)}, f32[128,128]{1,0:T(8,128)S(1)}, u32[]{:S(2)}, u32[]{:S(2)}) collective-permute-start(f32[128,128]{1,0:T(8,128)S(1)} %pad_maximum_fusion.1), channel_id=1, source_target_pairs={{0,64},{16,80},{32,96},{48,112},{64,0},{80,16},{96,32},{112,48},{1... | collective-permute-start | bytes 196616 | tf_op jit(solution)/shard_map/ppermute | solution.py:450

commit v5 on v3

--- a/solution.py
+++ b/solution.py
@@ -333,17 +333,26 @@
     )
 
 
-def params_kernel(in_ref, taps_ref, bias_ref):
-    half = in_ref.shape[1]
+def params_kernel(place_ref, *refs):
+    *parts, taps_ref, bias_ref, heads = refs
+    place = place_ref[0]
+    core, x, half = place % 2, place // 2 % len(parts), place // 8 % 2
+    for i, part in enumerate(parts):
+        for j in range(part.shape[0]):
+            for n in range(part.shape[1]):
+                other = (x + len(parts) - i) % len(parts)
+                head = (half + n) % 2 * 8 + other * 2 + (core + j) % 2
+                heads[head] = part[j, n]
+    rows = heads.shape[1]
     for h in range(0, HEADS, 2):
-        part = slice(h * HD, (h + 2) * HD)
-        a = in_ref[h]
-        b = in_ref[h + 1]
+        lanes = slice(h * HD, (h + 2) * HD)
+        a = heads[h]
+        b = heads[h + 1]
         low = lane_pair(a[:, :HD], b[:, :HD])
         high = lane_pair(a[:, HD:], b[:, HD:])
-        taps_ref[:half, part] = low
-        taps_ref[half:, part] = high[: TAPS - half]
-        bias_ref[:, part] = high[TAPS - half :]
+        taps_ref[:rows, lanes] = low
+        taps_ref[rows:, lanes] = high[: TAPS - rows]
+        bias_ref[:, lanes] = high[TAPS - rows :]
 
 
 def shape_of(*dims, dtype=BF16):
@@ -428,16 +437,17 @@
     )(field, e, gaug, vaug, kt, bogf)
 
 
-def unpack_params(parts):
+def unpack_params(place, parts):
     width = HEADS * HD
     taps, bias = pl.pallas_call(
         params_kernel,
         out_shape=[shape_of(TAPS, width, dtype=F32), shape_of(1, width, dtype=F32)],
-        in_specs=[VMEM],
+        in_specs=[SMEM] + [VMEM] * len(parts),
         out_specs=[VMEM] * 2,
+        scratch_shapes=[pltpu.VMEM((HEADS, *parts[0].shape[2:]), F32)],
         compiler_params=params(8),
         name="unpack_params",
-    )(parts)
+    )(place.reshape(1), *parts)
     return taps, bias.reshape(width)
 
 
@@ -450,30 +460,18 @@
     return lax.ppermute(field, axis, [(i, i ^ bit) for i in range(count)])
 
 
-def joined(field, axis, bit):
-    other = swap(field, axis, bit)
-    upper = (lax.axis_index(axis) & bit) != 0
-    first = jnp.where(upper, other, field)
-    second = jnp.where(upper, field, other)
-    return jnp.concatenate([first, second], axis=0)
-
-
-def over_utterances(part):
-    other = swap(part, "seq", 8) + swap(part, "seq", 24)
-    part = part + swap(part, "seq", 16)
-    upper = (lax.axis_index("seq") & 8) != 0
-    return jnp.concatenate([jnp.where(upper, other, part), jnp.where(upper, part, other)], axis=0)
-
-
-def over_devices(part):
+def along_x(field, steps):
+    seq = lax.axis_size("seq")
+    return lax.ppermute(field, "seq", [(i, i // 8 * 8 + (i + 2 * steps) % 8) for i in range(seq)])
+
+
+def reduce_rest(part, place):
     for bit in (4, 8):
         part = part + swap(part, "dp", bit)
-    part = part + swap(part, "dp", 1) + swap(part, "dp", 2) + swap(part, "dp", 3)
-    for bit in (1, 2, 4):
-        part = joined(part, "seq", bit)
-    half = (TAPS + 1) // 2
-    part = part.reshape(HEADS // 2, 2, half, LANES).swapaxes(0, 1)
-    return unpack_params(part.reshape(HEADS, half, LANES))
+    other = swap(part, "seq", 8) + swap(part, "seq", 24)
+    part = jnp.stack([part + swap(part, "seq", 16), other])
+    part = jnp.stack([part, swap(part, "seq", 1)])
+    return unpack_params(place, [part] + [along_x(part, steps) for steps in (1, 2, 3)])
 
 
 def on_device(
@@ -490,11 +488,14 @@
 
     field = exchange(pack(queries, key_vectors, value_vectors, features, cotangent))
     *state, bogf, part = forward(valid, field, taps)
-    part = over_utterances(part)
+    near = swap(part, "dp", 1)
     field = backward(field, *state, bogf)
+    field, part, near = lax.optimization_barrier((field, part, near))
+    part = part + near
+    part = part + swap(part, "dp", 2)
     field, part = lax.optimization_barrier((field, part))
     field = exchange(field)
-    grad_kernel, grad_bias = over_devices(part)
+    grad_kernel, grad_bias = reduce_rest(part, item)
     grad_q, grad_k, grad_v, block_out, grad_features = unpack(field, rows, utts)
     return block_out, grad_features, grad_q, grad_k, grad_v, grad_kernel, grad_bias
 

time: 217 us -> 220 us (1.014)
  waiting for transfers between devices: 104 us -> 107 us
    ppermute x11 -> x8, starting transfers between devices: 45.3 us -> 33.2 us  [swap(): return lax.ppermute(field, axis, [(i, i ^ bit) for i in range(count)])]
    ppermute x0 -> x3, starting transfers between devices: none -> 10.1 us  [along_x(): lax.ppermute(field, 'seq', [(i, i // 8 * 8 + (i + 2 * steps) % 8) for i i...]
    ppermute x0 -> x3, waiting for transfers between devices: none -> 3.1 us  [along_x(): lax.ppermute(field, 'seq', [(i, i // 8 * 8 + (i + 2 * steps) % 8) for i i...]
    ppermute x11 -> x8, waiting for transfers between devices: 40.2 us -> 40.4 us  [swap(): return lax.ppermute(field, axis, [(i, i ^ bit) for i in range(count)])]
  transfers between devices with their start and end apart: 13 -> 13, of which waited for: 9 -> 10; matrix products, arithmetic and copies ran while one was open for 0% -> 0% of each run, Pallas kernels for 5% -> 5%
where the time goes in v5:
time: 220 us; the launch traced here: 216 us
  waiting for transfers between devices  107 us (49%)
  starting transfers between devices  71.7 us (33%)
  Pallas kernels  35.3 us (16%)
    all_to_all x2, waiting for transfers between devices, exchange(): return lax.all_to_all(field, 'seq', split_axis=0, concat_axis=0, tiled=True)  63.4 us
    ppermute x8, waiting for transfers between devices, swap(): return lax.ppermute(field, axis, [(i, i ^ bit) for i in range(count)])  40.4 us
    ppermute x8, starting transfers between devices, swap(): return lax.ppermute(field, axis, [(i, i ^ bit) for i in range(count)])  33.2 us
    all_to_all x2, starting transfers between devices, exchange(): return lax.all_to_all(field, 'seq', split_axis=0, concat_axis=0, tiled=True)  28.4 us
    pallas_call x1, Pallas kernels, forward(): pl.pallas_call(forward_kernel, out_shape=[shape_of(length // QB, length,...  15.2 us
    ppermute x3, starting transfers between devices, along_x(): lax.ppermute(field, 'seq', [(i, i // 8 * 8 + (i + 2 * steps) % 8) for i i...  10.1 us
    pallas_call x1, Pallas kernels, backward(): pl.pallas_call(backward_kernel, out_shape=shape_of(*field.shape), in_spec...  9.76 us
    pallas_call x1, Pallas kernels, pack(): pl.pallas_call(pack_kernel, out_shape=shape_of(utts * HEADS, rows * 5 //...  6.34 us
  transfers between devices with their start and end apart: 13, of which 10 were waited for; matrix products, arithmetic and copies ran while one was open for 0% of the time, Pallas kernels for 5%

profile of v5, /device:TPU:1, one launch (start us, length us, event | category | flops | bytes accessed | tf_op | source)
XLA Modules:
  0.0 215.6 jit_solution(4716097623871072444)
XLA Ops:
  0.6 6.3 %pack.1 = bf16[32,160,128]{2,1,0:T(8,128)(2,1)} custom-call(bf16[64,2,1024]{2,1,0:T(2,128)(2,1)} %q_hbm.1, bf16[64,2,1024]{2,1,0:T(2,128)(2,1)} %k_hbm.1, bf16[64,2,1024]{2,1,0:T(2,128)(2,1)} %v_hbm.1, bf16[64,2,1024]{2,1,0:T(2,128)(2,1)} %f_hbm.1, bf16[64,2,1024]{2,1,0:T(2,128)(2,1)} %c_hbm.1), custom_call_target="tpu_custom_call" | custom-call | tf_op jit(solution)/shard_map/pack/pallas_call | solution.py:364
  7.0 0.0 copy-start.2
  7.0 19.4 %all-to-all-start = ((bf16[32,160,128]{2,1,0:T(8,128)(2,1)}), bf16[32,160,128]{2,1,0:T(8,128)(2,1)S(1)}, u32[]{:S(2)}, u32[]{:S(2)}) async-start(bf16[32,160,128]{2,1,0:T(8,128)(2,1)} %pack.1), calls=%async_computation | async-start | bytes 2621440 | tf_op jit(solution)/shard_map/all_to_all | solution.py:455
  26.4 0.6 fusion.1
  27.1 0.1 fusion
  27.1 0.1 pad_maximum_fusion.1.taps_ref
  27.2 63.4 %all-to-all-done.in_ref = bf16[32,160,128]{2,1,0:T(8,128)(2,1)S(1)} async-done(((bf16[32,160,128]{2,1,0:T(8,128)(2,1)}), bf16[32,160,128]{2,1,0:T(8,128)(2,1)S(1)}, u32[]{:S(2)}, u32[]{:S(2)}) %all-to-all-start) | async-done | bytes 1310752 | tf_op jit(solution)/shard_map/all_to_all | solution.py:455
  90.6 15.2 %forward.1 = (bf16[2,2048,1024]{2,1,0:T(8,128)(2,1)S(1)}, bf16[2048,128]{1,0:T(8,128)(2,1)S(1)}, bf16[2048,128]{1,0:T(8,128)(2,1)S(1)}, bf16[128,2048]{1,0:T(8,1...) custom-call(s32[1]{0:T(128)} %bitcast.frames_ref, bf16[32,160,128]{2,1,0:T(8,128)(2,1)S(1)} %all-to-all-done.in_ref, ...), custom_call_target="tpu_custom_call" | custom-call | flops 8000000000 | bytes 20000000 | tf_op jit(solution)/shard_map/forward/pallas_call | solution.py:392
  105.8 2.9 %collective-permute-start = (f32[16,128]{1,0:T(8,128)S(1)}, f32[16,128]{1,0:T(8,128)S(1)}, u32[]{:S(2)}, u32[]{:S(2)}) collective-permute-start(f32[16,128]{1,0:T(8,128)S(1)} %get-tuple-element.32), channel_id=1, source_target_pairs={{0,1},{1,0},{2,3},{3,2},{4,5},{5,4},{6,7},{7,6},{8,9},{9,8},{10,11... | collective-permute-start | bytes 24584 | tf_op jit(solution)/shard_map/ppermute | solution.py:460
  108.7 9.8 %backward.1 = bf16[32,160,128]{2,1,0:T(8,128)(2,1)} custom-call(bf16[32,160,128]{2,1,0:T(8,128)(2,1)S(1)} %all-to-all-done.in_ref, bf16[2,2048,1024]{2,1,0:T(8,128)(2,1)S(1)} %get-tuple-element.25.e_ref, bf16[2048,128]{1,0:T(8,128)(2,1)S(1)} %get-tuple-element.26.gaug_ref, bf16[2048,128]{1,0:T(8,128)(2,1)S(1)} %get-tuple-element.27.vaug, ...), custom_call_target="tpu_custom_call" | custom-call | flops 8999999488 | bytes 20000000 | tf_op jit(solution)/shard_map/backward/pallas_call | solution.py:426
  118.5 3.3 %collective-permute-start.1 = (f32[16,128]{1,0:T(8,128)S(1)}, f32[16,128]{1,0:T(8,128)S(1)}, u32[]{:S(2)}, u32[]{:S(2)}) collective-permute-start(f32[16,128]{1,0:T(8,128)S(1)} %add.28), channel_id=1, source_target_pairs={{0,2},{1,3},{2,0},{3,1},{4,6},{5,7},{6,4},{7,5},{8,10},{9,11},{10,... | collective-permute-start | bytes 24584 | tf_op jit(solution)/shard_map/ppermute | solution.py:460
  121.8 2.0 collective-permute-done.1
  123.8 9.0 %all-to-all-start.1 = ((bf16[32,160,128]{2,1,0:T(8,128)(2,1)}), bf16[32,160,128]{2,1,0:T(8,128)(2,1)S(1)}, u32[]{:S(2)}, u32[]{:S(2)}) async-start(bf16[32,160,128]{2,1,0:T(8,128)(2,1)} %backward.1), calls=%async_computation.1 | async-start | bytes 2621440 | tf_op jit(solution)/shard_map/all_to_all | solution.py:455
  132.8 3.2 %collective-permute-start.2 = (f32[16,128]{1,0:T(8,128)S(1)}, f32[16,128]{1,0:T(8,128)S(1)}, u32[]{:S(2)}, u32[]{:S(2)}) collective-permute-start(f32[16,128]{1,0:T(8,128)S(1)} %add.29), channel_id=1, source_target_pairs={{0,4},{1,5},{2,6},{3,7},{4,0},{5,1},{6,2},{7,3},{8,12},{9,13},{10,... | collective-permute-start | bytes 24584 | tf_op jit(solution)/shard_map/ppermute | solution.py:460
  136.0 1.5 collective-permute-done.2
  137.5 4.8 %collective-permute-start.3 = (f32[16,128]{1,0:T(8,128)S(1)}, f32[16,128]{1,0:T(8,128)S(1)}, u32[]{:S(2)}, u32[]{:S(2)}) collective-permute-start(f32[16,128]{1,0:T(8,128)S(1)} %add.30), channel_id=1, source_target_pairs={{0,8},{1,9},{2,10},{3,11},{4,12},{5,13},{6,14},{7,15},{8,0},{9,1},... | collective-permute-start | bytes 24584 | tf_op jit(solution)/shard_map/ppermute | solution.py:460
  142.3 1.4 collective-permute-done.3
  143.7 12.0 %collective-permute-start.4 = (f32[16,128]{1,0:T(8,128)S(1)}, f32[16,128]{1,0:T(8,128)S(1)}, u32[]{:S(2)}, u32[]{:S(2)}) collective-permute-start(f32[16,128]{1,0:T(8,128)S(1)} %add.31), channel_id=1, source_target_pairs={{0,256},{16,272},{32,288},{48,304},{64,320},{80,336},{96,352},{112... | collective-permute-start | bytes 24584 | tf_op jit(solution)/shard_map/ppermute | solution.py:460
  155.7 2.2 %collective-permute-start.6 = (f32[16,128]{1,0:T(8,128)S(1)}, f32[16,128]{1,0:T(8,128)S(1)}, u32[]{:S(2)}, u32[]{:S(2)}) collective-permute-start(f32[16,128]{1,0:T(8,128)S(1)} %add.31), channel_id=1, source_target_pairs={{0,384},{16,400},{32,416},{48,432},{64,448},{80,464},{96,480},{112... | collective-permute-start | bytes 24584 | tf_op jit(solution)/shard_map/ppermute | solution.py:460
  157.9 2.0 collective-permute-start.5
  159.9 11.6 %collective-permute-done.4 = f32[16,128]{1,0:T(8,128)S(1)} collective-permute-done((f32[16,128]{1,0:T(8,128)S(1)}, f32[16,128]{1,0:T(8,128)S(1)}, u32[]{:S(2)}, u32[]{:S(2)}) %collective-permute-start.4) | collective-permute-done | bytes 8224 | tf_op jit(solution)/shard_map/ppermute | solution.py:460
  171.5 17.9 %collective-permute-done.6 = f32[16,128]{1,0:T(8,128)S(1)} collective-permute-done((f32[16,128]{1,0:T(8,128)S(1)}, f32[16,128]{1,0:T(8,128)S(1)}, u32[]{:S(2)}, u32[]{:S(2)}) %collective-permute-start.6) | collective-permute-done | bytes 8224 | tf_op jit(solution)/shard_map/ppermute | solution.py:460
  189.4 5.3 %collective-permute-done.5 = f32[16,128]{1,0:T(8,128)S(1)} collective-permute-done((f32[16,128]{1,0:T(8,128)S(1)}, f32[16,128]{1,0:T(8,128)S(1)}, u32[]{:S(2)}, u32[]{:S(2)}) %collective-permute-start.5) | collective-permute-done | bytes 8224 | tf_op jit(solution)/shard_map/ppermute | solution.py:460
  194.7 2.8 %collective-permute-start.7 = (f32[2,16,128]{2,1,0:T(8,128)S(1)}, f32[2,16,128]{2,1,0:T(8,128)S(1)}, u32[]{:S(2)}, u32[]{:S(2)}) collective-permute-start(f32[2,16,128]{2,1,0:T(8,128)S(1)} %get-tuple-element.44), channel_id=1, source_target_pairs={{0,16},{16,0},{32,48},{48,32},{64,80},{80,64},{96,112},{112,96},{1... | collective-permute-start | bytes 49160 | tf_op jit(solution)/shard_map/ppermute | solution.py:460
  197.4 0.8 collective-permute-done.7
  198.3 4.2 %collective-permute-start.10 = (f32[2,2,16,128]{3,2,1,0:T(8,128)S(1)}, f32[2,2,16,128]{3,2,1,0:T(8,128)S(1)}, u32[]{:S(2)}, u32[]{:S(2)}) collective-permute-start(f32[2,2,16,128]{3,2,1,0:T(8,128)S(1)} %pad_maximum_fusion.refs_0_), channel_id=1, source_target_pairs={{0,96},{16,112},{32,0},{48,16},{64,32},{80,48},{96,64},{112,80},{1... | collective-permute-start | bytes 98312 | tf_op jit(solution)/shard_map/ppermute | solution.py:465
  202.5 3.1 %collective-permute-start.9 = (f32[2,2,16,128]{3,2,1,0:T(8,128)S(1)}, f32[2,2,16,128]{3,2,1,0:T(8,128)S(1)}, u32[]{:S(2)}, u32[]{:S(2)}) collective-permute-start(f32[2,2,16,128]{3,2,1,0:T(8,128)S(1)} %pad_maximum_fusion.refs_0_), channel_id=1, source_target_pairs={{0,64},{16,80},{32,96},{48,112},{64,0},{80,16},{96,32},{112,48},{1... | collective-permute-start | bytes 98312 | tf_op jit(solution)/shard_map/ppermute | solution.py:465
  205.7 2.8 %collective-permute-start.8 = (f32[2,2,16,128]{3,2,1,0:T(8,128)S(1)}, f32[2,2,16,128]{3,2,1,0:T(8,128)S(1)}, u32[]{:S(2)}, u32[]{:S(2)}) collective-permute-start(f32[2,2,16,128]{3,2,1,0:T(8,128)S(1)} %pad_maximum_fusion.refs_0_), channel_id=1, source_target_pairs={{0,32},{16,48},{32,64},{48,80},{64,96},{80,112},{96,0},{112,16},{1... | collective-permute-start | bytes 98312 | tf_op jit(solution)/shard_map/ppermute | solution.py:465
  208.4 0.2 collective-permute-done.9.refs_2_
  208.7 2.9 %collective-permute-done.8.refs_1_ = f32[2,2,16,128]{3,2,1,0:T(8,128)S(1)} collective-permute-done((f32[2,2,16,128]{3,2,1,0:T(8,128)S(1)}, f32[2,2,16,128]{3,2,1,0:T(8,128)S(1)}, u32[]{:S(2)}, u32[]{:S(2)}) %collective-permute-start.8) | collective-permute-done | bytes 32800 | tf_op jit(solution)/shard_map/ppermute | solution.py:465
  211.5 0.8 unpack_params.1
  212.3 3.2 %unpack.1 = (bf16[64,2,1024]{2,1,0:T(2,128)(2,1)}, bf16[64,2,1024]{2,1,0:T(2,128)(2,1)}, bf16[64,2,1024]{2,1,0:T(2,128)(2,1)}, bf16[64,2,1024]{2,1,0:T(2,128)(2,1)}, bf16[64,2,1024]{2,1,0:T(2,128)(2,1)}) custom-call(bf16[32,160,128]{2,1,0:T(8,128)(2,1)S(1)} %all-to-all-done.1.in_ref), custom_call_target="tpu_custom_call" | custom-call | tf_op jit(solution)/shard_map/unpack/pallas_call | solution.py:376
  (16 shorter events, 0.1 us)
Async XLA Ops:
  7.0 19.4 %copy-start.2 = (s32[2]{0:T(128)S(1)}, s32[2]{0:T(128)}, u32[]{:S(2)}) copy-start(s32[2]{0:T(128)} %param.13) | copy-start | bytes 28
  7.0 20.1 %copy-start = (f32[31,1024]{1,0:T(8,128)S(1)}, f32[31,1024]{1,0:T(8,128)}, u32[]{:S(2)}) copy-start(f32[31,1024]{1,0:T(8,128)} %param.14) | copy-start | bytes 380932
  7.0 20.1 %copy-start.1 = (f32[1024]{0:T(1024)S(1)}, f32[1024]{0:T(1024)}, u32[]{:S(2)}) copy-start(f32[1024]{0:T(1024)} %param.15) | copy-start | bytes 12292
  7.0 83.6 %all-to-all-start = ((bf16[32,160,128]{2,1,0:T(8,128)(2,1)}), bf16[32,160,128]{2,1,0:T(8,128)(2,1)S(1)}, u32[]{:S(2)}, u32[]{:S(2)}) async-start(bf16[32,160,128]{2,1,0:T(8,128)(2,1)} %pack.1), calls=%async_computation | async-start | bytes 2621440 | tf_op jit(solution)/shard_map/all_to_all | solution.py:455
  105.8 12.7 %collective-permute-start = (f32[16,128]{1,0:T(8,128)S(1)}, f32[16,128]{1,0:T(8,128)S(1)}, u32[]{:S(2)}, u32[]{:S(2)}) collective-permute-start(f32[16,128]{1,0:T(8,128)S(1)} %get-tuple-element.32), channel_id=1, source_target_pairs={{0,1},{1,0},{2,3},{3,2},{4,5},{5,4},{6,7},{7,6},{8,9},{9,8},{10,11... | collective-permute-start | bytes 24584 | tf_op jit(solution)/shard_map/ppermute | solution.py:460
  118.5 5.3 %collective-permute-start.1 = (f32[16,128]{1,0:T(8,128)S(1)}, f32[16,128]{1,0:T(8,128)S(1)}, u32[]{:S(2)}, u32[]{:S(2)}) collective-permute-start(f32[16,128]{1,0:T(8,128)S(1)} %add.28), channel_id=1, source_target_pairs={{0,2},{1,3},{2,0},{3,1},{4,6},{5,7},{6,4},{7,5},{8,10},{9,11},{10,... | collective-permute-start | bytes 24584 | tf_op jit(solution)/shard_map/ppermute | solution.py:460
  123.8 88.6 %all-to-all-start.1 = ((bf16[32,160,128]{2,1,0:T(8,128)(2,1)}), bf16[32,160,128]{2,1,0:T(8,128)(2,1)S(1)}, u32[]{:S(2)}, u32[]{:S(2)}) async-start(bf16[32,160,128]{2,1,0:T(8,128)(2,1)} %backward.1), calls=%async_computation.1 | async-start | bytes 2621440 | tf_op jit(solution)/shard_map/all_to_all | solution.py:455
  132.8 4.7 %collective-permute-start.2 = (f32[16,128]{1,0:T(8,128)S(1)}, f32[16,128]{1,0:T(8,128)S(1)}, u32[]{:S(2)}, u32[]{:S(2)}) collective-permute-start(f32[16,128]{1,0:T(8,128)S(1)} %add.29), channel_id=1, source_target_pairs={{0,4},{1,5},{2,6},{3,7},{4,0},{5,1},{6,2},{7,3},{8,12},{9,13},{10,... | collective-permute-start | bytes 24584 | tf_op jit(solution)/shard_map/ppermute | solution.py:460
  137.5 6.2 %collective-permute-start.3 = (f32[16,128]{1,0:T(8,128)S(1)}, f32[16,128]{1,0:T(8,128)S(1)}, u32[]{:S(2)}, u32[]{:S(2)}) collective-permute-start(f32[16,128]{1,0:T(8,128)S(1)} %add.30), channel_id=1, source_target_pairs={{0,8},{1,9},{2,10},{3,11},{4,12},{5,13},{6,14},{7,15},{8,0},{9,1},... | collective-permute-start | bytes 24584 | tf_op jit(solution)/shard_map/ppermute | solution.py:460
  143.7 27.8 %collective-permute-start.4 = (f32[16,128]{1,0:T(8,128)S(1)}, f32[16,128]{1,0:T(8,128)S(1)}, u32[]{:S(2)}, u32[]{:S(2)}) collective-permute-start(f32[16,128]{1,0:T(8,128)S(1)} %add.31), channel_id=1, source_target_pairs={{0,256},{16,272},{32,288},{48,304},{64,320},{80,336},{96,352},{112... | collective-permute-start | bytes 24584 | tf_op jit(solution)/shard_map/ppermute | solution.py:460
  155.7 33.7 %collective-permute-start.6 = (f32[16,128]{1,0:T(8,128)S(1)}, f32[16,128]{1,0:T(8,128)S(1)}, u32[]{:S(2)}, u32[]{:S(2)}) collective-permute-start(f32[16,128]{1,0:T(8,128)S(1)} %add.31), channel_id=1, source_target_pairs={{0,384},{16,400},{32,416},{48,432},{64,448},{80,464},{96,480},{112... | collective-permute-start | bytes 24584 | tf_op jit(solution)/shard_map/ppermute | solution.py:460
  157.9 36.8 %collective-permute-start.5 = (f32[16,128]{1,0:T(8,128)S(1)}, f32[16,128]{1,0:T(8,128)S(1)}, u32[]{:S(2)}, u32[]{:S(2)}) collective-permute-start(f32[16,128]{1,0:T(8,128)S(1)} %add.31), channel_id=1, source_target_pairs={{0,128},{16,144},{32,160},{48,176},{64,192},{80,208},{96,224},{112... | collective-permute-start | bytes 24584 | tf_op jit(solution)/shard_map/ppermute | solution.py:460
  194.7 3.6 %collective-permute-start.7 = (f32[2,16,128]{2,1,0:T(8,128)S(1)}, f32[2,16,128]{2,1,0:T(8,128)S(1)}, u32[]{:S(2)}, u32[]{:S(2)}) collective-permute-start(f32[2,16,128]{2,1,0:T(8,128)S(1)} %get-tuple-element.44), channel_id=1, source_target_pairs={{0,16},{16,0},{32,48},{48,32},{64,80},{80,64},{96,112},{112,96},{1... | collective-permute-start | bytes 49160 | tf_op jit(solution)/shard_map/ppermute | solution.py:460
  198.3 10.2 %collective-permute-start.10 = (f32[2,2,16,128]{3,2,1,0:T(8,128)S(1)}, f32[2,2,16,128]{3,2,1,0:T(8,128)S(1)}, u32[]{:S(2)}, u32[]{:S(2)}) collective-permute-start(f32[2,2,16,128]{3,2,1,0:T(8,128)S(1)} %pad_maximum_fusion.refs_0_), channel_id=1, source_target_pairs={{0,96},{16,112},{32,0},{48,16},{64,32},{80,48},{96,64},{112,80},{1... | collective-permute-start | bytes 98312 | tf_op jit(solution)/shard_map/ppermute | solution.py:465
  202.5 6.2 %collective-permute-start.9 = (f32[2,2,16,128]{3,2,1,0:T(8,128)S(1)}, f32[2,2,16,128]{3,2,1,0:T(8,128)S(1)}, u32[]{:S(2)}, u32[]{:S(2)}) collective-permute-start(f32[2,2,16,128]{3,2,1,0:T(8,128)S(1)} %pad_maximum_fusion.refs_0_), channel_id=1, source_target_pairs={{0,64},{16,80},{32,96},{48,112},{64,0},{80,16},{96,32},{112,48},{1... | collective-permute-start | bytes 98312 | tf_op jit(solution)/shard_map/ppermute | solution.py:465
  205.7 5.9 %collective-permute-start.8 = (f32[2,2,16,128]{3,2,1,0:T(8,128)S(1)}, f32[2,2,16,128]{3,2,1,0:T(8,128)S(1)}, u32[]{:S(2)}, u32[]{:S(2)}) collective-permute-start(f32[2,2,16,128]{3,2,1,0:T(8,128)S(1)} %pad_maximum_fusion.refs_0_), channel_id=1, source_target_pairs={{0,32},{16,48},{32,64},{48,80},{64,96},{80,112},{96,0},{112,16},{1... | collective-permute-start | bytes 98312 | tf_op jit(solution)/shard_map/ppermute | solution.py:465

commit v6 on v5

--- a/solution.py
+++ b/solution.py
@@ -44,26 +44,30 @@
     copies = [pltpu.make_async_copy(a, b, sems.at[n]) for n, (a, b) in enumerate(pairs)]
     for copy in copies:
         copy.start()
-    rows, utts, _ = q_ref.shape
+    rows, utts, width = q_ref.shape
+
+    def one_head(field, u, h):
+        return field[:, (u * HEADS + h) * HD : (u * HEADS + h + 1) * HD]
 
     def pair(a_ref, b_ref, first):
+        a = a_ref[...].reshape(rows, utts * width)
+        b = b_ref[...].reshape(rows, utts * width)
         for u in range(utts):
-            a = a_ref[:, u, :]
-            b = b_ref[:, u, :]
             for h in range(HEADS):
-                part = slice(h * HD, (h + 1) * HD)
-                out_ref[u * HEADS + h, first : first + rows, :] = lane_pair(a[:, part], b[:, part])
+                out_ref[u * HEADS + h, first : first + rows, :] = lane_pair(
+                    one_head(a, u, h), one_head(b, u, h)
+                )
 
     copies[0].wait()
     copies[1].wait()
     pair(q_ref, k_ref, 0)
     copies[2].wait()
+    values = v_ref[...].reshape(rows, utts * width)
     for u in range(utts):
-        v = v_ref[:, u, :]
         for h in range(HEADS):
-            part = slice(h * HD, (h + 1) * HD)
+            v = one_head(values, u, h)
             out_ref[u * HEADS + h, rows : rows * 3 // 2, :] = lane_pair(
-                v[: rows // 2, part], v[rows // 2 :, part]
+                v[: rows // 2], v[rows // 2 :]
             )
     copies[3].wait()
     copies[4].wait()
@@ -79,8 +83,8 @@
             blocks = [in_ref[u * HEADS + h, first : first + rows, :] for h in range(HEADS)]
             firsts.append(jnp.concatenate([x[:, :HD] for x in blocks], axis=1))
             seconds.append(jnp.concatenate([x[:, HD:] for x in blocks], axis=1))
-        a_ref[...] = jnp.stack(firsts, axis=1)
-        b_ref[...] = jnp.stack(seconds, axis=1)
+        a_ref[...] = jnp.concatenate(firsts, axis=1).reshape(a_ref.shape)
+        b_ref[...] = jnp.concatenate(seconds, axis=1).reshape(b_ref.shape)
 
     pair(f_ref, c_ref, rows * 3 // 2)
     pair(q_ref, k_ref, 0)
@@ -90,7 +94,7 @@
         top = jnp.concatenate([x[:, :HD] for x in blocks], axis=1)
         bottom = jnp.concatenate([x[:, HD:] for x in blocks], axis=1)
         values.append(jnp.concatenate([top, bottom], axis=0))
-    v_ref[...] = jnp.stack(values, axis=1)
+    v_ref[...] = jnp.concatenate(values, axis=1).reshape(v_ref.shape)
 
 
 def attend_forward(valid, in_ref, e_ref, ctx_ref, kaug, vaug, vt, kt, scores):
@@ -333,16 +337,14 @@
     )
 
 
-def params_kernel(place_ref, *refs):
-    *parts, taps_ref, bias_ref, heads = refs
+def params_kernel(place_ref, same_ref, other_ref, taps_ref, bias_ref, heads):
     place = place_ref[0]
-    core, x, half = place % 2, place // 2 % len(parts), place // 8 % 2
-    for i, part in enumerate(parts):
-        for j in range(part.shape[0]):
-            for n in range(part.shape[1]):
-                other = (x + len(parts) - i) % len(parts)
-                head = (half + n) % 2 * 8 + other * 2 + (core + j) % 2
-                heads[head] = part[j, n]
+    core, x, half = place % 2, place // 2 % 4, place // 8 % 2
+    for n, part in enumerate((same_ref, other_ref)):
+        for i in range(part.shape[0]):
+            for j in range(part.shape[1]):
+                head = (half + n) % 2 * 8 + (x + 4 - i) % 4 * 2 + (core + j) % 2
+                heads[head] = part[i, j]
     rows = heads.shape[1]
     for h in range(0, HEADS, 2):
         lanes = slice(h * HD, (h + 2) * HD)
@@ -468,10 +470,12 @@
 def reduce_rest(part, place):
     for bit in (4, 8):
         part = part + swap(part, "dp", bit)
-    other = swap(part, "seq", 8) + swap(part, "seq", 24)
-    part = jnp.stack([part + swap(part, "seq", 16), other])
     part = jnp.stack([part, swap(part, "seq", 1)])
-    return unpack_params(place, [part] + [along_x(part, steps) for steps in (1, 2, 3)])
+    part = jnp.stack([part] + [along_x(part, steps) for steps in (1, 2, 3)]).astype(BF16)
+    wide = part.astype(F32)
+    same = wide + swap(part, "seq", 16).astype(F32)
+    other = swap(part, "seq", 8).astype(F32) + swap(part, "seq", 24).astype(F32)
+    return unpack_params(place, [same, other])
 
 
 def on_device(

time: 220 us -> 202 us (0.918)
  waiting for transfers between devices: 107 us -> 93.2 us
  Pallas kernels: 35.3 us -> 29.9 us
  starting transfers between devices: 71.7 us -> 74 us
    ppermute x8, waiting for transfers between devices: 40.4 us -> 28.4 us  [swap(): return lax.ppermute(field, axis, [(i, i ^ bit) for i in range(count)])]
    pallas_call x1, Pallas kernels: 6.34 us -> 2.8 us  [pack(): pl.pallas_call(pack_kernel, out_shape=shape_of(utts * HEADS, rows * 5 //...]
    ppermute x3, waiting for transfers between devices: 3.1 us -> 0.76 us  [along_x(): lax.ppermute(field, 'seq', [(i, i // 8 * 8 + (i + 2 * steps) % 8) for i i...]
  transfers between devices with their start and end apart: 13 -> 13, of which waited for: 10 -> 9; matrix products, arithmetic and copies ran while one was open for 0% -> 0% of each run, Pallas kernels for 5% -> 5%
where the time goes in v6:
time: 202 us; the launch traced here: 199 us
  waiting for transfers between devices  93.2 us (46%)
  starting transfers between devices  74 us (37%)
  Pallas kernels  29.9 us (15%)
    all_to_all x2, waiting for transfers between devices, exchange(): return lax.all_to_all(field, 'seq', split_axis=0, concat_axis=0, tiled=True)  64 us
    ppermute x8, starting transfers between devices, swap(): return lax.ppermute(field, axis, [(i, i ^ bit) for i in range(count)])  34.2 us
    ppermute x8, waiting for transfers between devices, swap(): return lax.ppermute(field, axis, [(i, i ^ bit) for i in range(count)])  28.4 us
    all_to_all x2, starting transfers between devices, exchange(): return lax.all_to_all(field, 'seq', split_axis=0, concat_axis=0, tiled=True)  28.4 us
    pallas_call x1, Pallas kernels, forward(): pl.pallas_call(forward_kernel, out_shape=[shape_of(length // QB, length,...  15.2 us
    ppermute x3, starting transfers between devices, along_x(): lax.ppermute(field, 'seq', [(i, i // 8 * 8 + (i + 2 * steps) % 8) for i i...  11.4 us
    pallas_call x1, Pallas kernels, backward(): pl.pallas_call(backward_kernel, out_shape=shape_of(*field.shape), in_spec...  9.77 us
  transfers between devices with their start and end apart: 13, of which 9 were waited for; matrix products, arithmetic and copies ran while one was open for 0% of the time, Pallas kernels for 5%

profile of v6, /device:TPU:1, one launch (start us, length us, event | category | flops | bytes accessed | tf_op | source)
XLA Modules:
  0.0 198.9 jit_solution(3006515447348671610)
XLA Ops:
  0.6 2.8 %pack.1 = bf16[32,160,128]{2,1,0:T(8,128)(2,1)} custom-call(bf16[64,2,1024]{2,1,0:T(2,128)(2,1)} %q_hbm.1, bf16[64,2,1024]{2,1,0:T(2,128)(2,1)} %k_hbm.1, bf16[64,2,1024]{2,1,0:T(2,128)(2,1)} %v_hbm.1, bf16[64,2,1024]{2,1,0:T(2,128)(2,1)} %f_hbm.1, bf16[64,2,1024]{2,1,0:T(2,128)(2,1)} %c_hbm.1), custom_call_target="tpu_custom_call" | custom-call | tf_op jit(solution)/shard_map/pack/pallas_call | solution.py:366
  3.4 0.0 copy-start.2
  3.5 0.0 copy-start
  3.5 19.4 %all-to-all-start = ((bf16[32,160,128]{2,1,0:T(8,128)(2,1)}), bf16[32,160,128]{2,1,0:T(8,128)(2,1)S(1)}, u32[]{:S(2)}, u32[]{:S(2)}) async-start(bf16[32,160,128]{2,1,0:T(8,128)(2,1)} %pack.1), calls=%async_computation | async-start | bytes 2621440 | tf_op jit(solution)/shard_map/all_to_all | solution.py:457
  22.9 0.6 fusion.1
  23.5 0.1 fusion
  23.6 0.1 pad_maximum_fusion.1.taps_ref
  23.7 63.4 %all-to-all-done.in_ref = bf16[32,160,128]{2,1,0:T(8,128)(2,1)S(1)} async-done(((bf16[32,160,128]{2,1,0:T(8,128)(2,1)}), bf16[32,160,128]{2,1,0:T(8,128)(2,1)S(1)}, u32[]{:S(2)}, u32[]{:S(2)}) %all-to-all-start) | async-done | bytes 1310752 | tf_op jit(solution)/shard_map/all_to_all | solution.py:457
  87.0 15.2 %forward.1 = (bf16[2,2048,1024]{2,1,0:T(8,128)(2,1)S(1)}, bf16[2048,128]{1,0:T(8,128)(2,1)S(1)}, bf16[2048,128]{1,0:T(8,128)(2,1)S(1)}, bf16[128,2048]{1,0:T(8,1...) custom-call(s32[1]{0:T(128)} %bitcast.frames_ref, bf16[32,160,128]{2,1,0:T(8,128)(2,1)S(1)} %all-to-all-done.in_ref, ...), custom_call_target="tpu_custom_call" | custom-call | flops 8000000000 | bytes 20000000 | tf_op jit(solution)/shard_map/forward/pallas_call | solution.py:394
  102.2 3.1 %collective-permute-start = (f32[16,128]{1,0:T(8,128)S(1)}, f32[16,128]{1,0:T(8,128)S(1)}, u32[]{:S(2)}, u32[]{:S(2)}) collective-permute-start(f32[16,128]{1,0:T(8,128)S(1)} %get-tuple-element.32), channel_id=1, source_target_pairs={{0,1},{1,0},{2,3},{3,2},{4,5},{5,4},{6,7},{7,6},{8,9},{9,8},{10,11... | collective-permute-start | bytes 24584 | tf_op jit(solution)/shard_map/ppermute | solution.py:462
  105.3 9.8 %backward.1 = bf16[32,160,128]{2,1,0:T(8,128)(2,1)} custom-call(bf16[32,160,128]{2,1,0:T(8,128)(2,1)S(1)} %all-to-all-done.in_ref, bf16[2,2048,1024]{2,1,0:T(8,128)(2,1)S(1)} %get-tuple-element.25.e_ref, bf16[2048,128]{1,0:T(8,128)(2,1)S(1)} %get-tuple-element.26.gaug_ref, bf16[2048,128]{1,0:T(8,128)(2,1)S(1)} %get-tuple-element.27.vaug, ...), custom_call_target="tpu_custom_call" | custom-call | flops 8999999488 | bytes 20000000 | tf_op jit(solution)/shard_map/backward/pallas_call | solution.py:428
  115.1 3.1 %collective-permute-start.1 = (f32[16,128]{1,0:T(8,128)S(1)}, f32[16,128]{1,0:T(8,128)S(1)}, u32[]{:S(2)}, u32[]{:S(2)}) collective-permute-start(f32[16,128]{1,0:T(8,128)S(1)} %add.28), channel_id=1, source_target_pairs={{0,2},{1,3},{2,0},{3,1},{4,6},{5,7},{6,4},{7,5},{8,10},{9,11},{10,... | collective-permute-start | bytes 24584 | tf_op jit(solution)/shard_map/ppermute | solution.py:462
  118.2 2.2 %collective-permute-done.1 = f32[16,128]{1,0:T(8,128)S(1)} collective-permute-done((f32[16,128]{1,0:T(8,128)S(1)}, f32[16,128]{1,0:T(8,128)S(1)}, u32[]{:S(2)}, u32[]{:S(2)}) %collective-permute-start.1) | collective-permute-done | bytes 8224 | tf_op jit(solution)/shard_map/ppermute | solution.py:462
  120.4 9.0 %all-to-all-start.1 = ((bf16[32,160,128]{2,1,0:T(8,128)(2,1)}), bf16[32,160,128]{2,1,0:T(8,128)(2,1)S(1)}, u32[]{:S(2)}, u32[]{:S(2)}) async-start(bf16[32,160,128]{2,1,0:T(8,128)(2,1)} %backward.1), calls=%async_computation.1 | async-start | bytes 2621440 | tf_op jit(solution)/shard_map/all_to_all | solution.py:457
  129.4 3.2 %collective-permute-start.2 = (f32[16,128]{1,0:T(8,128)S(1)}, f32[16,128]{1,0:T(8,128)S(1)}, u32[]{:S(2)}, u32[]{:S(2)}) collective-permute-start(f32[16,128]{1,0:T(8,128)S(1)} %add.29), channel_id=1, source_target_pairs={{0,4},{1,5},{2,6},{3,7},{4,0},{5,1},{6,2},{7,3},{8,12},{9,13},{10,... | collective-permute-start | bytes 24584 | tf_op jit(solution)/shard_map/ppermute | solution.py:462
  132.7 1.5 collective-permute-done.2
  134.1 4.8 %collective-permute-start.3 = (f32[16,128]{1,0:T(8,128)S(1)}, f32[16,128]{1,0:T(8,128)S(1)}, u32[]{:S(2)}, u32[]{:S(2)}) collective-permute-start(f32[16,128]{1,0:T(8,128)S(1)} %add.30), channel_id=1, source_target_pairs={{0,8},{1,9},{2,10},{3,11},{4,12},{5,13},{6,14},{7,15},{8,0},{9,1},... | collective-permute-start | bytes 24584 | tf_op jit(solution)/shard_map/ppermute | solution.py:462
  139.0 1.4 collective-permute-done.3
  140.3 3.8 %collective-permute-start.4 = (bf16[16,128]{1,0:T(8,128)(2,1)S(1)}, bf16[16,128]{1,0:T(8,128)(2,1)S(1)}, u32[]{:S(2)}, u32[]{:S(2)}) collective-permute-start(bf16[16,128]{1,0:T(8,128)(2,1)S(1)} %add.31), channel_id=1, source_target_pairs={{0,16},{16,0},{32,48},{48,32},{64,80},{80,64},{96,112},{112,96},{1... | collective-permute-start | bytes 12296 | tf_op jit(solution)/shard_map/ppermute | solution.py:462
  144.2 0.8 collective-permute-done.4
  145.0 4.9 %collective-permute-start.6 = (bf16[2,16,128]{2,1,0:T(8,128)(2,1)S(1)}, bf16[2,16,128]{2,1,0:T(8,128)(2,1)S(1)}, u32[]{:S(2)}, u32[]{:S(2)}) collective-permute-start(bf16[2,16,128]{2,1,0:T(8,128)(2,1)S(1)} %get-tuple-element.44), channel_id=1, source_target_pairs={{0,64},{16,80},{32,96},{48,112},{64,0},{80,16},{96,32},{112,48},{1... | collective-permute-start | bytes 24584 | tf_op jit(solution)/shard_map/ppermute | solution.py:467
  149.9 2.2 %collective-permute-start.5 = (bf16[2,16,128]{2,1,0:T(8,128)(2,1)S(1)}, bf16[2,16,128]{2,1,0:T(8,128)(2,1)S(1)}, u32[]{:S(2)}, u32[]{:S(2)}) collective-permute-start(bf16[2,16,128]{2,1,0:T(8,128)(2,1)S(1)} %get-tuple-element.44), channel_id=1, source_target_pairs={{0,32},{16,48},{32,64},{48,80},{64,96},{80,112},{96,0},{112,16},{1... | collective-permute-start | bytes 24584 | tf_op jit(solution)/shard_map/ppermute | solution.py:467
  152.1 4.3 %collective-permute-start.7 = (bf16[2,16,128]{2,1,0:T(8,128)(2,1)S(1)}, bf16[2,16,128]{2,1,0:T(8,128)(2,1)S(1)}, u32[]{:S(2)}, u32[]{:S(2)}) collective-permute-start(bf16[2,16,128]{2,1,0:T(8,128)(2,1)S(1)} %get-tuple-element.44), channel_id=1, source_target_pairs={{0,96},{16,112},{32,0},{48,16},{64,32},{80,48},{96,64},{112,80},{1... | collective-permute-start | bytes 24584 | tf_op jit(solution)/shard_map/ppermute | solution.py:467
  156.4 0.8 collective-permute-done.7
  157.2 11.8 %collective-permute-start.8 = (bf16[4,2,16,128]{3,2,1,0:T(8,128)(2,1)S(1)}, bf16[4,2,16,128]{3,2,1,0:T(8,128)(2,1)S(1)}, u32[]{:S(2)}, u32[]{:S(2)}) collective-permute-start(bf16[4,2,16,128]{3,2,1,0:T(8,128)(2,1)S(1)} %pad_maximum_fusion), channel_id=1, source_target_pairs={{0,256},{16,272},{32,288},{48,304},{64,320},{80,336},{96,352},{112... | collective-permute-start | bytes 98312 | tf_op jit(solution)/shard_map/ppermute | solution.py:462
  169.0 2.2 %collective-permute-start.9 = (bf16[4,2,16,128]{3,2,1,0:T(8,128)(2,1)S(1)}, bf16[4,2,16,128]{3,2,1,0:T(8,128)(2,1)S(1)}, u32[]{:S(2)}, u32[]{:S(2)}) collective-permute-start(bf16[4,2,16,128]{3,2,1,0:T(8,128)(2,1)S(1)} %pad_maximum_fusion), channel_id=1, source_target_pairs={{0,128},{16,144},{32,160},{48,176},{64,192},{80,208},{96,224},{112... | collective-permute-start | bytes 98312 | tf_op jit(solution)/shard_map/ppermute | solution.py:462
  171.3 2.1 %collective-permute-start.10 = (bf16[4,2,16,128]{3,2,1,0:T(8,128)(2,1)S(1)}, bf16[4,2,16,128]{3,2,1,0:T(8,128)(2,1)S(1)}, u32[]{:S(2)}, u32[]{:S(2)}) collective-permute-start(bf16[4,2,16,128]{3,2,1,0:T(8,128)(2,1)S(1)} %pad_maximum_fusion), channel_id=1, source_target_pairs={{0,384},{16,400},{32,416},{48,432},{64,448},{80,464},{96,480},{112... | collective-permute-start | bytes 98312 | tf_op jit(solution)/shard_map/ppermute | solution.py:462
  173.4 19.2 %collective-permute-done.8 = bf16[4,2,16,128]{3,2,1,0:T(8,128)(2,1)S(1)} collective-permute-done((bf16[4,2,16,128]{3,2,1,0:T(8,128)(2,1)S(1)}, bf16[4,2,16,128]{3,2,1,0:T(8,128)(2,1)S(1)}, u32[]{:S(2)}, u32[]{:S(2)}) %collective-permute-start.8) | collective-permute-done | bytes 32800 | tf_op jit(solution)/shard_map/ppermute | solution.py:462
  192.6 3.4 %collective-permute-done.9 = bf16[4,2,16,128]{3,2,1,0:T(8,128)(2,1)S(1)} collective-permute-done((bf16[4,2,16,128]{3,2,1,0:T(8,128)(2,1)S(1)}, bf16[4,2,16,128]{3,2,1,0:T(8,128)(2,1)S(1)}, u32[]{:S(2)}, u32[]{:S(2)}) %collective-permute-start.9) | collective-permute-done | bytes 32800 | tf_op jit(solution)/shard_map/ppermute | solution.py:462
  196.0 0.8 unpack_params.1
  196.8 0.7 all-to-all-done.1.in_ref
  197.5 1.3 unpack.1
  (16 shorter events, 0.1 us)
Async XLA Ops:
  3.4 19.4 %copy-start.2 = (s32[2]{0:T(128)S(1)}, s32[2]{0:T(128)}, u32[]{:S(2)}) copy-start(s32[2]{0:T(128)} %param.13) | copy-start | bytes 28
  3.5 20.1 %copy-start = (f32[31,1024]{1,0:T(8,128)S(1)}, f32[31,1024]{1,0:T(8,128)}, u32[]{:S(2)}) copy-start(f32[31,1024]{1,0:T(8,128)} %param.14) | copy-start | bytes 380932
  3.5 20.0 %copy-start.1 = (f32[1024]{0:T(1024)S(1)}, f32[1024]{0:T(1024)}, u32[]{:S(2)}) copy-start(f32[1024]{0:T(1024)} %param.15) | copy-start | bytes 12292
  3.5 83.6 %all-to-all-start = ((bf16[32,160,128]{2,1,0:T(8,128)(2,1)}), bf16[32,160,128]{2,1,0:T(8,128)(2,1)S(1)}, u32[]{:S(2)}, u32[]{:S(2)}) async-start(bf16[32,160,128]{2,1,0:T(8,128)(2,1)} %pack.1), calls=%async_computation | async-start | bytes 2621440 | tf_op jit(solution)/shard_map/all_to_all | solution.py:457
  102.2 12.9 %collective-permute-start = (f32[16,128]{1,0:T(8,128)S(1)}, f32[16,128]{1,0:T(8,128)S(1)}, u32[]{:S(2)}, u32[]{:S(2)}) collective-permute-start(f32[16,128]{1,0:T(8,128)S(1)} %get-tuple-element.32), channel_id=1, source_target_pairs={{0,1},{1,0},{2,3},{3,2},{4,5},{5,4},{6,7},{7,6},{8,9},{9,8},{10,11... | collective-permute-start | bytes 24584 | tf_op jit(solution)/shard_map/ppermute | solution.py:462
  115.1 5.3 %collective-permute-start.1 = (f32[16,128]{1,0:T(8,128)S(1)}, f32[16,128]{1,0:T(8,128)S(1)}, u32[]{:S(2)}, u32[]{:S(2)}) collective-permute-start(f32[16,128]{1,0:T(8,128)S(1)} %add.28), channel_id=1, source_target_pairs={{0,2},{1,3},{2,0},{3,1},{4,6},{5,7},{6,4},{7,5},{8,10},{9,11},{10,... | collective-permute-start | bytes 24584 | tf_op jit(solution)/shard_map/ppermute | solution.py:462
  120.4 77.1 %all-to-all-start.1 = ((bf16[32,160,128]{2,1,0:T(8,128)(2,1)}), bf16[32,160,128]{2,1,0:T(8,128)(2,1)S(1)}, u32[]{:S(2)}, u32[]{:S(2)}) async-start(bf16[32,160,128]{2,1,0:T(8,128)(2,1)} %backward.1), calls=%async_computation.1 | async-start | bytes 2621440 | tf_op jit(solution)/shard_map/all_to_all | solution.py:457
  129.4 4.7 %collective-permute-start.2 = (f32[16,128]{1,0:T(8,128)S(1)}, f32[16,128]{1,0:T(8,128)S(1)}, u32[]{:S(2)}, u32[]{:S(2)}) collective-permute-start(f32[16,128]{1,0:T(8,128)S(1)} %add.29), channel_id=1, source_target_pairs={{0,4},{1,5},{2,6},{3,7},{4,0},{5,1},{6,2},{7,3},{8,12},{9,13},{10,... | collective-permute-start | bytes 24584 | tf_op jit(solution)/shard_map/ppermute | solution.py:462
  134.1 6.2 %collective-permute-start.3 = (f32[16,128]{1,0:T(8,128)S(1)}, f32[16,128]{1,0:T(8,128)S(1)}, u32[]{:S(2)}, u32[]{:S(2)}) collective-permute-start(f32[16,128]{1,0:T(8,128)S(1)} %add.30), channel_id=1, source_target_pairs={{0,8},{1,9},{2,10},{3,11},{4,12},{5,13},{6,14},{7,15},{8,0},{9,1},... | collective-permute-start | bytes 24584 | tf_op jit(solution)/shard_map/ppermute | solution.py:462
  140.3 4.7 %collective-permute-start.4 = (bf16[16,128]{1,0:T(8,128)(2,1)S(1)}, bf16[16,128]{1,0:T(8,128)(2,1)S(1)}, u32[]{:S(2)}, u32[]{:S(2)}) collective-permute-start(bf16[16,128]{1,0:T(8,128)(2,1)S(1)} %add.31), channel_id=1, source_target_pairs={{0,16},{16,0},{32,48},{48,32},{64,80},{80,64},{96,112},{112,96},{1... | collective-permute-start | bytes 12296 | tf_op jit(solution)/shard_map/ppermute | solution.py:462
  145.0 11.4 %collective-permute-start.6 = (bf16[2,16,128]{2,1,0:T(8,128)(2,1)S(1)}, bf16[2,16,128]{2,1,0:T(8,128)(2,1)S(1)}, u32[]{:S(2)}, u32[]{:S(2)}) collective-permute-start(bf16[2,16,128]{2,1,0:T(8,128)(2,1)S(1)} %get-tuple-element.44), channel_id=1, source_target_pairs={{0,64},{16,80},{32,96},{48,112},{64,0},{80,16},{96,32},{112,48},{1... | collective-permute-start | bytes 24584 | tf_op jit(solution)/shard_map/ppermute | solution.py:467
  149.9 6.5 %collective-permute-start.5 = (bf16[2,16,128]{2,1,0:T(8,128)(2,1)S(1)}, bf16[2,16,128]{2,1,0:T(8,128)(2,1)S(1)}, u32[]{:S(2)}, u32[]{:S(2)}) collective-permute-start(bf16[2,16,128]{2,1,0:T(8,128)(2,1)S(1)} %get-tuple-element.44), channel_id=1, source_target_pairs={{0,32},{16,48},{32,64},{48,80},{64,96},{80,112},{96,0},{112,16},{1... | collective-permute-start | bytes 24584 | tf_op jit(solution)/shard_map/ppermute | solution.py:467
  152.1 5.1 %collective-permute-start.7 = (bf16[2,16,128]{2,1,0:T(8,128)(2,1)S(1)}, bf16[2,16,128]{2,1,0:T(8,128)(2,1)S(1)}, u32[]{:S(2)}, u32[]{:S(2)}) collective-permute-start(bf16[2,16,128]{2,1,0:T(8,128)(2,1)S(1)} %get-tuple-element.44), channel_id=1, source_target_pairs={{0,96},{16,112},{32,0},{48,16},{64,32},{80,48},{96,64},{112,80},{1... | collective-permute-start | bytes 24584 | tf_op jit(solution)/shard_map/ppermute | solution.py:467
  157.2 35.4 %collective-permute-start.8 = (bf16[4,2,16,128]{3,2,1,0:T(8,128)(2,1)S(1)}, bf16[4,2,16,128]{3,2,1,0:T(8,128)(2,1)S(1)}, u32[]{:S(2)}, u32[]{:S(2)}) collective-permute-start(bf16[4,2,16,128]{3,2,1,0:T(8,128)(2,1)S(1)} %pad_maximum_fusion), channel_id=1, source_target_pairs={{0,256},{16,272},{32,288},{48,304},{64,320},{80,336},{96,352},{112... | collective-permute-start | bytes 98312 | tf_op jit(solution)/shard_map/ppermute | solution.py:462
  169.0 27.0 %collective-permute-start.9 = (bf16[4,2,16,128]{3,2,1,0:T(8,128)(2,1)S(1)}, bf16[4,2,16,128]{3,2,1,0:T(8,128)(2,1)S(1)}, u32[]{:S(2)}, u32[]{:S(2)}) collective-permute-start(bf16[4,2,16,128]{3,2,1,0:T(8,128)(2,1)S(1)} %pad_maximum_fusion), channel_id=1, source_target_pairs={{0,128},{16,144},{32,160},{48,176},{64,192},{80,208},{96,224},{112... | collective-permute-start | bytes 98312 | tf_op jit(solution)/shard_map/ppermute | solution.py:462
  171.3 24.8 %collective-permute-start.10 = (bf16[4,2,16,128]{3,2,1,0:T(8,128)(2,1)S(1)}, bf16[4,2,16,128]{3,2,1,0:T(8,128)(2,1)S(1)}, u32[]{:S(2)}, u32[]{:S(2)}) collective-permute-start(bf16[4,2,16,128]{3,2,1,0:T(8,128)(2,1)S(1)} %pad_maximum_fusion), channel_id=1, source_target_pairs={{0,384},{16,400},{32,416},{48,432},{64,448},{80,464},{96,480},{112... | collective-permute-start | bytes 98312 | tf_op jit(solution)/shard_map/ppermute | solution.py:462

commit v7 on v6

--- a/solution.py
+++ b/solution.py
@@ -14,6 +14,7 @@
 PAD = 16
 QB = 1024
 KC = 256
+CONV_ROWS = 256
 F32 = jnp.float32
 BF16 = jnp.bfloat16
 NEG = -1e30
@@ -168,16 +169,14 @@
     finish(blocks - 1, total)
 
 
-def convolve(
-    valid, in_ref, ctx_ref, taps_ref, out_ref, part_ref, gaug_ref, field, grad, hid, cot, bo, sums_ref
-):
+def convolve(valid, in_ref, ctx_ref, taps_ref, part_ref, field, grad, hid, cot, bo, sums_ref):
     sources = in_ref.shape[0]
     rows = in_ref.shape[1] * 2 // 5
     first = rows * 3 // 2
     length = sources * rows
     half = length // 2
     mid = sources // 2
-    step = 64
+    step = CONV_ROWS
     steps = half // step
     lane = lane_ids((half, LANES))
     fc_low = in_ref[:mid, first:, :].reshape(half, LANES).astype(F32)
@@ -221,6 +220,15 @@
     part_ref[...] = jnp.where(part_lane < HD, folded[:taps_half], folded[taps_half:])
     grad[:PAD, :] = jnp.where(small < HD, 0.0, swap_halves(grad[half : half + PAD, :]))
     grad[PAD + half :, :] = jnp.where(small < HD, swap_halves(grad[PAD : 2 * PAD, :]), 0.0)
+
+
+def conv_backward_kernel(frames_ref, grad, cot, bo, ctx_ref, taps_ref, out_ref, gaug_ref):
+    valid = frames_ref[0]
+    sources, rows, _ = out_ref.shape
+    half = cot.shape[0]
+    mid = sources // 2
+    step = CONV_ROWS
+    steps = half // step
     lane_step = lane_ids((step, LANES))
     rows_step = lax.broadcasted_iota(jnp.int32, (step, LANES), 0)
     place = rows_step + jnp.where(lane_step < HD, 0, half)
@@ -314,27 +322,23 @@
     in_ref,
     taps_ref,
     e_ref,
-    gaug_ref,
     vaug,
     kt,
-    bogf_ref,
+    ctx_ref,
+    grad,
+    cot,
+    bo,
     part_ref,
     scores,
-    ctx_ref,
     kaug,
     vt,
     field,
-    grad,
     hid,
-    cot,
-    bo,
     sums_ref,
 ):
     valid = frames_ref[0]
     attend_forward(valid, in_ref, e_ref, ctx_ref, kaug, vaug, vt, kt, scores)
-    convolve(
-        valid, in_ref, ctx_ref, taps_ref, bogf_ref, part_ref, gaug_ref, field, grad, hid, cot, bo, sums_ref
-    )
+    convolve(valid, in_ref, ctx_ref, taps_ref, part_ref, field, grad, hid, cot, bo, sums_ref)
 
 
 def params_kernel(place_ref, same_ref, other_ref, taps_ref, bias_ref, heads):
@@ -396,22 +400,20 @@
         out_shape=[
             shape_of(length // QB, length, QB),
             shape_of(*wide),
-            shape_of(*wide),
             shape_of(LANES, length),
-            shape_of(sources, rows, LANES),
+            shape_of(*wide, dtype=F32),
+            shape_of(half + 2 * PAD, LANES, dtype=F32),
+            shape_of(half, LANES, dtype=F32),
+            shape_of(half, LANES, dtype=F32),
             shape_of((TAPS + 1) // 2, LANES, dtype=F32),
         ],
         in_specs=[SMEM, VMEM, VMEM],
-        out_specs=[VMEM] * 6,
+        out_specs=[VMEM] * 8,
         scratch_shapes=[
             pltpu.VMEM((2, length, QB), F32),
-            pltpu.VMEM(wide, F32),
             pltpu.VMEM(wide, BF16),
             pltpu.VMEM((LANES, length), BF16),
             pltpu.VMEM((half + 2 * PAD, LANES), F32),
-            pltpu.VMEM((half + 2 * PAD, LANES), F32),
-            pltpu.VMEM((half, LANES), F32),
-            pltpu.VMEM((half, LANES), F32),
             pltpu.VMEM((half, LANES), F32),
             pltpu.VMEM((8 * (TAPS + 1), LANES), F32),
         ],
@@ -421,6 +423,21 @@
         ),
         name="forward",
     )(frames, field, taps)
+
+
+def conv_backward(frames, grad, cot, bo, ctx, taps, sources):
+    length = ctx.shape[0]
+    return pl.pallas_call(
+        conv_backward_kernel,
+        out_shape=[shape_of(sources, length // sources, LANES), shape_of(length, LANES)],
+        in_specs=[SMEM] + [VMEM] * 5,
+        out_specs=[VMEM] * 2,
+        compiler_params=params(24),
+        cost_estimate=pl.CostEstimate(
+            flops=2_000_000_000, bytes_accessed=4_000_000, transcendentals=0
+        ),
+        name="conv_backward",
+    )(frames, grad, cot, bo, ctx, taps)
 
 
 def backward(field, e, gaug, vaug, kt, bogf):
@@ -491,13 +508,15 @@
     taps = jnp.concatenate([taps, taps], axis=1)
 
     field = exchange(pack(queries, key_vectors, value_vectors, features, cotangent))
-    *state, bogf, part = forward(valid, field, taps)
+    e, vaug, kt, ctx, grad, cot, bo, part = forward(valid, field, taps)
     near = swap(part, "dp", 1)
-    field = backward(field, *state, bogf)
+    bogf, gaug = conv_backward(valid, grad, cot, bo, ctx, taps, field.shape[0])
+    gaug, part, near = lax.optimization_barrier((gaug, part, near))
+    part = part + near
+    near = swap(part, "dp", 2)
+    field = backward(field, e, gaug, vaug, kt, bogf)
     field, part, near = lax.optimization_barrier((field, part, near))
     part = part + near
-    part = part + swap(part, "dp", 2)
-    field, part = lax.optimization_barrier((field, part))
     field = exchange(field)
     grad_kernel, grad_bias = reduce_rest(part, item)
     grad_q, grad_k, grad_v, block_out, grad_features = unpack(field, rows, utts)

time: 202 us -> 200 us (0.990); the launches traced: 199 us -> 200 us
  waiting for transfers between devices: 93.2 us -> 98.4 us
  starting transfers between devices: 74 us -> 70.8 us
    pallas_call x1, Pallas kernels: 15.2 us -> 11 us  [forward(): pl.pallas_call(forward_kernel, out_shape=[shape_of(length // QB, length,...]
    pallas_call x0 -> x1, Pallas kernels: none -> 3.3 us  [conv_backward(): pl.pallas_call(conv_backward_kernel, out_shape=[shape_of(sources, length...]
    ppermute x8, waiting for transfers between devices: 28.4 us -> 31.6 us  [swap(): return lax.ppermute(field, axis, [(i, i ^ bit) for i in range(count)])]
    ppermute x3, waiting for transfers between devices: 0.76 us -> 3.4 us  [along_x(): lax.ppermute(field, 'seq', [(i, i // 8 * 8 + (i + 2 * steps) % 8) for i i...]
  transfers between devices with their start and end apart: 13 -> 13, of which waited for: 9 -> 8; matrix products, arithmetic and copies ran while one was open for 0% -> 0% of each run, Pallas kernels for 5% -> 7%
where the time goes in v7:
time: 200 us
  waiting for transfers between devices  98.4 us (49%)
  starting transfers between devices  70.8 us (35%)
  Pallas kernels  28.9 us (14%)
    all_to_all x2, waiting for transfers between devices, exchange(): return lax.all_to_all(field, 'seq', split_axis=0, concat_axis=0, tiled=True)  63.4 us
    ppermute x8, starting transfers between devices, swap(): return lax.ppermute(field, axis, [(i, i ^ bit) for i in range(count)])  34.2 us
    ppermute x8, waiting for transfers between devices, swap(): return lax.ppermute(field, axis, [(i, i ^ bit) for i in range(count)])  31.6 us
    all_to_all x2, starting transfers between devices, exchange(): return lax.all_to_all(field, 'seq', split_axis=0, concat_axis=0, tiled=True)  27 us
    pallas_call x1, Pallas kernels, forward(): pl.pallas_call(forward_kernel, out_shape=[shape_of(length // QB, length,...  11 us
    pallas_call x1, Pallas kernels, backward(): pl.pallas_call(backward_kernel, out_shape=shape_of(*field.shape), in_spec...  9.64 us
    ppermute x3, starting transfers between devices, along_x(): lax.ppermute(field, 'seq', [(i, i // 8 * 8 + (i + 2 * steps) % 8) for i i...  9.59 us
  transfers between devices with their start and end apart: 13, of which 8 were waited for; matrix products, arithmetic and copies ran while one was open for 0% of the time, Pallas kernels for 7%

profile of v7, /device:TPU:1, one launch (start us, length us, event | category | flops | bytes accessed | tf_op | source)
XLA Modules:
  0.0 199.8 jit_solution(1563183986780820127)
XLA Ops:
  0.6 2.8 %pack.1 = bf16[32,160,128]{2,1,0:T(8,128)(2,1)} custom-call(bf16[64,2,1024]{2,1,0:T(2,128)(2,1)} %q_hbm.1, bf16[64,2,1024]{2,1,0:T(2,128)(2,1)} %k_hbm.1, bf16[64,2,1024]{2,1,0:T(2,128)(2,1)} %v_hbm.1, bf16[64,2,1024]{2,1,0:T(2,128)(2,1)} %f_hbm.1, bf16[64,2,1024]{2,1,0:T(2,128)(2,1)} %c_hbm.1), custom_call_target="tpu_custom_call" | custom-call | tf_op jit(solution)/shard_map/pack/pallas_call | solution.py:370
  3.4 0.0 copy-start.2
  3.5 0.0 copy-start.1
  3.5 19.4 %all-to-all-start = ((bf16[32,160,128]{2,1,0:T(8,128)(2,1)}), bf16[32,160,128]{2,1,0:T(8,128)(2,1)S(1)}, u32[]{:S(2)}, u32[]{:S(2)}) async-start(bf16[32,160,128]{2,1,0:T(8,128)(2,1)} %pack.1), calls=%async_computation | async-start | bytes 2621440 | tf_op jit(solution)/shard_map/all_to_all | solution.py:474
  22.9 0.6 fusion.1
  23.5 0.1 fusion
  23.6 0.1 pad_maximum_fusion.1.taps_ref
  23.7 63.4 %all-to-all-done.in_ref = bf16[32,160,128]{2,1,0:T(8,128)(2,1)S(1)} async-done(((bf16[32,160,128]{2,1,0:T(8,128)(2,1)}), bf16[32,160,128]{2,1,0:T(8,128)(2,1)S(1)}, u32[]{:S(2)}, u32[]{:S(2)}) %all-to-all-start) | async-done | bytes 1310752 | tf_op jit(solution)/shard_map/all_to_all | solution.py:474
  87.0 11.0 %forward.1 = (bf16[2,2048,1024]{2,1,0:T(8,128)(2,1)S(1)}, bf16[2048,128]{1,0:T(8,128)(2,1)S(1)}, bf16[128,2048]{1,0:T(8,128)(2,1)S(1)}, f32[2048,128]{1,0:T(8,12...) custom-call(s32[1]{0:T(128)} %bitcast.frames_ref, ...), custom_call_target="tpu_custom_call" | custom-call | flops 8000000000 | bytes 20000000 | tf_op jit(solution)/shard_map/forward/pallas_call | solution.py:398
  98.0 2.9 %collective-permute-start = (f32[16,128]{1,0:T(8,128)S(1)}, f32[16,128]{1,0:T(8,128)S(1)}, u32[]{:S(2)}, u32[]{:S(2)}) collective-permute-start(f32[16,128]{1,0:T(8,128)S(1)} %get-tuple-element.41), channel_id=1, source_target_pairs={{0,1},{1,0},{2,3},{3,2},{4,5},{5,4},{6,7},{7,6},{8,9},{9,8},{10,11... | collective-permute-start | bytes 24584 | tf_op jit(solution)/shard_map/ppermute | solution.py:479
  100.9 3.3 %conv_backward.1 = (bf16[32,64,128]{2,1,0:T(8,128)(2,1)S(1)}, bf16[2048,128]{1,0:T(8,128)(2,1)S(1)}) custom-call(s32[1]{0:T(128)} %bitcast.frames_ref, f32[1056,128]{1,0:T(8,128)S(1)} %get-tuple-element.31.grad, f32[1024,128]{1,0:T(8,128)S(1)} %get-tuple-element.32.cot, f32[1024,128]{1,0:T(8,128)S(1)} %get-tuple-element.33.bo, ...), custom_call_target="tpu_custom_call" | custom-call | flops 2000000000 | bytes 4000000 | tf_op jit(solution)/shard_map/conv_backward/pallas_call | solution.py:430
  104.3 3.3 %collective-permute-start.1 = (f32[16,128]{1,0:T(8,128)S(1)}, f32[16,128]{1,0:T(8,128)S(1)}, u32[]{:S(2)}, u32[]{:S(2)}) collective-permute-start(f32[16,128]{1,0:T(8,128)S(1)} %add.28), channel_id=1, source_target_pairs={{0,2},{1,3},{2,0},{3,1},{4,6},{5,7},{6,4},{7,5},{8,10},{9,11},{10,... | collective-permute-start | bytes 24584 | tf_op jit(solution)/shard_map/ppermute | solution.py:479
  107.5 9.6 %backward.1 = bf16[32,160,128]{2,1,0:T(8,128)(2,1)} custom-call(bf16[32,160,128]{2,1,0:T(8,128)(2,1)S(1)} %all-to-all-done.in_ref, bf16[2,2048,1024]{2,1,0:T(8,128)(2,1)S(1)} %get-tuple-element.30.e_ref, bf16[2048,128]{1,0:T(8,128)(2,1)S(1)} %get-tuple-element.37.gaug_ref, bf16[2048,128]{1,0:T(8,128)(2,1)S(1)} %get-tuple-element.38.vaug, ...), custom_call_target="tpu_custom_call" | custom-call | flops 8999999488 | bytes 20000000 | tf_op jit(solution)/shard_map/backward/pallas_call | solution.py:445
  117.2 7.7 %all-to-all-start.1 = ((bf16[32,160,128]{2,1,0:T(8,128)(2,1)}), bf16[32,160,128]{2,1,0:T(8,128)(2,1)S(1)}, u32[]{:S(2)}, u32[]{:S(2)}) async-start(bf16[32,160,128]{2,1,0:T(8,128)(2,1)} %backward.1), calls=%async_computation.1 | async-start | bytes 2621440 | tf_op jit(solution)/shard_map/all_to_all | solution.py:474
  124.9 3.2 %collective-permute-start.2 = (f32[16,128]{1,0:T(8,128)S(1)}, f32[16,128]{1,0:T(8,128)S(1)}, u32[]{:S(2)}, u32[]{:S(2)}) collective-permute-start(f32[16,128]{1,0:T(8,128)S(1)} %add.29), channel_id=1, source_target_pairs={{0,4},{1,5},{2,6},{3,7},{4,0},{5,1},{6,2},{7,3},{8,12},{9,13},{10,... | collective-permute-start | bytes 24584 | tf_op jit(solution)/shard_map/ppermute | solution.py:479
  128.1 1.5 collective-permute-done.2
  129.6 4.8 %collective-permute-start.3 = (f32[16,128]{1,0:T(8,128)S(1)}, f32[16,128]{1,0:T(8,128)S(1)}, u32[]{:S(2)}, u32[]{:S(2)}) collective-permute-start(f32[16,128]{1,0:T(8,128)S(1)} %add.30), channel_id=1, source_target_pairs={{0,8},{1,9},{2,10},{3,11},{4,12},{5,13},{6,14},{7,15},{8,0},{9,1},... | collective-permute-start | bytes 24584 | tf_op jit(solution)/shard_map/ppermute | solution.py:479
  134.4 1.4 collective-permute-done.3
  135.8 3.8 %collective-permute-start.4 = (bf16[16,128]{1,0:T(8,128)(2,1)S(1)}, bf16[16,128]{1,0:T(8,128)(2,1)S(1)}, u32[]{:S(2)}, u32[]{:S(2)}) collective-permute-start(bf16[16,128]{1,0:T(8,128)(2,1)S(1)} %add.31), channel_id=1, source_target_pairs={{0,16},{16,0},{32,48},{48,32},{64,80},{80,64},{96,112},{112,96},{1... | collective-permute-start | bytes 12296 | tf_op jit(solution)/shard_map/ppermute | solution.py:479
  139.6 0.8 collective-permute-done.4
  140.4 4.6 %collective-permute-start.7 = (bf16[2,16,128]{2,1,0:T(8,128)(2,1)S(1)}, bf16[2,16,128]{2,1,0:T(8,128)(2,1)S(1)}, u32[]{:S(2)}, u32[]{:S(2)}) collective-permute-start(bf16[2,16,128]{2,1,0:T(8,128)(2,1)S(1)} %get-tuple-element.54), channel_id=1, source_target_pairs={{0,96},{16,112},{32,0},{48,16},{64,32},{80,48},{96,64},{112,80},{1... | collective-permute-start | bytes 24584 | tf_op jit(solution)/shard_map/ppermute | solution.py:484
  145.1 2.5 %collective-permute-start.6 = (bf16[2,16,128]{2,1,0:T(8,128)(2,1)S(1)}, bf16[2,16,128]{2,1,0:T(8,128)(2,1)S(1)}, u32[]{:S(2)}, u32[]{:S(2)}) collective-permute-start(bf16[2,16,128]{2,1,0:T(8,128)(2,1)S(1)} %get-tuple-element.54), channel_id=1, source_target_pairs={{0,64},{16,80},{32,96},{48,112},{64,0},{80,16},{96,32},{112,48},{1... | collective-permute-start | bytes 24584 | tf_op jit(solution)/shard_map/ppermute | solution.py:484
  147.5 2.5 %collective-permute-start.5 = (bf16[2,16,128]{2,1,0:T(8,128)(2,1)S(1)}, bf16[2,16,128]{2,1,0:T(8,128)(2,1)S(1)}, u32[]{:S(2)}, u32[]{:S(2)}) collective-permute-start(bf16[2,16,128]{2,1,0:T(8,128)(2,1)S(1)} %get-tuple-element.54), channel_id=1, source_target_pairs={{0,32},{16,48},{32,64},{48,80},{64,96},{80,112},{96,0},{112,16},{1... | collective-permute-start | bytes 24584 | tf_op jit(solution)/shard_map/ppermute | solution.py:484
  150.0 1.2 collective-permute-done.6
  151.2 2.2 %collective-permute-done.5 = bf16[2,16,128]{2,1,0:T(8,128)(2,1)S(1)} collective-permute-done((bf16[2,16,128]{2,1,0:T(8,128)(2,1)S(1)}, bf16[2,16,128]{2,1,0:T(8,128)(2,1)S(1)}, u32[]{:S(2)}, u32[]{:S(2)}) %collective-permute-start.5) | collective-permute-done | bytes 8224 | tf_op jit(solution)/shard_map/ppermute | solution.py:484
  153.5 11.8 %collective-permute-start.8 = (bf16[4,2,16,128]{3,2,1,0:T(8,128)(2,1)S(1)}, bf16[4,2,16,128]{3,2,1,0:T(8,128)(2,1)S(1)}, u32[]{:S(2)}, u32[]{:S(2)}) collective-permute-start(bf16[4,2,16,128]{3,2,1,0:T(8,128)(2,1)S(1)} %pad_maximum_fusion), channel_id=1, source_target_pairs={{0,256},{16,272},{32,288},{48,304},{64,320},{80,336},{96,352},{112... | collective-permute-start | bytes 98312 | tf_op jit(solution)/shard_map/ppermute | solution.py:479
  165.3 1.9 collective-permute-start.10
  167.2 2.4 %collective-permute-start.9 = (bf16[4,2,16,128]{3,2,1,0:T(8,128)(2,1)S(1)}, bf16[4,2,16,128]{3,2,1,0:T(8,128)(2,1)S(1)}, u32[]{:S(2)}, u32[]{:S(2)}) collective-permute-start(bf16[4,2,16,128]{3,2,1,0:T(8,128)(2,1)S(1)} %pad_maximum_fusion), channel_id=1, source_target_pairs={{0,128},{16,144},{32,160},{48,176},{64,192},{80,208},{96,224},{112... | collective-permute-start | bytes 98312 | tf_op jit(solution)/shard_map/ppermute | solution.py:479
  169.7 26.7 %collective-permute-done.8 = bf16[4,2,16,128]{3,2,1,0:T(8,128)(2,1)S(1)} collective-permute-done((bf16[4,2,16,128]{3,2,1,0:T(8,128)(2,1)S(1)}, bf16[4,2,16,128]{3,2,1,0:T(8,128)(2,1)S(1)}, u32[]{:S(2)}, u32[]{:S(2)}) %collective-permute-start.8) | collective-permute-done | bytes 32800 | tf_op jit(solution)/shard_map/ppermute | solution.py:479
  196.4 1.2 collective-permute-done.10
  197.6 0.8 unpack_params.1
  198.4 1.3 unpack.1
  (17 shorter events, 0.1 us)
Async XLA Ops:
  3.4 19.4 %copy-start.2 = (s32[2]{0:T(128)S(1)}, s32[2]{0:T(128)}, u32[]{:S(2)}) copy-start(s32[2]{0:T(128)} %param.13) | copy-start | bytes 28
  3.4 20.1 %copy-start = (f32[31,1024]{1,0:T(8,128)S(1)}, f32[31,1024]{1,0:T(8,128)}, u32[]{:S(2)}) copy-start(f32[31,1024]{1,0:T(8,128)} %param.14) | copy-start | bytes 380932
  3.5 20.0 %copy-start.1 = (f32[1024]{0:T(1024)S(1)}, f32[1024]{0:T(1024)}, u32[]{:S(2)}) copy-start(f32[1024]{0:T(1024)} %param.15) | copy-start | bytes 12292
  3.5 83.6 %all-to-all-start = ((bf16[32,160,128]{2,1,0:T(8,128)(2,1)}), bf16[32,160,128]{2,1,0:T(8,128)(2,1)S(1)}, u32[]{:S(2)}, u32[]{:S(2)}) async-start(bf16[32,160,128]{2,1,0:T(8,128)(2,1)} %pack.1), calls=%async_computation | async-start | bytes 2621440 | tf_op jit(solution)/shard_map/all_to_all | solution.py:474
  98.0 6.2 %collective-permute-start = (f32[16,128]{1,0:T(8,128)S(1)}, f32[16,128]{1,0:T(8,128)S(1)}, u32[]{:S(2)}, u32[]{:S(2)}) collective-permute-start(f32[16,128]{1,0:T(8,128)S(1)} %get-tuple-element.41), channel_id=1, source_target_pairs={{0,1},{1,0},{2,3},{3,2},{4,5},{5,4},{6,7},{7,6},{8,9},{9,8},{10,11... | collective-permute-start | bytes 24584 | tf_op jit(solution)/shard_map/ppermute | solution.py:479
  104.3 12.9 %collective-permute-start.1 = (f32[16,128]{1,0:T(8,128)S(1)}, f32[16,128]{1,0:T(8,128)S(1)}, u32[]{:S(2)}, u32[]{:S(2)}) collective-permute-start(f32[16,128]{1,0:T(8,128)S(1)} %add.28), channel_id=1, source_target_pairs={{0,2},{1,3},{2,0},{3,1},{4,6},{5,7},{6,4},{7,5},{8,10},{9,11},{10,... | collective-permute-start | bytes 24584 | tf_op jit(solution)/shard_map/ppermute | solution.py:479
  117.2 81.3 %all-to-all-start.1 = ((bf16[32,160,128]{2,1,0:T(8,128)(2,1)}), bf16[32,160,128]{2,1,0:T(8,128)(2,1)S(1)}, u32[]{:S(2)}, u32[]{:S(2)}) async-start(bf16[32,160,128]{2,1,0:T(8,128)(2,1)} %backward.1), calls=%async_computation.1 | async-start | bytes 2621440 | tf_op jit(solution)/shard_map/all_to_all | solution.py:474
  124.9 4.7 %collective-permute-start.2 = (f32[16,128]{1,0:T(8,128)S(1)}, f32[16,128]{1,0:T(8,128)S(1)}, u32[]{:S(2)}, u32[]{:S(2)}) collective-permute-start(f32[16,128]{1,0:T(8,128)S(1)} %add.29), channel_id=1, source_target_pairs={{0,4},{1,5},{2,6},{3,7},{4,0},{5,1},{6,2},{7,3},{8,12},{9,13},{10,... | collective-permute-start | bytes 24584 | tf_op jit(solution)/shard_map/ppermute | solution.py:479
  129.6 6.2 %collective-permute-start.3 = (f32[16,128]{1,0:T(8,128)S(1)}, f32[16,128]{1,0:T(8,128)S(1)}, u32[]{:S(2)}, u32[]{:S(2)}) collective-permute-start(f32[16,128]{1,0:T(8,128)S(1)} %add.30), channel_id=1, source_target_pairs={{0,8},{1,9},{2,10},{3,11},{4,12},{5,13},{6,14},{7,15},{8,0},{9,1},... | collective-permute-start | bytes 24584 | tf_op jit(solution)/shard_map/ppermute | solution.py:479
  135.8 4.7 %collective-permute-start.4 = (bf16[16,128]{1,0:T(8,128)(2,1)S(1)}, bf16[16,128]{1,0:T(8,128)(2,1)S(1)}, u32[]{:S(2)}, u32[]{:S(2)}) collective-permute-start(bf16[16,128]{1,0:T(8,128)(2,1)S(1)} %add.31), channel_id=1, source_target_pairs={{0,16},{16,0},{32,48},{48,32},{64,80},{80,64},{96,112},{112,96},{1... | collective-permute-start | bytes 12296 | tf_op jit(solution)/shard_map/ppermute | solution.py:479
  140.4 9.6 %collective-permute-start.7 = (bf16[2,16,128]{2,1,0:T(8,128)(2,1)S(1)}, bf16[2,16,128]{2,1,0:T(8,128)(2,1)S(1)}, u32[]{:S(2)}, u32[]{:S(2)}) collective-permute-start(bf16[2,16,128]{2,1,0:T(8,128)(2,1)S(1)} %get-tuple-element.54), channel_id=1, source_target_pairs={{0,96},{16,112},{32,0},{48,16},{64,32},{80,48},{96,64},{112,80},{1... | collective-permute-start | bytes 24584 | tf_op jit(solution)/shard_map/ppermute | solution.py:484
  145.1 6.2 %collective-permute-start.6 = (bf16[2,16,128]{2,1,0:T(8,128)(2,1)S(1)}, bf16[2,16,128]{2,1,0:T(8,128)(2,1)S(1)}, u32[]{:S(2)}, u32[]{:S(2)}) collective-permute-start(bf16[2,16,128]{2,1,0:T(8,128)(2,1)S(1)} %get-tuple-element.54), channel_id=1, source_target_pairs={{0,64},{16,80},{32,96},{48,112},{64,0},{80,16},{96,32},{112,48},{1... | collective-permute-start | bytes 24584 | tf_op jit(solution)/shard_map/ppermute | solution.py:484
  147.5 5.9 %collective-permute-start.5 = (bf16[2,16,128]{2,1,0:T(8,128)(2,1)S(1)}, bf16[2,16,128]{2,1,0:T(8,128)(2,1)S(1)}, u32[]{:S(2)}, u32[]{:S(2)}) collective-permute-start(bf16[2,16,128]{2,1,0:T(8,128)(2,1)S(1)} %get-tuple-element.54), channel_id=1, source_target_pairs={{0,32},{16,48},{32,64},{48,80},{64,96},{80,112},{96,0},{112,16},{1... | collective-permute-start | bytes 24584 | tf_op jit(solution)/shard_map/ppermute | solution.py:484
  153.5 42.9 %collective-permute-start.8 = (bf16[4,2,16,128]{3,2,1,0:T(8,128)(2,1)S(1)}, bf16[4,2,16,128]{3,2,1,0:T(8,128)(2,1)S(1)}, u32[]{:S(2)}, u32[]{:S(2)}) collective-permute-start(bf16[4,2,16,128]{3,2,1,0:T(8,128)(2,1)S(1)} %pad_maximum_fusion), channel_id=1, source_target_pairs={{0,256},{16,272},{32,288},{48,304},{64,320},{80,336},{96,352},{112... | collective-permute-start | bytes 98312 | tf_op jit(solution)/shard_map/ppermute | solution.py:479
  165.3 32.3 %collective-permute-start.10 = (bf16[4,2,16,128]{3,2,1,0:T(8,128)(2,1)S(1)}, bf16[4,2,16,128]{3,2,1,0:T(8,128)(2,1)S(1)}, u32[]{:S(2)}, u32[]{:S(2)}) collective-permute-start(bf16[4,2,16,128]{3,2,1,0:T(8,128)(2,1)S(1)} %pad_maximum_fusion), channel_id=1, source_target_pairs={{0,384},{16,400},{32,416},{48,432},{64,448},{80,464},{96,480},{112... | collective-permute-start | bytes 98312 | tf_op jit(solution)/shard_map/ppermute | solution.py:479
  167.2 30.4 %collective-permute-start.9 = (bf16[4,2,16,128]{3,2,1,0:T(8,128)(2,1)S(1)}, bf16[4,2,16,128]{3,2,1,0:T(8,128)(2,1)S(1)}, u32[]{:S(2)}, u32[]{:S(2)}) collective-permute-start(bf16[4,2,16,128]{3,2,1,0:T(8,128)(2,1)S(1)} %pad_maximum_fusion), channel_id=1, source_target_pairs={{0,128},{16,144},{32,160},{48,176},{64,192},{80,208},{96,224},{112... | collective-permute-start | bytes 98312 | tf_op jit(solution)/shard_map/ppermute | solution.py:479

commit v8 on v7

--- a/solution.py
+++ b/solution.py
@@ -341,14 +341,14 @@
     convolve(valid, in_ref, ctx_ref, taps_ref, part_ref, field, grad, hid, cot, bo, sums_ref)
 
 
-def params_kernel(place_ref, same_ref, other_ref, taps_ref, bias_ref, heads):
+def params_kernel(place_ref, parts_ref, taps_ref, bias_ref, heads):
     place = place_ref[0]
     core, x, half = place % 2, place // 2 % 4, place // 8 % 2
-    for n, part in enumerate((same_ref, other_ref)):
-        for i in range(part.shape[0]):
-            for j in range(part.shape[1]):
+    for i in range(parts_ref.shape[0]):
+        for j in range(parts_ref.shape[1]):
+            for n in range(parts_ref.shape[2]):
                 head = (half + n) % 2 * 8 + (x + 4 - i) % 4 * 2 + (core + j) % 2
-                heads[head] = part[i, j]
+                heads[head] = parts_ref[i, j, n]
     rows = heads.shape[1]
     for h in range(0, HEADS, 2):
         lanes = slice(h * HD, (h + 2) * HD)
@@ -461,12 +461,12 @@
     taps, bias = pl.pallas_call(
         params_kernel,
         out_shape=[shape_of(TAPS, width, dtype=F32), shape_of(1, width, dtype=F32)],
-        in_specs=[SMEM] + [VMEM] * len(parts),
+        in_specs=[SMEM, VMEM],
         out_specs=[VMEM] * 2,
-        scratch_shapes=[pltpu.VMEM((HEADS, *parts[0].shape[2:]), F32)],
+        scratch_shapes=[pltpu.VMEM((HEADS, *parts.shape[3:]), F32)],
         compiler_params=params(8),
         name="unpack_params",
-    )(place.reshape(1), *parts)
+    )(place.reshape(1), parts)
     return taps, bias.reshape(width)
 
 
@@ -490,9 +490,8 @@
     part = jnp.stack([part, swap(part, "seq", 1)])
     part = jnp.stack([part] + [along_x(part, steps) for steps in (1, 2, 3)]).astype(BF16)
     wide = part.astype(F32)
-    same = wide + swap(part, "seq", 16).astype(F32)
-    other = swap(part, "seq", 8).astype(F32) + swap(part, "seq", 24).astype(F32)
-    return unpack_params(place, [same, other])
+    first, second, third = [swap(part, "dp", bit).astype(F32) for bit in (1, 2, 3)]
+    return unpack_params(place, (wide + first) + (second + third))
 
 
 def on_device(
@@ -509,14 +508,14 @@
 
     field = exchange(pack(queries, key_vectors, value_vectors, features, cotangent))
     e, vaug, kt, ctx, grad, cot, bo, part = forward(valid, field, taps)
-    near = swap(part, "dp", 1)
+    near = swap(part, "seq", 16)
     bogf, gaug = conv_backward(valid, grad, cot, bo, ctx, taps, field.shape[0])
     gaug, part, near = lax.optimization_barrier((gaug, part, near))
     part = part + near
-    near = swap(part, "dp", 2)
+    near = swap(part, "seq", 8)
     field = backward(field, e, gaug, vaug, kt, bogf)
     field, part, near = lax.optimization_barrier((field, part, near))
-    part = part + near
+    part = jnp.stack([part, near])
     field = exchange(field)
     grad_kernel, grad_bias = reduce_rest(part, item)
     grad_q, grad_k, grad_v, block_out, grad_features = unpack(field, rows, utts)

time: 200 us -> 205 us (1.025)
  waiting for transfers between devices: 98.4 us -> 101 us
    ppermute x8, waiting for transfers between devices: 31.6 us -> 34.4 us  [swap(): return lax.ppermute(field, axis, [(i, i ^ bit) for i in range(count)])]
  transfers between devices with their start and end apart: 13 -> 13, of which waited for: 8 -> 10; matrix products, arithmetic and copies ran while one was open for 0% -> 0% of each run, Pallas kernels for 7% -> 7%
where the time goes in v8:
time: 205 us; the launch traced here: 204 us
  waiting for transfers between devices  101 us (49%)
  starting transfers between devices  72 us (35%)
  Pallas kernels  28.9 us (14%)
    all_to_all x2, waiting for transfers between devices, exchange(): return lax.all_to_all(field, 'seq', split_axis=0, concat_axis=0, tiled=True)  63.4 us
    ppermute x8, starting transfers between devices, swap(): return lax.ppermute(field, axis, [(i, i ^ bit) for i in range(count)])  35.9 us
    ppermute x8, waiting for transfers between devices, swap(): return lax.ppermute(field, axis, [(i, i ^ bit) for i in range(count)])  34.4 us
    all_to_all x2, starting transfers between devices, exchange(): return lax.all_to_all(field, 'seq', split_axis=0, concat_axis=0, tiled=True)  26.5 us
    pallas_call x1, Pallas kernels, forward(): pl.pallas_call(forward_kernel, out_shape=[shape_of(length // QB, length,...  11 us
    pallas_call x1, Pallas kernels, backward(): pl.pallas_call(backward_kernel, out_shape=shape_of(*field.shape), in_spec...  9.64 us
    ppermute x3, starting transfers between devices, along_x(): lax.ppermute(field, 'seq', [(i, i // 8 * 8 + (i + 2 * steps) % 8) for i i...  9.59 us
  transfers between devices with their start and end apart: 13, of which 10 were waited for; matrix products, arithmetic and copies ran while one was open for 0% of the time, Pallas kernels for 7%

profile of v8, /device:TPU:1, one launch (start us, length us, event | category | flops | bytes accessed | tf_op | source)
XLA Modules:
  0.0 203.8 jit_solution(2648453468427502039)
XLA Ops:
  0.6 2.8 %pack.1 = bf16[32,160,128]{2,1,0:T(8,128)(2,1)} custom-call(bf16[64,2,1024]{2,1,0:T(2,128)(2,1)} %q_hbm.1, bf16[64,2,1024]{2,1,0:T(2,128)(2,1)} %k_hbm.1, bf16[64,2,1024]{2,1,0:T(2,128)(2,1)} %v_hbm.1, bf16[64,2,1024]{2,1,0:T(2,128)(2,1)} %f_hbm.1, bf16[64,2,1024]{2,1,0:T(2,128)(2,1)} %c_hbm.1), custom_call_target="tpu_custom_call" | custom-call | tf_op jit(solution)/shard_map/pack/pallas_call | solution.py:370
  3.5 19.4 %all-to-all-start = ((bf16[32,160,128]{2,1,0:T(8,128)(2,1)}), bf16[32,160,128]{2,1,0:T(8,128)(2,1)S(1)}, u32[]{:S(2)}, u32[]{:S(2)}) async-start(bf16[32,160,128]{2,1,0:T(8,128)(2,1)} %pack.1), calls=%async_computation | async-start | bytes 2621440 | tf_op jit(solution)/shard_map/all_to_all | solution.py:474
  22.9 0.6 fusion.1
  23.5 0.1 fusion
  23.6 0.1 pad_maximum_fusion.2.taps_ref
  23.7 63.4 %all-to-all-done.in_ref = bf16[32,160,128]{2,1,0:T(8,128)(2,1)S(1)} async-done(((bf16[32,160,128]{2,1,0:T(8,128)(2,1)}), bf16[32,160,128]{2,1,0:T(8,128)(2,1)S(1)}, u32[]{:S(2)}, u32[]{:S(2)}) %all-to-all-start) | async-done | bytes 1310752 | tf_op jit(solution)/shard_map/all_to_all | solution.py:474
  87.0 11.0 %forward.1 = (bf16[2,2048,1024]{2,1,0:T(8,128)(2,1)S(1)}, bf16[2048,128]{1,0:T(8,128)(2,1)S(1)}, bf16[128,2048]{1,0:T(8,128)(2,1)S(1)}, f32[2048,128]{1,0:T(8,12...) custom-call(s32[1]{0:T(128)} %bitcast.frames_ref, ...), custom_call_target="tpu_custom_call" | custom-call | flops 8000000000 | bytes 20000000 | tf_op jit(solution)/shard_map/forward/pallas_call | solution.py:398
  98.0 7.1 %collective-permute-start = (f32[16,128]{1,0:T(8,128)S(1)}, f32[16,128]{1,0:T(8,128)S(1)}, u32[]{:S(2)}, u32[]{:S(2)}) collective-permute-start(f32[16,128]{1,0:T(8,128)S(1)} %get-tuple-element.41), channel_id=1, source_target_pairs={{0,256},{16,272},{32,288},{48,304},{64,320},{80,336},{96,352},{112... | collective-permute-start | bytes 24584 | tf_op jit(solution)/shard_map/ppermute | solution.py:479
  105.2 3.3 %conv_backward.1 = (bf16[32,64,128]{2,1,0:T(8,128)(2,1)S(1)}, bf16[2048,128]{1,0:T(8,128)(2,1)S(1)}) custom-call(s32[1]{0:T(128)} %bitcast.frames_ref, f32[1056,128]{1,0:T(8,128)S(1)} %get-tuple-element.31.grad, f32[1024,128]{1,0:T(8,128)S(1)} %get-tuple-element.32.cot, f32[1024,128]{1,0:T(8,128)S(1)} %get-tuple-element.33.bo, ...), custom_call_target="tpu_custom_call" | custom-call | flops 2000000000 | bytes 4000000 | tf_op jit(solution)/shard_map/conv_backward/pallas_call | solution.py:430
  108.5 2.7 %collective-permute-done = f32[16,128]{1,0:T(8,128)S(1)} collective-permute-done((f32[16,128]{1,0:T(8,128)S(1)}, f32[16,128]{1,0:T(8,128)S(1)}, u32[]{:S(2)}, u32[]{:S(2)}) %collective-permute-start) | collective-permute-done | bytes 8224 | tf_op jit(solution)/shard_map/ppermute | solution.py:479
  111.1 7.6 %collective-permute-start.1 = (f32[16,128]{1,0:T(8,128)S(1)}, f32[16,128]{1,0:T(8,128)S(1)}, u32[]{:S(2)}, u32[]{:S(2)}) collective-permute-start(f32[16,128]{1,0:T(8,128)S(1)} %add.28), channel_id=1, source_target_pairs={{0,128},{16,144},{32,160},{48,176},{64,192},{80,208},{96,224},{112... | collective-permute-start | bytes 24584 | tf_op jit(solution)/shard_map/ppermute | solution.py:479
  118.8 9.6 %backward.1 = bf16[32,160,128]{2,1,0:T(8,128)(2,1)} custom-call(bf16[32,160,128]{2,1,0:T(8,128)(2,1)S(1)} %all-to-all-done.in_ref, bf16[2,2048,1024]{2,1,0:T(8,128)(2,1)S(1)} %get-tuple-element.30.e_ref, bf16[2048,128]{1,0:T(8,128)(2,1)S(1)} %get-tuple-element.37.gaug_ref, bf16[2048,128]{1,0:T(8,128)(2,1)S(1)} %get-tuple-element.38.vaug, ...), custom_call_target="tpu_custom_call" | custom-call | flops 8999999488 | bytes 20000000 | tf_op jit(solution)/shard_map/backward/pallas_call | solution.py:445
  128.4 7.2 %all-to-all-start.1 = ((bf16[32,160,128]{2,1,0:T(8,128)(2,1)}), bf16[32,160,128]{2,1,0:T(8,128)(2,1)S(1)}, u32[]{:S(2)}, u32[]{:S(2)}) async-start(bf16[32,160,128]{2,1,0:T(8,128)(2,1)} %backward.1), calls=%async_computation.1 | async-start | bytes 2621440 | tf_op jit(solution)/shard_map/all_to_all | solution.py:474
  135.6 3.2 %collective-permute-start.2 = (f32[2,16,128]{2,1,0:T(8,128)S(1)}, f32[2,16,128]{2,1,0:T(8,128)S(1)}, u32[]{:S(2)}, u32[]{:S(2)}) collective-permute-start(f32[2,16,128]{2,1,0:T(8,128)S(1)} %pad_maximum_fusion.3), channel_id=1, source_target_pairs={{0,4},{1,5},{2,6},{3,7},{4,0},{5,1},{6,2},{7,3},{8,12},{9,13},{10,... | collective-permute-start | bytes 49160 | tf_op jit(solution)/shard_map/ppermute | solution.py:479
  138.8 1.6 collective-permute-done.2
  140.4 4.8 %collective-permute-start.3 = (f32[2,16,128]{2,1,0:T(8,128)S(1)}, f32[2,16,128]{2,1,0:T(8,128)S(1)}, u32[]{:S(2)}, u32[]{:S(2)}) collective-permute-start(f32[2,16,128]{2,1,0:T(8,128)S(1)} %fusion.2), channel_id=1, source_target_pairs={{0,8},{1,9},{2,10},{3,11},{4,12},{5,13},{6,14},{7,15},{8,0},{9,1},... | collective-permute-start | bytes 49160 | tf_op jit(solution)/shard_map/ppermute | solution.py:479
  145.2 1.4 collective-permute-done.3
  146.6 3.8 %collective-permute-start.4 = (bf16[2,16,128]{2,1,0:T(8,128)(2,1)S(1)}, bf16[2,16,128]{2,1,0:T(8,128)(2,1)S(1)}, u32[]{:S(2)}, u32[]{:S(2)}) collective-permute-start(bf16[2,16,128]{2,1,0:T(8,128)(2,1)S(1)} %fusion.3), channel_id=1, source_target_pairs={{0,16},{16,0},{32,48},{48,32},{64,80},{80,64},{96,112},{112,96},{1... | collective-permute-start | bytes 24584 | tf_op jit(solution)/shard_map/ppermute | solution.py:479
  150.5 0.8 collective-permute-done.4
  151.3 4.6 %collective-permute-start.7 = (bf16[2,2,16,128]{3,2,1,0:T(8,128)(2,1)S(1)}, bf16[2,2,16,128]{3,2,1,0:T(8,128)(2,1)S(1)}, u32[]{:S(2)}, u32[]{:S(2)}) collective-permute-start(bf16[2,2,16,128]{3,2,1,0:T(8,128)(2,1)S(1)} %get-tuple-element.54), channel_id=1, source_target_pairs={{0,96},{16,112},{32,0},{48,16},{64,32},{80,48},{96,64},{112,80},{1... | collective-permute-start | bytes 49160 | tf_op jit(solution)/shard_map/ppermute | solution.py:484
  155.9 2.5 %collective-permute-start.6 = (bf16[2,2,16,128]{3,2,1,0:T(8,128)(2,1)S(1)}, bf16[2,2,16,128]{3,2,1,0:T(8,128)(2,1)S(1)}, u32[]{:S(2)}, u32[]{:S(2)}) collective-permute-start(bf16[2,2,16,128]{3,2,1,0:T(8,128)(2,1)S(1)} %get-tuple-element.54), channel_id=1, source_target_pairs={{0,64},{16,80},{32,96},{48,112},{64,0},{80,16},{96,32},{112,48},{1... | collective-permute-start | bytes 49160 | tf_op jit(solution)/shard_map/ppermute | solution.py:484
  158.4 2.5 %collective-permute-start.5 = (bf16[2,2,16,128]{3,2,1,0:T(8,128)(2,1)S(1)}, bf16[2,2,16,128]{3,2,1,0:T(8,128)(2,1)S(1)}, u32[]{:S(2)}, u32[]{:S(2)}) collective-permute-start(bf16[2,2,16,128]{3,2,1,0:T(8,128)(2,1)S(1)} %get-tuple-element.54), channel_id=1, source_target_pairs={{0,32},{16,48},{32,64},{48,80},{64,96},{80,112},{96,0},{112,16},{1... | collective-permute-start | bytes 49160 | tf_op jit(solution)/shard_map/ppermute | solution.py:484
  160.9 1.5 collective-permute-done.6
  162.4 2.0 collective-permute-done.5
  164.4 4.5 %collective-permute-start.10 = (bf16[4,2,2,16,128]{4,3,2,1,0:T(8,128)(2,1)S(1)}, bf16[4,2,2,16,128]{4,3,2,1,0:T(8,128)(2,1)S(1)}, u32[]{:S(2)}, u32[]{:S(2)}) collective-permute-start(bf16[4,2,2,16,128]{4,3,2,1,0:T(8,128)(2,1)S(1)} %pad_maximum_fusion), channel_id=1, source_target_pairs={{0,3},{1,2},{2,1},{3,0},{4,7},{5,6},{6,5},{7,4},{8,11},{9,10},{10,... | collective-permute-start | bytes 196616 | tf_op jit(solution)/shard_map/ppermute | solution.py:479
  168.9 2.5 %collective-permute-start.8 = (bf16[4,2,2,16,128]{4,3,2,1,0:T(8,128)(2,1)S(1)}, bf16[4,2,2,16,128]{4,3,2,1,0:T(8,128)(2,1)S(1)}, u32[]{:S(2)}, u32[]{:S(2)}) collective-permute-start(bf16[4,2,2,16,128]{4,3,2,1,0:T(8,128)(2,1)S(1)} %pad_maximum_fusion), channel_id=1, source_target_pairs={{0,1},{1,0},{2,3},{3,2},{4,5},{5,4},{6,7},{7,6},{8,9},{9,8},{10,11... | collective-permute-start | bytes 196616 | tf_op jit(solution)/shard_map/ppermute | solution.py:479
  171.4 2.3 %collective-permute-start.9 = (bf16[4,2,2,16,128]{4,3,2,1,0:T(8,128)(2,1)S(1)}, bf16[4,2,2,16,128]{4,3,2,1,0:T(8,128)(2,1)S(1)}, u32[]{:S(2)}, u32[]{:S(2)}) collective-permute-start(bf16[4,2,2,16,128]{4,3,2,1,0:T(8,128)(2,1)S(1)} %pad_maximum_fusion), channel_id=1, source_target_pairs={{0,2},{1,3},{2,0},{3,1},{4,6},{5,7},{6,4},{7,5},{8,10},{9,11},{10,... | collective-permute-start | bytes 196616 | tf_op jit(solution)/shard_map/ppermute | solution.py:479
  173.7 13.1 %collective-permute-done.10 = bf16[4,2,2,16,128]{4,3,2,1,0:T(8,128)(2,1)S(1)} collective-permute-done((bf16[4,2,2,16,128]{4,3,2,1,0:T(8,128)(2,1)S(1)}, bf16[4,2,2,16,128]{4,3,2,1,0:T(8,128)(2,1)S(1)}, u32[]{:S(2)}, u32[]{:S(2)}) %collective-permute-start.10) | collective-permute-done | bytes 65568 | tf_op jit(solution)/shard_map/ppermute | solution.py:479
  186.8 11.5 %collective-permute-done.8 = bf16[4,2,2,16,128]{4,3,2,1,0:T(8,128)(2,1)S(1)} collective-permute-done((bf16[4,2,2,16,128]{4,3,2,1,0:T(8,128)(2,1)S(1)}, bf16[4,2,2,16,128]{4,3,2,1,0:T(8,128)(2,1)S(1)}, u32[]{:S(2)}, u32[]{:S(2)}) %collective-permute-start.8) | collective-permute-done | bytes 65568 | tf_op jit(solution)/shard_map/ppermute | solution.py:479
  198.4 3.2 %collective-permute-done.9 = bf16[4,2,2,16,128]{4,3,2,1,0:T(8,128)(2,1)S(1)} collective-permute-done((bf16[4,2,2,16,128]{4,3,2,1,0:T(8,128)(2,1)S(1)}, bf16[4,2,2,16,128]{4,3,2,1,0:T(8,128)(2,1)S(1)}, u32[]{:S(2)}, u32[]{:S(2)}) %collective-permute-start.9) | collective-permute-done | bytes 65568 | tf_op jit(solution)/shard_map/ppermute | solution.py:479
  201.7 0.8 unpack_params.1
  202.5 1.3 unpack.1
  (16 shorter events, 0.1 us)
Async XLA Ops:
  3.4 19.4 %copy-start.2 = (s32[2]{0:T(128)S(1)}, s32[2]{0:T(128)}, u32[]{:S(2)}) copy-start(s32[2]{0:T(128)} %param.13) | copy-start | bytes 28
  3.4 20.1 %copy-start = (f32[31,1024]{1,0:T(8,128)S(1)}, f32[31,1024]{1,0:T(8,128)}, u32[]{:S(2)}) copy-start(f32[31,1024]{1,0:T(8,128)} %param.14) | copy-start | bytes 380932
  3.5 20.0 %copy-start.1 = (f32[1024]{0:T(1024)S(1)}, f32[1024]{0:T(1024)}, u32[]{:S(2)}) copy-start(f32[1024]{0:T(1024)} %param.15) | copy-start | bytes 12292
  3.5 83.6 %all-to-all-start = ((bf16[32,160,128]{2,1,0:T(8,128)(2,1)}), bf16[32,160,128]{2,1,0:T(8,128)(2,1)S(1)}, u32[]{:S(2)}, u32[]{:S(2)}) async-start(bf16[32,160,128]{2,1,0:T(8,128)(2,1)} %pack.1), calls=%async_computation | async-start | bytes 2621440 | tf_op jit(solution)/shard_map/all_to_all | solution.py:474
  98.0 13.1 %collective-permute-start = (f32[16,128]{1,0:T(8,128)S(1)}, f32[16,128]{1,0:T(8,128)S(1)}, u32[]{:S(2)}, u32[]{:S(2)}) collective-permute-start(f32[16,128]{1,0:T(8,128)S(1)} %get-tuple-element.41), channel_id=1, source_target_pairs={{0,256},{16,272},{32,288},{48,304},{64,320},{80,336},{96,352},{112... | collective-permute-start | bytes 24584 | tf_op jit(solution)/shard_map/ppermute | solution.py:479
  111.1 17.3 %collective-permute-start.1 = (f32[16,128]{1,0:T(8,128)S(1)}, f32[16,128]{1,0:T(8,128)S(1)}, u32[]{:S(2)}, u32[]{:S(2)}) collective-permute-start(f32[16,128]{1,0:T(8,128)S(1)} %add.28), channel_id=1, source_target_pairs={{0,128},{16,144},{32,160},{48,176},{64,192},{80,208},{96,224},{112... | collective-permute-start | bytes 24584 | tf_op jit(solution)/shard_map/ppermute | solution.py:479
  128.4 74.1 %all-to-all-start.1 = ((bf16[32,160,128]{2,1,0:T(8,128)(2,1)}), bf16[32,160,128]{2,1,0:T(8,128)(2,1)S(1)}, u32[]{:S(2)}, u32[]{:S(2)}) async-start(bf16[32,160,128]{2,1,0:T(8,128)(2,1)} %backward.1), calls=%async_computation.1 | async-start | bytes 2621440 | tf_op jit(solution)/shard_map/all_to_all | solution.py:474
  135.6 4.8 %collective-permute-start.2 = (f32[2,16,128]{2,1,0:T(8,128)S(1)}, f32[2,16,128]{2,1,0:T(8,128)S(1)}, u32[]{:S(2)}, u32[]{:S(2)}) collective-permute-start(f32[2,16,128]{2,1,0:T(8,128)S(1)} %pad_maximum_fusion.3), channel_id=1, source_target_pairs={{0,4},{1,5},{2,6},{3,7},{4,0},{5,1},{6,2},{7,3},{8,12},{9,13},{10,... | collective-permute-start | bytes 49160 | tf_op jit(solution)/shard_map/ppermute | solution.py:479
  140.4 6.3 %collective-permute-start.3 = (f32[2,16,128]{2,1,0:T(8,128)S(1)}, f32[2,16,128]{2,1,0:T(8,128)S(1)}, u32[]{:S(2)}, u32[]{:S(2)}) collective-permute-start(f32[2,16,128]{2,1,0:T(8,128)S(1)} %fusion.2), channel_id=1, source_target_pairs={{0,8},{1,9},{2,10},{3,11},{4,12},{5,13},{6,14},{7,15},{8,0},{9,1},... | collective-permute-start | bytes 49160 | tf_op jit(solution)/shard_map/ppermute | solution.py:479
  146.6 4.7 %collective-permute-start.4 = (bf16[2,16,128]{2,1,0:T(8,128)(2,1)S(1)}, bf16[2,16,128]{2,1,0:T(8,128)(2,1)S(1)}, u32[]{:S(2)}, u32[]{:S(2)}) collective-permute-start(bf16[2,16,128]{2,1,0:T(8,128)(2,1)S(1)} %fusion.3), channel_id=1, source_target_pairs={{0,16},{16,0},{32,48},{48,32},{64,80},{80,64},{96,112},{112,96},{1... | collective-permute-start | bytes 24584 | tf_op jit(solution)/shard_map/ppermute | solution.py:479
  151.3 9.6 %collective-permute-start.7 = (bf16[2,2,16,128]{3,2,1,0:T(8,128)(2,1)S(1)}, bf16[2,2,16,128]{3,2,1,0:T(8,128)(2,1)S(1)}, u32[]{:S(2)}, u32[]{:S(2)}) collective-permute-start(bf16[2,2,16,128]{3,2,1,0:T(8,128)(2,1)S(1)} %get-tuple-element.54), channel_id=1, source_target_pairs={{0,96},{16,112},{32,0},{48,16},{64,32},{80,48},{96,64},{112,80},{1... | collective-permute-start | bytes 49160 | tf_op jit(solution)/shard_map/ppermute | solution.py:484
  155.9 6.5 %collective-permute-start.6 = (bf16[2,2,16,128]{3,2,1,0:T(8,128)(2,1)S(1)}, bf16[2,2,16,128]{3,2,1,0:T(8,128)(2,1)S(1)}, u32[]{:S(2)}, u32[]{:S(2)}) collective-permute-start(bf16[2,2,16,128]{3,2,1,0:T(8,128)(2,1)S(1)} %get-tuple-element.54), channel_id=1, source_target_pairs={{0,64},{16,80},{32,96},{48,112},{64,0},{80,16},{96,32},{112,48},{1... | collective-permute-start | bytes 49160 | tf_op jit(solution)/shard_map/ppermute | solution.py:484
  158.4 6.0 %collective-permute-start.5 = (bf16[2,2,16,128]{3,2,1,0:T(8,128)(2,1)S(1)}, bf16[2,2,16,128]{3,2,1,0:T(8,128)(2,1)S(1)}, u32[]{:S(2)}, u32[]{:S(2)}) collective-permute-start(bf16[2,2,16,128]{3,2,1,0:T(8,128)(2,1)S(1)} %get-tuple-element.54), channel_id=1, source_target_pairs={{0,32},{16,48},{32,64},{48,80},{64,96},{80,112},{96,0},{112,16},{1... | collective-permute-start | bytes 49160 | tf_op jit(solution)/shard_map/ppermute | solution.py:484
  164.4 22.4 %collective-permute-start.10 = (bf16[4,2,2,16,128]{4,3,2,1,0:T(8,128)(2,1)S(1)}, bf16[4,2,2,16,128]{4,3,2,1,0:T(8,128)(2,1)S(1)}, u32[]{:S(2)}, u32[]{:S(2)}) collective-permute-start(bf16[4,2,2,16,128]{4,3,2,1,0:T(8,128)(2,1)S(1)} %pad_maximum_fusion), channel_id=1, source_target_pairs={{0,3},{1,2},{2,1},{3,0},{4,7},{5,6},{6,5},{7,4},{8,11},{9,10},{10,... | collective-permute-start | bytes 196616 | tf_op jit(solution)/shard_map/ppermute | solution.py:479
  168.9 29.5 %collective-permute-start.8 = (bf16[4,2,2,16,128]{4,3,2,1,0:T(8,128)(2,1)S(1)}, bf16[4,2,2,16,128]{4,3,2,1,0:T(8,128)(2,1)S(1)}, u32[]{:S(2)}, u32[]{:S(2)}) collective-permute-start(bf16[4,2,2,16,128]{4,3,2,1,0:T(8,128)(2,1)S(1)} %pad_maximum_fusion), channel_id=1, source_target_pairs={{0,1},{1,0},{2,3},{3,2},{4,5},{5,4},{6,7},{7,6},{8,9},{9,8},{10,11... | collective-permute-start | bytes 196616 | tf_op jit(solution)/shard_map/ppermute | solution.py:479
  171.4 30.2 %collective-permute-start.9 = (bf16[4,2,2,16,128]{4,3,2,1,0:T(8,128)(2,1)S(1)}, bf16[4,2,2,16,128]{4,3,2,1,0:T(8,128)(2,1)S(1)}, u32[]{:S(2)}, u32[]{:S(2)}) collective-permute-start(bf16[4,2,2,16,128]{4,3,2,1,0:T(8,128)(2,1)S(1)} %pad_maximum_fusion), channel_id=1, source_target_pairs={{0,2},{1,3},{2,0},{3,1},{4,6},{5,7},{6,4},{7,5},{8,10},{9,11},{10,... | collective-permute-start | bytes 196616 | tf_op jit(solution)/shard_map/ppermute | solution.py:479
